TPU v7x, 32 devices: a whole 2x2x4 slice. The times are simulated.
32 devices in a mesh: seq: 8 (over z, y), grp: 4 (over x, core).
Axes of the slice: x: 2, y: 2, z: 4, core: 2. Of those that a mesh axis runs over, the one named last changes fastest.
Arguments:
- hidden: bfloat16 [4096, 2688], P(('seq', 'grp')), may hold values from -30 to 30
- conv_input: bfloat16 [4096, 3072], P(('seq', 'grp')), may hold values from -30 to 30
- z_stream: bfloat16 [4096, 2048], P(('seq', 'grp')), may hold values from -6 to 6
- log_decay: float32 [32, 4096], P(None, ('seq', 'grp')), may hold values from -1.5 to 0
- conv_weight: float32 [4, 3072], replicated, may hold values from -3 to 3
- norm_gain: float32 [2048], replicated, may hold values from 0.5 to 1.5
- out_weight: bfloat16 [2048, 2688], P('grp'), may hold values from -0.125 to 0.125
- moe_gain: float32 [2688], replicated, may hold values from 0.5 to 1.5
- routes: int32 [4096, 6], P(('seq', 'grp')), may hold values from 0 to 31, all different within a row; in each aligned block of 128 rows (0 to 127, 128 to 255, ...) at most 36 rows name the same one
- gate_weights: float32 [4096, 6], P(('seq', 'grp')), may hold values from 0.1 to 1
- expert_home: int32 [32], replicated, may hold values from 0 to 31, each once
- up_weight: bfloat16 [32, 2688, 1024], P(('seq', 'grp')), may hold values from -0.125 to 0.125
- down_weight: bfloat16 [32, 1024, 2688], P(('seq', 'grp')), may hold values from -0.1875 to 0.1875
Outputs:
- output: bfloat16 [4096, 2688], P(('seq', 'grp'))
Inputs may be any that keep to these rules, and one draw needn't show every extreme that they name: `routes`: among the rows of one device no expert is named more than 36 times, a bound that some block reaches. `expert_home`: each expert is held by exactly one device, and each device holds one expert.
All inputs are finite; a program needn't handle non-finite values.
Results may differ from a plain program's by a relative error of at most 0.013.
Values may be sent and summed in bfloat16 or wider, within the bound.
No kernel may reach another device: no remote copies, remote signals or barrier semaphores. Data moves between devices by JAX's collectives and lax.ppermute only.
A program may use at most 128 MiB of HBM per device.

v0:
```python
import jax
import jax.numpy as jnp
from jax import lax
from jax.sharding import PartitionSpec as P

N = 64
G = 8
QB = 128


epsilon = 1e-05
highest = lax.Precision.HIGHEST


def passed_along(value, axis, by):
    count = lax.axis_size(axis)
    pairs = [(i, i + by) for i in range(count) if 0 <= i + by < count]
    return lax.ppermute(value, axis, pairs)


def carried_in(value, axis, join, neutral):
    place = lax.axis_index(axis)
    gathered = jax.tree.map(
        lambda a, kind: lax.all_gather(a.astype(kind), axis),
        value,
        jax.tree.map(lambda a: jnp.bfloat16 if a.dtype == jnp.float32 else a.dtype, value),
    )
    state = jax.tree.map(lambda a, e: jnp.zeros_like(a) + jnp.asarray(e, a.dtype), value, neutral)

    def one(step, state):
        return join(
            state,
            jax.tree.map(
                lambda a, own: lax.dynamic_index_in_dim(a, step, 0, False).astype(own.dtype),
                gathered,
                value,
            ),
        )

    return lax.fori_loop(0, place, one, state)


def from_root(block, axis, holder):
    block = jnp.where(lax.axis_index(axis) == holder, block, jnp.zeros_like(block))
    return lax.psum(block, axis)


def entering_2(value, axis, join, neutral):
    count, mine = (lax.axis_size(axis), lax.axis_index(axis))
    pieces = jax.tree.map(lambda part: lax.all_gather(part, axis), value)
    so_far = jax.tree.map(
        lambda part, zero: jnp.full_like(part, 0) + jnp.asarray(zero, part.dtype), value, neutral
    )

    def step(position, so_far):
        longer = join(so_far, jax.tree.map(lambda part: part[position], pieces))
        return jax.tree.map(lambda new, old: jnp.where(position < mine, new, old), longer, so_far)

    return lax.fori_loop(0, count - 1, step, so_far)


def convolve(stream, previous, conv_weight):
    length = stream.shape[0]
    padded = jnp.concatenate([previous, stream], axis=0).astype(jnp.float32)
    summed = conv_weight[0][None, :] * padded[0:length]
    for offset in range(1, conv_weight.shape[0]):
        summed = summed + conv_weight[offset][None, :] * padded[offset : offset + length]
    return jax.nn.silu(summed).astype(jnp.bfloat16)


def span_parts(value_block, inkey_block, outkey_block, decay_block):
    cumulative = jnp.cumsum(decay_block, axis=-1)
    block_len = decay_block.shape[-1]
    intersection = jnp.einsum("tgn,sgn->gts", outkey_block, inkey_block, precision=highest)
    causal = lax.broadcasted_iota(jnp.int32, (block_len, block_len), 0) >= lax.broadcasted_iota(
        jnp.int32, (block_len, block_len), 1
    )
    spread = cumulative[..., :, None] - cumulative[..., None, :]
    mixing = jnp.where(causal, jnp.exp(jnp.where(causal, spread, 0.0)), 0.0) * intersection[:, None]
    inside = jnp.einsum("gjts,sgjp->tgjp", mixing, value_block, precision=highest)
    to_end = jnp.exp(cumulative[..., -1:] - cumulative)
    end_state = jnp.einsum(
        "gjs,sgjp,sgn->gjpn", to_end, value_block, inkey_block, precision=highest
    )
    return (inside, end_state, cumulative)


def entering(outkey_block, carried, cumulative):
    reach = jnp.einsum("tgn,gjpn->tgjp", outkey_block, carried, precision=highest)
    return reach * jnp.exp(jnp.transpose(cumulative, (2, 0, 1)))[..., None]


def merge_states(earlier, later):
    decay_one, state_one = earlier
    decay_two, state_two = later
    return (decay_one + decay_two, jnp.exp(decay_two)[..., None, None] * state_one + state_two)


def gated_norm(ssm_out, z_stream, norm_gain, group_count):
    gated_out = ssm_out * jax.nn.silu(z_stream.astype(jnp.float32))
    row_count = gated_out.shape[0]
    grouped = gated_out.reshape(row_count, group_count, -1)
    scaled = grouped * lax.rsqrt(jnp.mean(grouped * grouped, axis=-1, keepdims=True) + epsilon)
    return (scaled.reshape(row_count, -1) * norm_gain[None, :]).astype(jnp.bfloat16)


def token_norm(stream, gain):
    widened = stream.astype(jnp.float32)
    scaled = widened * lax.rsqrt(jnp.mean(widened * widened, axis=-1, keepdims=True) + epsilon)
    return (scaled * gain[None, :]).astype(jnp.bfloat16)


def local(
    hidden,
    conv_input,
    z_stream,
    log_decay,
    conv_weight,
    norm_gain,
    out_weight,
    moe_gain,
    routes,
    gate_weights,
    expert_home,
    up_weight,
    down_weight,
):
    length = conv_input.shape[0]
    kernel = conv_weight.shape[0]
    previous = passed_along(conv_input[length - kernel + 1 :], ("seq", "grp"), 1)
    active = convolve(conv_input, previous, conv_weight)
    head_count = log_decay.shape[0]
    inner_width = z_stream.shape[1]
    head_size = inner_width // head_count
    per_group = head_count // G
    blocks = length // QB
    key_width = G * N
    values = active[:, :inner_width].astype(jnp.float32)
    in_keys = active[:, inner_width : inner_width + key_width].astype(jnp.float32)
    out_keys = active[:, inner_width + key_width :].astype(jnp.float32)
    value_spans = values.reshape(blocks, QB, G, per_group, head_size)
    inkey_spans = in_keys.reshape(blocks, QB, G, N)
    outkey_spans = out_keys.reshape(blocks, QB, G, N)
    decay_spans = log_decay.reshape(G, per_group, blocks, QB).transpose(2, 0, 1, 3)
    inside, end_states, cumulatives = jax.vmap(span_parts)(
        value_spans, inkey_spans, outkey_spans, decay_spans
    )
    span_decays = cumulatives[..., -1]

    def fold_span(carried, pieces):
        return (merge_states(carried, pieces), None)

    identity = (
        jnp.zeros((G, per_group), jnp.float32),
        jnp.zeros((G, per_group, head_size, N), jnp.float32),
    )
    own_state, _ = lax.scan(fold_span, identity, (span_decays, end_states))
    within = carried_in(own_state, "grp", merge_states, identity)
    through = merge_states(within, own_state)
    group_sum = (
        from_root(through[0], "grp", lax.axis_size("grp") - 1),
        from_root(through[1], "grp", lax.axis_size("grp") - 1),
    )
    before = entering_2(group_sum, "seq", merge_states, identity)
    incoming = merge_states(before, within)

    def advance(carried, pieces):
        span_decay, end_state, cumulative, outkey_block = pieces
        carried_out = entering(outkey_block, carried, cumulative)
        return (jnp.exp(span_decay)[..., None, None] * carried + end_state, carried_out)

    _, entered = lax.scan(
        advance, incoming[1], (span_decays, end_states, cumulatives, outkey_spans)
    )
    ssm_out = (inside + entered).reshape(length, inner_width)
    mixed_norm = gated_norm(ssm_out, z_stream, norm_gain, G)
    model_width = hidden.shape[1]
    mamba_out = jnp.dot(
        mixed_norm,
        lax.all_gather(out_weight, "grp", axis=0, tiled=True),
        preferred_element_type=jnp.float32,
    )
    residual_one = (hidden.astype(jnp.float32) + mamba_out).astype(jnp.bfloat16)
    moe_in = token_norm(residual_one, moe_gain)
    top_count = routes.shape[1]
    devices = lax.axis_size("seq") * lax.axis_size("grp")
    capacity = max(2, 3 * length * top_count // (2 * devices))
    experts_total = expert_home.shape[0]
    flat_routes = routes.reshape(-1)
    chosen = (flat_routes[:, None] == jnp.arange(experts_total, dtype=jnp.int32)[None, :]).astype(
        jnp.int32
    )
    target_device = jnp.sum(chosen * expert_home[None, :], axis=1)
    slot_rank = jnp.sum(chosen * (jnp.cumsum(chosen, axis=0) - 1), axis=1)
    slot_index = target_device * capacity + slot_rank
    outgoing = (
        jnp.zeros((devices * capacity, model_width), jnp.bfloat16)
        .at[slot_index]
        .set(jnp.repeat(moe_in, top_count, axis=0))
    )
    up_local = up_weight[0]
    down_local = down_weight[0]
    arrived = lax.all_to_all(
        outgoing.reshape(devices, capacity, model_width),
        ("seq", "grp"),
        split_axis=0,
        concat_axis=0,
        tiled=True,
    )
    flattened = arrived.reshape(-1, arrived.shape[-1])
    up_result = jnp.dot(flattened, up_local, preferred_element_type=jnp.float32)
    squared = jnp.square(jax.nn.relu(up_result)).astype(jnp.bfloat16)
    result = jnp.dot(squared, down_local, preferred_element_type=jnp.float32).astype(jnp.bfloat16)
    returned = lax.all_to_all(
        result.reshape(arrived.shape), ("seq", "grp"), split_axis=0, concat_axis=0, tiled=True
    )
    returned = returned.reshape(devices * capacity, model_width)
    pair_out = returned[slot_index].reshape(length, top_count, model_width)
    mixture = residual_one.astype(jnp.float32)
    for pick_index in range(top_count):
        mixture = mixture + gate_weights[:, pick_index : pick_index + 1] * pair_out[
            :, pick_index
        ].astype(jnp.float32)
    return mixture.astype(jnp.bfloat16)


def solution(mesh):
    placed = (
        P(("seq", "grp"), None),
        P(("seq", "grp"), None),
        P(("seq", "grp"), None),
        P(None, ("seq", "grp")),
        P(),
        P(),
        P("grp", None),
        P(),
        P(("seq", "grp"), None),
        P(("seq", "grp"), None),
        P(),
        P(("seq", "grp"), None, None),
        P(("seq", "grp"), None, None),
    )
    return jax.shard_map(
        local, mesh=mesh, in_specs=placed, out_specs=P(("seq", "grp"), None), check_vma=False
    )
```

profile of v0, /device:TPU:0, one launch (start us, length us, event | category | flops | bytes accessed | tf_op | source)
XLA Modules:
  0.0 726.1 jit_solution(8369794992906035461)
XLA Ops:
  6.5 0.8 slice.83
  7.4 2.4 collective-permute-start
  9.7 1.0 fusion.69
  10.7 0.7 copy.103
  11.4 1.1 reduce_window_sum.24
  12.9 1.4 maximum_convert_fusion
  14.3 1.0 multiply_convert_fusion
  15.7 1.5 fusion.71
  17.3 7.1 all-gather
  24.4 18.1 %all-gather.10.cloned.1.call-done = bf16[32,4,64,64]{3,2,1,0:T(8,128)(2,1)} async-done(((bf16[8,4,64,64]{3,2,1,0:T(8,128)(2,1)}), bf16[32,4,64,64]{3,2,1,0:T(8,128)(2,1)}) %all-gather.10.cloned.1.call-update) | async-done | bytes 1048592 | tf_op jit(solution)/shard_map/all_gather | solution.py:24
  42.8 1.2 select_bitcast_fusion
  44.0 40.4 %all-reduce.2.cloned.1.call-done = f32[1,8,4,64,64]{4,3,2,1,0:T(8,128)} async-done(((f32[1,8,4,64,64]{4,3,2,1,0:T(8,128)}), f32[1,8,4,64,64]{4,3,2,1,0:T(8,128)}) %all-reduce.2.cloned.1.call-update) | async-done | bytes 524304 | tf_op jit(solution)/shard_map/psum | solution.py:45
  84.5 0.5 all-gather.8.cloned.1.call-update
  85.6 1.7 reduce-window.6
  88.3 5.9 psum.14
  94.1 27.0 %all_gather.26 = f32[8,8,4]{1,2,0:T(4,128)S(1)} all-gather(f32[1,8,4]{1,2,0:T(4,128)S(1)} %psum.14), channel_id=1, replica_groups=mesh['seq'=8,'grp'=4] {'seq'}, dimensions={0}, use_global_device_ids=true | all-gather | bytes 1152 | tf_op jit(solution)/shard_map/all_gather | solution.py:50
  121.2 91.2 %all-gather.6.cloned.1.call-done = f32[8,8,4,64,64]{4,3,2,1,0:T(8,128)} async-done(((f32[1,8,4,64,64]{4,3,2,1,0:T(8,128)}), f32[8,8,4,64,64]{4,3,2,1,0:T(8,128)}) %all-gather.6.cloned.1.call-update) | async-done | bytes 4194320 | tf_op jit(solution)/shard_map/all_gather | solution.py:50
  212.4 11.6 %while.8 = (s32[]{:T(128)}, f32[8,4,64,64]{3,2,1,0:T(8,128)S(1)}, s32[]{:T(128)}, f32[8,8,4]{1,2,0:T(4,128)S(1)}, f32[8,8,4,64,64]{4,3,2,1,0:T(8,128)}, /*index=5*/s32[]{:T(128)}, s32[]{:T(128)}) while((s32[]{:T(128)}, f32[8,4,64,64]{3,2,1,0:T(8,128)S(1)}, s32[]{:T(128)}, f32[8,8,4]{1,2,0:T(4,128)S(1)}, ...), condition=%wide.region_6.7_spmd.clone, body=%wide.region_5.6_spmd.clone.sunk | while | flops 524292 | bytes 1573609 | solution.py:59
  212.5 1.5 fusion.81
  214.1 1.5 fusion.81
  215.6 1.5 fusion.81
  217.2 1.6 fusion.81
  218.9 1.6 fusion.81
  220.7 1.7 fusion.81
  222.5 1.6 fusion.81
  224.0 0.8 fusion.37
  224.8 2.4 fusion.38
  227.2 0.3 copy.114
  227.5 0.7 copy-done
  228.5 0.3 copy.136
  229.5 0.3 copy.137
  229.8 55.4 %all-gather.8.cloned.1.call-done = bf16[2048,2688]{1,0:T(8,128)(2,1)} async-done(((bf16[512,2688]{1,0:T(8,128)(2,1)}), bf16[2048,2688]{1,0:T(8,128)(2,1)}) %all-gather.8.cloned.1.call-update) | async-done | bytes 11010064 | tf_op jit(solution)/shard_map/all_gather | solution.py:180
  285.3 6.3 multiply_reduce_fusion
  291.8 3.0 broadcast_in_dim.51
  294.8 7.3 %reshape.224 = bf16[768,2688]{1,0:T(8,128)(2,1)} reshape(bf16[128,6,2688]{2,1,0:T(8,128)(2,1)} %broadcast_in_dim.51) | data formatting | bytes 8257536 | tf_op jit(solution)/shard_map/reshape | solution.py:199
  302.1 13.4 %scatter_custom_fusion = bf16[1152,2688]{1,0:T(8,128)(2,1)} fusion(s32[768]{0:T(1024)S(1)} %fusion.62, bf16[768,2688]{1,0:T(8,128)(2,1)} %reshape.224, bf16[]{:T(256)} %constant.101.clone.1), kind=kCustom, calls=%fused_computation.18 | custom fusion | bytes 6193664 | tf_op jit(solution)/shard_map/scatter | solution.py:199
  315.5 8.2 %reshape.199 = bf16[32,36,2688]{2,1,0:T(8,128)(2,1)} reshape(bf16[1152,2688]{1,0:T(8,128)(2,1)} %scatter_custom_fusion) | data formatting | bytes 12386304 | tf_op jit(solution)/shard_map/reshape | solution.py:204
  323.7 156.3 %all_to_all.10 = bf16[32,36,2688]{2,1,0:T(8,128)(2,1)} all-to-all(bf16[32,36,2688]{2,1,0:T(8,128)(2,1)} %reshape.199), channel_id=1, replica_groups=mesh['seq'=8,'grp'=4] {'seq','grp'}, dimensions={0} | all-to-all | bytes 12386304 | tf_op jit(solution)/shard_map/all_to_all | solution.py:203
  480.0 8.3 %reshape.200 = bf16[1152,2688]{1,0:T(8,128)(2,1)} reshape(bf16[32,36,2688]{2,1,0:T(8,128)(2,1)} %all_to_all.10) | data formatting | bytes 12386304 | tf_op jit(solution)/shard_map/reshape | solution.py:210
  488.3 20.7 %convolution_convert_fusion = bf16[1152,2688]{1,0:T(8,128)(2,1)} fusion(bf16[1,1024,2688]{2,1,0:T(8,128)(2,1)} %param.29, bf16[1152,2688]{1,0:T(8,128)(2,1)} %reshape.200, bf16[1,2688,1024]{2,1,0:T(8,128)(2,1)} %param.28), kind=kOutput, calls=%fused_computation.8 | convolution fusion | flops 12690210816 | bytes 23396352 | tf_op jit(solution)/shard_map/dot_general | solution.py:213
  509.0 8.3 %reshape.201 = bf16[32,36,2688]{2,1,0:T(8,128)(2,1)} reshape(bf16[1152,2688]{1,0:T(8,128)(2,1)} %convolution_convert_fusion) | data formatting | bytes 12386304 | tf_op jit(solution)/shard_map/reshape | solution.py:215
  517.3 4.1 all-to-all-start.1
  521.4 152.9 %all-to-all-done.1 = bf16[32,36,2688]{2,1,0:T(8,128)(2,1)} async-done(((bf16[32,36,2688]{2,1,0:T(8,128)(2,1)}), bf16[32,36,2688]{2,1,0:T(8,128)(2,1)}, u32[]{:S(2)}, u32[]{:S(2)}) %all-to-all-start.1) | async-done | bytes 6193184 | tf_op jit(solution)/shard_map/all_to_all | solution.py:214
  674.3 8.3 %reshape.202 = bf16[1152,2688]{1,0:T(8,128)(2,1)} reshape(bf16[32,36,2688]{2,1,0:T(8,128)(2,1)} %all-to-all-done.1) | data formatting | bytes 12386304 | tf_op jit(solution)/shard_map/reshape | solution.py:217
  682.6 12.3 %gather_fusion = bf16[768,2688]{1,0:T(8,128)(2,1)} fusion(bf16[1152,2688]{1,0:T(8,128)(2,1)} %reshape.202, s32[1024]{0:T(1024)S(1)} %pad_clamp_fusion), kind=kCustom, calls=%fused_computation | custom fusion | bytes 8260608 | tf_op jit(solution)/shard_map/gather | solution.py:218
  694.9 7.3 %reshape.203 = bf16[128,6,2688]{2,1,0:T(8,128)(2,1)} reshape(bf16[768,2688]{1,0:T(8,128)(2,1)} %gather_fusion) | data formatting | bytes 8257536 | tf_op jit(solution)/shard_map/reshape | solution.py:218
  702.2 15.6 %fusion.67 = (bf16[128,1,2688]{2,1,0:T(2,128)(2,1)S(1)}, bf16[128,1,2688]{2,1,0:T(2,128)(2,1)S(1)}, bf16[128,1,2688]{2,1,0:T(2,128)(2,1)S(1)}, bf16[128,1,2688]{...) fusion(bf16[128,6,2688]{2,1,0:T(8,128)(2,1)} %reshape.203), kind=kLoop, calls=%fused_computation.112 | loop fusion | bytes 8257536 | tf_op jit(solution)/shard_map/slice | solution.py:221
  717.8 1.8 fusion.27
  (75 shorter events, 4.3 us)
Async XLA Ops:
  6.5 36.0 %all-gather.10.cloned.1.call-start = ((), (), s32[]{:S(2)}) async-start(), calls=%async_computation.5 | async-start | bytes 2621440 | tf_op jit(solution)/shard_map/all_gather | solution.py:24
  7.4 5.6 collective-permute-start
  17.2 67.2 %all-reduce.2.cloned.1.call-start = ((), (), s32[]{:S(2)}) async-start(), calls=%async_computation.2 | async-start | bytes 2097152 | tf_op jit(solution)/shard_map/psum | solution.py:45
  44.0 168.4 %all-gather.6.cloned.1.call-start = ((), (), s32[]{:S(2)}) async-start(), calls=%async_computation.3 | async-start | bytes 9437184 | tf_op jit(solution)/shard_map/all_gather | solution.py:50
  84.4 0.7 copy-start.2
  84.4 3.2 copy-start.4
  84.4 200.8 %all-gather.8.cloned.1.call-start = ((), (), s32[]{:S(2)}) async-start(), calls=%async_computation.4 | async-start | bytes 13762560 | tf_op jit(solution)/shard_map/all_gather | solution.py:180
  227.2 1.0 copy-start
  229.3 56.0 %copy-start.5 = (f32[2048]{0:T(1024)S(1)}, f32[2048]{0:T(1024)}, u32[]{:S(2)}) copy-start(f32[2048]{0:T(1024)} %param.22) | copy-start | bytes 24580
  285.3 6.3 copy-start.1
  517.3 4.1 copy-start.3
  517.3 157.0 %all-to-all-start.1 = ((bf16[32,36,2688]{2,1,0:T(8,128)(2,1)}), bf16[32,36,2688]{2,1,0:T(8,128)(2,1)}, u32[]{:S(2)}, u32[]{:S(2)}) async-start(bf16[32,36,2688]{2,1,0:T(8,128)(2,1)} %reshape.201), calls=%async_computation.1 | async-start | bytes 13762560 | tf_op jit(solution)/shard_map/all_to_all | solution.py:214
Sparse Core Ops, SparseCore 0:
  17.4 25.1 all-gather.9
  44.9 39.4 all-reduce.1
  86.7 125.6 all-gather.5
  213.9 71.3 all-gather.7
where the time goes:
time: 728 us; the launch traced here: 726 us
  waiting for transfers between devices  359 us (49%)
  blocking collectives  196 us (27%)
  local copies, waits for them, and re-layouts  99.1 us (14%)
  matrix products  31.9 us (4%)
  other arithmetic  20 us (3%)
  between operations  13.5 us (2%)
    all_to_all x1, blocking collectives, local(): lax.all_to_all(outgoing.reshape(devices, capacity, model_width), ('seq',...  156 us
    all_to_all x1, waiting for transfers between devices, local(): lax.all_to_all(result.reshape(arrived.shape), ('seq', 'grp'), split_axis=...  153 us
    all_gather x1, waiting for transfers between devices, entering_2(): pieces = jax.tree.map(lambda part: lax.all_gather(part, axis), value)  91.2 us
    all_gather x1, waiting for transfers between devices, local(): lax.all_gather(out_weight, 'grp', axis=0, tiled=True)  55.4 us
    psum x1, waiting for transfers between devices, from_root(): return lax.psum(block, axis)  40.4 us
    all_gather x1, blocking collectives, entering_2(): pieces = jax.tree.map(lambda part: lax.all_gather(part, axis), value)  27 us
    dot_general x1, matrix products, local(): jnp.dot(squared, down_local, preferred_element_type=jnp.float32)  20.7 us
    all_gather x1, waiting for transfers between devices, carried_in(): lax.all_gather(a.astype(kind), axis)  18.1 us
  transfers between devices with their start and end apart: 6, of which 5 were waited for; matrix products, arithmetic and copies ran while one was open for 3% of the time, Pallas kernels for 0%

commit v1 on v0

v1 whole, which is shorter than its diff:
```python
import functools

import jax
import jax.numpy as jnp
from jax import lax
from jax.experimental import pallas as pl
from jax.experimental.pallas import tpu as pltpu
from jax.sharding import PartitionSpec as P

AXES = ("seq", "grp")
N = 64
G = 8
EPS = 1e-05
DEC = 16
VMEM_LIMIT = 48 * 1024 * 1024
f32 = jnp.float32
bf16 = jnp.bfloat16


def dot(a, b, contract, precision=None):
    return lax.dot_general(
        a, b, ((contract[0], contract[1]), ((), ())), preferred_element_type=f32, precision=precision
    )


def spread_lanes(columns, width):
    count = len(columns)
    rows = columns[0].shape[0]
    lane = lax.broadcasted_iota(jnp.int32, (rows, count * width), 1)
    out = jnp.broadcast_to(columns[-1], (rows, count * width))
    for j in range(count - 2, -1, -1):
        out = jnp.where(lane < (j + 1) * width, columns[j], out)
    return out


def split_decay(d):
    whole = jnp.floor(d)
    part = d - whole
    coarse = jnp.floor(part * 256.0) * (1.0 / 256.0)
    fine = part - coarse
    row = lax.broadcasted_iota(jnp.int32, (DEC, d.shape[1]), 0)
    rows = jnp.where(row == 0, whole, jnp.where(row == 1, coarse, jnp.where(row == 2, fine, 0.0)))
    return rows.astype(bf16)


def join_decay(rows):
    return jnp.sum(rows.astype(f32), axis=0, keepdims=True)


def silu(x):
    return x * (1.0 / (1.0 + jnp.exp(-x)))


def start_kernel(plane, r_ref, x_ref, prev_ref, cw_ref, ld_ref, act_ref, cum_ref, cumt_ref, *rest):
    outs, scr = rest[:plane], rest[plane]
    length, channels = x_ref.shape
    heads = ld_ref.shape[0]
    per_group = heads // G
    inner = channels - 2 * G * N
    width = inner // G
    head_size = width // per_group
    halo, taps = prev_ref.shape[0], cw_ref.shape[0]
    ld = ld_ref[...]
    low = (
        lax.broadcasted_iota(jnp.int32, (length, length), 0)
        >= lax.broadcasted_iota(jnp.int32, (length, length), 1)
    ).astype(f32)
    cum_ref[...] = dot(ld, low, ((1,), (1,)), lax.Precision.HIGHEST)
    cumt = dot(low, ld, ((1,), (1,)), lax.Precision.HIGHEST)
    cumt_ref[...] = cumt
    last = cumt[length - 1 : length, :]
    to_end = jnp.exp(last - cumt)
    for c in range(0, channels, width):
        cols = slice(c, c + width)
        padded = jnp.concatenate([prev_ref[:, cols], x_ref[:, cols]], axis=0).astype(f32)
        first = halo - taps + 1
        total = cw_ref[0:1, cols] * padded[first : first + length]
        for k in range(1, taps):
            total = total + cw_ref[k : k + 1, cols] * padded[first + k : first + k + length]
        act_ref[:, cols] = silu(total).astype(bf16)
    for g in range(G):
        v = act_ref[:, g * width : (g + 1) * width].astype(f32)
        ik = act_ref[:, inner + g * N : inner + (g + 1) * N]
        hs = range(g * per_group, (g + 1) * per_group)
        weighted = (v * spread_lanes([to_end[:, h : h + 1] for h in hs], head_size)).astype(bf16)
        scr[g, :N, :] = dot(ik, weighted, ((0,), (0,))).astype(bf16)
        scr[g, N:, :] = split_decay(spread_lanes([last[:, h : h + 1] for h in hs], head_size))
    r = r_ref[0]
    for m in range(plane):
        outs[m][...] = scr[r ^ m]


def plane_kernel(plane, r_ref, *rest):
    chunks, out, scr = rest[:plane], rest[plane], rest[plane + 1]
    r = r_ref[0]
    for m in range(plane):
        scr[r ^ m] = chunks[m][...]
    state = jnp.zeros((N, out.shape[1]), f32)
    total = jnp.zeros((1, out.shape[1]), f32)
    for s in range(plane):
        decay = join_decay(scr[s, N:, :])
        state = jnp.exp(decay) * state + scr[s, :N, :].astype(f32)
        total = total + decay
    out[:N, :] = state.astype(bf16)
    out[N:, :] = split_decay(total)


def enter_kernel(plane, outer, r_ref, *rest):
    chunks, earlier = rest[:plane], rest[plane : plane + outer - 1]
    outs, scr, inc = rest[plane + outer - 1 : 2 * plane + outer - 1], rest[-2], rest[-1]
    r = r_ref[0]
    for m in range(plane):
        scr[r ^ m] = chunks[m][...]
    state = jnp.zeros((N, scr.shape[2]), f32)
    passed = jnp.zeros((1, scr.shape[2]), f32)
    for e in earlier:
        state = state + jnp.exp(passed) * e[:N, :].astype(f32)
        passed = passed + join_decay(e[N:, :])
    for s in range(plane):
        inc[s] = state.astype(bf16)
        state = jnp.exp(join_decay(scr[s, N:, :])) * state + scr[s, :N, :].astype(f32)
    for m in range(plane):
        outs[m][...] = inc[r ^ m]


def inside_kernel(act_ref, cum_ref, cumt_ref, out_ref):
    length, channels = act_ref.shape
    heads = cum_ref.shape[0]
    per_group = heads // G
    inner = channels - 2 * G * N
    head_size = inner // heads
    causal = lax.broadcasted_iota(jnp.int32, (length, length), 0) >= lax.broadcasted_iota(
        jnp.int32, (length, length), 1
    )
    cum = cum_ref[...]
    cumt = cumt_ref[...]
    for g in range(G):
        ik = act_ref[:, inner + g * N : inner + (g + 1) * N]
        ok = act_ref[:, inner + (G + g) * N : inner + (G + g + 1) * N]
        meet = jnp.where(causal, dot(ok, ik, ((1,), (1,))), 0.0)
        for h in range(g * per_group, (g + 1) * per_group):
            gap = jnp.where(causal, cumt[:, h : h + 1] - cum[h : h + 1, :], 0.0)
            mixing = (jnp.exp(gap) * meet).astype(bf16)
            cols = slice(h * head_size, (h + 1) * head_size)
            out_ref[:, cols] = dot(mixing, act_ref[:, cols], ((1,), (0,)))


def norm_kernel(plane, r_ref, act_ref, cumt_ref, inside_ref, z_ref, gain_ref, *rest):
    incoming, out_ref, scr = rest[:plane], rest[plane], rest[plane + 1]
    r = r_ref[0]
    for m in range(plane):
        scr[r ^ m] = incoming[m][...]
    inner = z_ref.shape[1]
    heads = cumt_ref.shape[1]
    per_group = heads // G
    width = inner // G
    head_size = inner // heads
    reach = jnp.exp(cumt_ref[...])
    for g in range(G):
        cols = slice(g * width, (g + 1) * width)
        ok = act_ref[:, inner + (G + g) * N : inner + (G + g + 1) * N]
        hs = range(g * per_group, (g + 1) * per_group)
        far = dot(ok, scr[g], ((1,), (0,)))
        ssm = inside_ref[:, cols] + far * spread_lanes([reach[:, h : h + 1] for h in hs], head_size)
        gated = ssm * silu(z_ref[:, cols].astype(f32))
        square = jnp.mean(gated * gated, axis=1, keepdims=True)
        out_ref[g] = (gated * lax.rsqrt(square + EPS) * gain_ref[:, cols]).astype(bf16)


def call(kernel, out_shape, scratch=(), flops=0, moved=0):
    return pl.pallas_call(
        kernel,
        out_shape=out_shape,
        scratch_shapes=list(scratch),
        compiler_params=pltpu.CompilerParams(vmem_limit_bytes=VMEM_LIMIT),
        cost_estimate=pl.CostEstimate(flops=flops, bytes_accessed=moved, transcendentals=0),
    )


def token_norm(stream, gain):
    widened = stream.astype(f32)
    scaled = widened * lax.rsqrt(jnp.mean(widened * widened, axis=-1, keepdims=True) + EPS)
    return (scaled * gain[None, :]).astype(bf16)


def local(
    hidden,
    conv_input,
    z_stream,
    log_decay,
    conv_weight,
    norm_gain,
    out_weight,
    moe_gain,
    routes,
    gate_weights,
    expert_home,
    up_weight,
    down_weight,
):
    n_grp = lax.axis_size("grp")
    devices = lax.axis_size("seq") * n_grp
    plane = 2 * n_grp
    outer = devices // plane
    me = lax.axis_index("seq") * n_grp + lax.axis_index("grp")
    r = lax.rem(me, plane)
    place = lax.div(me, plane)
    rs = r.reshape(1).astype(jnp.int32)

    def swap(x, m):
        return lax.ppermute(x, AXES, [(d, d ^ m) for d in range(devices)])

    def onward(x, by):
        return lax.ppermute(
            x, AXES, [(d, d + by) for d in range(devices) if d + by < devices]
        )

    def turn(x):
        return lax.ppermute(x, AXES, [(d, (d + plane) % devices) for d in range(devices)])

    length, channels = conv_input.shape
    heads = log_decay.shape[0]
    inner = z_stream.shape[1]
    width = inner // G
    model = hidden.shape[1]
    smem = pl.BlockSpec(memory_space=pltpu.SMEM)
    halo = 16

    previous = onward(conv_input[length - halo :], 1)

    per_shard = out_weight.shape[0] // width
    half = out_weight.shape[0] // 2
    side = lax.div(r, n_grp)
    mine_half = lax.dynamic_slice_in_dim(out_weight, side * half, half, 0)
    grp = lax.axis_index("grp")
    cuts = [mine_half[: half // 2], mine_half[half // 2 :]]
    by_x = [swap(c, 2) for c in cuts]
    by_y = [swap(c, n_grp) for c in by_x]
    own_pair = swap(out_weight, 1)
    by_x_pair = [swap(c, 1) for c in by_x]
    by_y_pair = [swap(c, 1) for c in by_y]

    shapes = jax.ShapeDtypeStruct
    chunk = shapes((N + DEC, width), bf16)
    first = pl.pallas_call(
        functools.partial(start_kernel, plane),
        out_shape=[
            shapes((length, channels), bf16),
            shapes((heads, length), f32),
            shapes((length, heads), f32),
        ]
        + [chunk] * plane,
        in_specs=[smem] + [pl.BlockSpec(memory_space=pltpu.VMEM)] * 4,
        scratch_shapes=[pltpu.VMEM((G, N + DEC, width), bf16)],
        compiler_params=pltpu.CompilerParams(vmem_limit_bytes=VMEM_LIMIT),
        cost_estimate=pl.CostEstimate(flops=50000000, bytes_accessed=8000000, transcendentals=0),
    )(rs, conv_input, previous, conv_weight, log_decay)
    active, cum, cumt = first[:3]
    chunks = [first[3]] + [swap(first[3 + m], m) for m in range(1, plane)]

    inside = call(
        inside_kernel, shapes((length, inner), f32), flops=100000000, moved=15000000
    )(active, cum, cumt)

    vm = pl.BlockSpec(memory_space=pltpu.VMEM)
    whole = pl.pallas_call(
        functools.partial(plane_kernel, plane),
        out_shape=chunk,
        in_specs=[smem] + [vm] * plane,
        scratch_shapes=[pltpu.VMEM((plane, N + DEC, width), bf16)],
        compiler_params=pltpu.CompilerParams(vmem_limit_bytes=VMEM_LIMIT),
        cost_estimate=pl.CostEstimate(flops=1000000, bytes_accessed=2000000, transcendentals=0),
    )(rs, *chunks)
    earlier = [onward(whole, plane * k) for k in range(1, outer)]
    entering = pl.pallas_call(
        functools.partial(enter_kernel, plane, outer),
        out_shape=[shapes((N, width), bf16)] * plane,
        in_specs=[smem] + [vm] * (plane + outer - 1),
        scratch_shapes=[
            pltpu.VMEM((plane, N + DEC, width), bf16),
            pltpu.VMEM((plane, N, width), bf16),
        ],
        compiler_params=pltpu.CompilerParams(vmem_limit_bytes=VMEM_LIMIT),
        cost_estimate=pl.CostEstimate(flops=1000000, bytes_accessed=2000000, transcendentals=0),
    )(rs, *chunks, *earlier)
    incoming = [entering[0]] + [swap(entering[m], m) for m in range(1, plane)]
    mixed = pl.pallas_call(
        functools.partial(norm_kernel, plane),
        out_shape=shapes((G, length, width), bf16),
        in_specs=[smem] + [vm] * (5 + plane),
        scratch_shapes=[pltpu.VMEM((G, N, width), bf16)],
        compiler_params=pltpu.CompilerParams(vmem_limit_bytes=VMEM_LIMIT),
        cost_estimate=pl.CostEstimate(flops=40000000, bytes_accessed=6000000, transcendentals=0),
    )(rs, active, cumt, inside, z_stream, norm_gain[None, :], *incoming)

    flat = mixed.transpose(1, 0, 2).reshape(length, inner)
    shard = out_weight.shape[0]

    def project(rows, start):
        part = lax.dynamic_slice_in_dim(flat, start, rows.shape[0], 1)
        return jnp.dot(part, rows, preferred_element_type=f32)

    other = 1 - side
    quarter = half // 2
    total = hidden.astype(f32)
    total = total + project(out_weight, grp * shard) + project(own_pair, (grp ^ 1) * shard)
    for k in range(2):
        total = total + project(by_x[k], (grp ^ 2) * shard + side * half + k * quarter)
        total = total + project(by_x_pair[k], (grp ^ 3) * shard + side * half + k * quarter)
        total = total + project(by_y[k], (grp ^ 2) * shard + other * half + k * quarter)
        total = total + project(by_y_pair[k], (grp ^ 3) * shard + other * half + k * quarter)
    residual_one = total.astype(bf16)
    moe_in = token_norm(residual_one, moe_gain)

    top_count = routes.shape[1]
    capacity = max(2, 3 * length * top_count // (2 * devices))
    experts = expert_home.shape[0]
    picked = routes[:, :, None] == jnp.arange(experts, dtype=jnp.int32)[None, None, :]
    target = jnp.sum(jnp.where(picked, expert_home[None, None, :], 0), axis=2)
    at_device = target[:, :, None] == jnp.arange(devices, dtype=jnp.int32)[None, None, :]
    chosen = jnp.any(at_device, axis=1)
    gates = jnp.sum(jnp.where(at_device, gate_weights[:, :, None], 0.0), axis=1)
    before = (
        lax.broadcasted_iota(jnp.int32, (length, length), 0)
        > lax.broadcasted_iota(jnp.int32, (length, length), 1)
    ).astype(bf16)
    rank = jnp.dot(before, chosen.astype(bf16), preferred_element_type=f32)
    slots = jnp.where(chosen, rank, -1.0)
    gate_high = jnp.floor(gates * 128.0) * (1.0 / 128.0)
    meta = jnp.concatenate([slots, gate_high, gates - gate_high], axis=1).astype(bf16)
    extra = -(-3 * devices // 128) * 128
    meta = jnp.pad(meta, ((0, 0), (0, extra - 3 * devices)))

    up_local = up_weight[0]
    down_local = down_weight[0]
    hops = list(range(0, plane, 2))
    two = 2 * capacity

    def serve(block):
        both = jnp.concatenate([block, swap(block, 1)], axis=0)
        here = both[:, model:]
        ours = lax.dynamic_slice(
            jnp.stack([here[:, :devices], here[:, devices : 2 * devices], here[:, 2 * devices : 3 * devices]]),
            (0, 0, place * plane),
            (3, 2 * length, plane),
        ).astype(f32)
        column = [lax.dynamic_slice_in_dim(ours, r ^ m, 1, 2) for m in hops]
        column = jnp.concatenate(column, axis=2)
        slot = jnp.where(column[0] < 0, -1.0, column[0])
        late = (lax.broadcasted_iota(jnp.int32, slot.shape, 0) >= length) & (slot >= 0)
        slot = slot + jnp.where(late, float(capacity), 0.0)
        gate = column[1] + column[2]
        wanted = slot[:, :, None] == jnp.arange(two, dtype=f32)[None, None, :]
        take = wanted.astype(bf16).reshape(2 * length, len(hops) * two)
        weigh = (
            jnp.where(wanted, gate[:, :, None], 0.0).astype(bf16).reshape(2 * length, len(hops) * two)
        )
        sent = dot(take, both[:, :model], ((0,), (0,))).astype(bf16)
        sent = [sent[k * two : (k + 1) * two] for k in range(len(hops))]
        arrived = [sent[0]] + [swap(sent[k], hops[k]) for k in range(1, len(hops))]
        return weigh, arrived

    def work(arrived):
        rows = jnp.concatenate(arrived, axis=0)
        up = jnp.dot(rows, up_local, preferred_element_type=f32)
        squared = jnp.square(jax.nn.relu(up)).astype(bf16)
        result = jnp.dot(squared, down_local, preferred_element_type=f32).astype(bf16)
        parts = [result[k * two : (k + 1) * two] for k in range(len(hops))]
        return [parts[0]] + [swap(parts[k], hops[k]) for k in range(1, len(hops))]

    def gather_up(weigh, returned):
        part = jnp.dot(weigh, jnp.concatenate(returned, axis=0), preferred_element_type=f32)
        return part[:length] + swap(part[length:].astype(bf16), 1).astype(f32)

    block = jnp.concatenate([moe_in, meta], axis=1)
    blocks = [block]
    for _ in range(outer - 1):
        blocks.append(turn(blocks[-1]))
    served = [serve(b) for b in blocks]
    returned = [work(s[1]) for s in served]
    carried = None
    for step in list(range(1, outer)) + [0]:
        part = gather_up(served[step][0], returned[step])
        if carried is not None:
            part = part + carried.astype(f32)
        if step:
            carried = turn(part.astype(bf16))
    return (residual_one.astype(f32) + part).astype(bf16)


def solution(mesh):
    placed = (
        P(AXES, None),
        P(AXES, None),
        P(AXES, None),
        P(None, AXES),
        P(),
        P(),
        P("grp", None),
        P(),
        P(AXES, None),
        P(AXES, None),
        P(),
        P(AXES, None, None),
        P(AXES, None, None),
    )
    return jax.shard_map(local, mesh=mesh, in_specs=placed, out_specs=P(AXES, None), check_vma=False)
```

time: 728 us -> 349 us (0.48)
  blocking collectives: 196 us -> 0 us
  waiting for transfers between devices: 359 us -> 207 us
  local copies, waits for them, and re-layouts: 99.1 us -> 33 us
  starting transfers between devices: 6.53 us -> 62.5 us
  other arithmetic: 20 us -> 7.16 us
  between operations: 13.5 us -> 1.02 us
    ppermute x1 -> x65, waiting for transfers between devices: 0.01 us -> 207 us  [the longest x55 136 us: swap(): return lax.ppermute(x, AXES, [(d, d ^ m) for d in range(devices)])]
    all_gather x3 -> x0, waiting for transfers between devices: 165 us -> none  [the longest x1 91.2 us: entering_2(): pieces = jax.tree.map(lambda part: lax.all_gather(part, axis), value)]
    all_to_all x1 -> x0, blocking collectives: 156 us -> none  [local(): lax.all_to_all(outgoing.reshape(devices, capacity, model_width), ('seq',...]
    all_to_all x1 -> x0, waiting for transfers between devices: 153 us -> none  [local(): lax.all_to_all(result.reshape(arrived.shape), ('seq', 'grp'), split_axis=...]
    ppermute x1 -> x65, starting transfers between devices: 2.36 us -> 62.5 us  [the longest x55 49.8 us: swap(): return lax.ppermute(x, AXES, [(d, d ^ m) for d in range(devices)])]
    reshape x7 -> x0, local copies, waits for them, and re-layouts: 48 us -> none  [the longest x1 8.31 us: local(): flattened = arrived.reshape(-1, arrived.shape[-1])]
    psum x1 -> x0, waiting for transfers between devices: 40.4 us -> none  [from_root(): return lax.psum(block, axis)]
    all_gather x2 -> x0, blocking collectives: 34.2 us -> none  [the longest x1 27 us: entering_2(): pieces = jax.tree.map(lambda part: lax.all_gather(part, axis), value)]
  transfers between devices with their start and end apart: 6 -> 65, of which waited for: 5 -> 28; matrix products, arithmetic and copies ran while one was open for 3% -> 16% of each run, Pallas kernels for 0% -> 2%
where the time goes in v1:
time: 349 us; the launch traced here: 348 us
  waiting for transfers between devices  207 us (59%)
  starting transfers between devices  62.5 us (18%)
  local copies, waits for them, and re-layouts  33 us (9%)
  matrix products  31.4 us (9%)
  other arithmetic  7.16 us (2%)
  Pallas kernels  5.51 us (2%)
    ppermute x55, waiting for transfers between devices, swap(): return lax.ppermute(x, AXES, [(d, d ^ m) for d in range(devices)])  136 us
    ppermute x6, waiting for transfers between devices, turn(): lax.ppermute(x, AXES, [(d, (d + plane) % devices) for d in range(devices)])  69.3 us
    ppermute x55, starting transfers between devices, swap(): return lax.ppermute(x, AXES, [(d, d ^ m) for d in range(devices)])  49.8 us
    another operation x15, local copies, waits for them, and re-layouts, serve(): jnp.stack([here[:, :devices], here[:, devices:2 * devices], here[:, 2 * d...  17.5 us
    ppermute x4, starting transfers between devices, onward(): lax.ppermute(x, AXES, [(d, d + by) for d in range(devices) if d + by < de...  11.6 us
    dot_general x10, matrix products, project(): return jnp.dot(part, rows, preferred_element_type=f32)  9.97 us
    dot_general x4, matrix products, work(): jnp.dot(squared, down_local, preferred_element_type=f32).astype(bf16)  7.65 us
    dot_general x4, matrix products, work(): up = jnp.dot(rows, up_local, preferred_element_type=f32)  7.64 us
  transfers between devices with their start and end apart: 65, of which 28 were waited for; matrix products, arithmetic and copies ran while one was open for 16% of the time, Pallas kernels for 2%

profile of v1, /device:TPU:0, one launch (start us, length us, event | category | flops | bytes accessed | tf_op | source)
XLA Modules:
  0.0 347.9 jit_solution(17293129900211913373)
XLA Ops:
  1.0 2.4 collective-permute-start
  3.3 2.7 collective-permute-start.18
  6.0 2.5 constant_dynamic-slice_fusion.16
  8.6 2.0 shard_map.127
  12.6 2.3 collective-permute-start.4
  14.9 2.2 collective-permute-start.6
  19.8 2.1 collective-permute-done.7.rest_7_
  22.0 5.4 %collective-permute-start.10 = (bf16[80,256]{1,0:T(8,128)(2,1)S(1)}, bf16[80,256]{1,0:T(8,128)(2,1)S(1)}, u32[]{:S(2)}, u32[]{:S(2)}) collective-permute-start(bf16[80,256]{1,0:T(8,128)(2,1)S(1)} %shard_map.129), channel_id=1, source_target_pairs={{0,24},{1,25},{2,26},{3,27},{4,28},{5,29},{6,30},{7,31}} | collective-permute-start | bytes 122888 | tf_op jit(solution)/shard_map/ppermute | solution.py:214
  28.8 2.5 collective-permute-start.9
  31.3 1.6 collective-permute-done.9.rest_9_
  33.1 1.6 collective-permute-start.12
  35.0 1.6 collective-permute-start.23
  41.0 3.0 collective-permute-start.16
  44.4 1.6 shard_map.128.inside_ref
  46.1 9.1 %collective-permute-done.16.rest_6_ = bf16[64,256]{1,0:T(8,128)(2,1)S(1)} collective-permute-done((bf16[64,256]{1,0:T(8,128)(2,1)S(1)}, bf16[64,256]{1,0:T(8,128)(2,1)S(1)}, u32[]{:S(2)}, u32[]{:S(2)}) %collective-permute-start.16) | collective-permute-done | bytes 32800 | tf_op jit(solution)/shard_map/ppermute | solution.py:211
  55.2 1.7 shard_map.131
  57.7 2.4 convolution_add_fusion.5
  60.2 1.6 collective-permute-start.25
  64.9 10.9 %collective-permute-done.21 = bf16[128,2688]{1,0:T(8,128)(2,1)S(1)} collective-permute-done((bf16[128,2688]{1,0:T(8,128)(2,1)}, bf16[128,2688]{1,0:T(8,128)(2,1)S(1)}, u32[]{:S(2)}, u32[]{:S(2)}) %collective-permute-start.21) | collective-permute-done | bytes 688160 | tf_op jit(solution)/shard_map/ppermute | solution.py:211
  76.1 13.6 %collective-permute-done.25 = bf16[128,2688]{1,0:T(8,128)(2,1)S(1)} collective-permute-done((bf16[128,2688]{1,0:T(8,128)(2,1)}, bf16[128,2688]{1,0:T(8,128)(2,1)S(1)}, u32[]{:S(2)}, u32[]{:S(2)}) %collective-permute-start.25) | collective-permute-done | bytes 688160 | tf_op jit(solution)/shard_map/ppermute | solution.py:211
  90.1 2.4 fusion.31
  95.8 19.3 %collective-permute-done.35 = bf16[128,2816]{1,0:T(8,128)(2,1)} collective-permute-done((bf16[128,2816]{1,0:T(8,128)(2,1)S(1)}, bf16[128,2816]{1,0:T(8,128)(2,1)}, u32[]{:S(2)}, u32[]{:S(2)}) %collective-permute-start.35) | collective-permute-done | bytes 720928 | tf_op jit(solution)/shard_map/ppermute | solution.py:219
  119.0 15.9 %collective-permute-done.36 = bf16[128,2816]{1,0:T(8,128)(2,1)} collective-permute-done((bf16[128,2816]{1,0:T(8,128)(2,1)}, bf16[128,2816]{1,0:T(8,128)(2,1)}, u32[]{:S(2)}, u32[]{:S(2)}) %collective-permute-start.36) | collective-permute-done | bytes 720928 | tf_op jit(solution)/shard_map/ppermute | solution.py:219
  151.7 10.5 %collective-permute-done.37 = bf16[128,2816]{1,0:T(8,128)(2,1)} collective-permute-done((bf16[128,2816]{1,0:T(8,128)(2,1)}, bf16[128,2816]{1,0:T(8,128)(2,1)}, u32[]{:S(2)}, u32[]{:S(2)}) %collective-permute-start.37) | collective-permute-done | bytes 720928 | tf_op jit(solution)/shard_map/ppermute | solution.py:219
  176.1 1.7 collective-permute-start.57
  182.9 3.2 collective-permute-done.55
  187.3 8.4 %collective-permute-done.56 = bf16[72,2688]{1,0:T(8,128)(2,1)S(1)} collective-permute-done((bf16[72,2688]{1,0:T(8,128)(2,1)S(1)}, bf16[72,2688]{1,0:T(8,128)(2,1)S(1)}, u32[]{:S(2)}, u32[]{:S(2)}) %collective-permute-start.56) | collective-permute-done | bytes 387104 | tf_op jit(solution)/shard_map/ppermute | solution.py:211
  197.7 1.9 fusion.146
  199.6 1.8 fusion.25
  204.0 8.4 %collective-permute-done.48 = bf16[72,2688]{1,0:T(8,128)(2,1)S(1)} collective-permute-done((bf16[72,2688]{1,0:T(8,128)(2,1)S(1)}, bf16[72,2688]{1,0:T(8,128)(2,1)S(1)}, u32[]{:S(2)}, u32[]{:S(2)}) %collective-permute-start.48) | collective-permute-done | bytes 387104 | tf_op jit(solution)/shard_map/ppermute | solution.py:211
  214.2 1.9 fusion.151
  216.1 1.9 fusion.22
  220.6 8.4 %collective-permute-done.40 = bf16[72,2688]{1,0:T(8,128)(2,1)S(1)} collective-permute-done((bf16[72,2688]{1,0:T(8,128)(2,1)S(1)}, bf16[72,2688]{1,0:T(8,128)(2,1)S(1)}, u32[]{:S(2)}, u32[]{:S(2)}) %collective-permute-start.40) | collective-permute-done | bytes 387104 | tf_op jit(solution)/shard_map/ppermute | solution.py:211
  230.8 1.9 fusion.156
  232.8 2.1 fusion.19
  234.9 17.4 %collective-permute-done.58 = bf16[72,2688]{1,0:T(8,128)(2,1)S(1)} collective-permute-done((bf16[72,2688]{1,0:T(8,128)(2,1)S(1)}, bf16[72,2688]{1,0:T(8,128)(2,1)S(1)}, u32[]{:S(2)}, u32[]{:S(2)}) %collective-permute-start.58) | collective-permute-done | bytes 387104 | tf_op jit(solution)/shard_map/ppermute | solution.py:211
  255.1 9.9 %collective-permute-done.60 = bf16[72,2688]{1,0:T(8,128)(2,1)S(1)} collective-permute-done((bf16[72,2688]{1,0:T(8,128)(2,1)S(1)}, bf16[72,2688]{1,0:T(8,128)(2,1)S(1)}, u32[]{:S(2)}, u32[]{:S(2)}) %collective-permute-start.60) | collective-permute-done | bytes 387104 | tf_op jit(solution)/shard_map/ppermute | solution.py:211
  267.2 1.7 collective-permute-start.52
  269.6 1.9 fusion.161
  273.9 9.1 %collective-permute-done.51 = bf16[72,2688]{1,0:T(8,128)(2,1)S(1)} collective-permute-done((bf16[72,2688]{1,0:T(8,128)(2,1)S(1)}, bf16[72,2688]{1,0:T(8,128)(2,1)S(1)}, u32[]{:S(2)}, u32[]{:S(2)}) %collective-permute-start.51) | collective-permute-done | bytes 387104 | tf_op jit(solution)/shard_map/ppermute | solution.py:211
  285.6 1.9 fusion.16
  287.4 2.3 collective-permute-done.42
  289.7 8.6 %collective-permute-done.43 = bf16[72,2688]{1,0:T(8,128)(2,1)S(1)} collective-permute-done((bf16[72,2688]{1,0:T(8,128)(2,1)S(1)}, bf16[72,2688]{1,0:T(8,128)(2,1)S(1)}, u32[]{:S(2)}, u32[]{:S(2)}) %collective-permute-start.43) | collective-permute-done | bytes 387104 | tf_op jit(solution)/shard_map/ppermute | solution.py:211
  299.4 5.7 %collective-permute-done.62 = bf16[128,2688]{1,0:T(8,128)(2,1)S(1)} collective-permute-done((bf16[128,2688]{1,0:T(8,128)(2,1)S(1)}, bf16[128,2688]{1,0:T(8,128)(2,1)S(1)}, u32[]{:S(2)}, u32[]{:S(2)}) %collective-permute-start.62) | collective-permute-done | bytes 688160 | tf_op jit(solution)/shard_map/ppermute | solution.py:219
  309.2 8.4 %collective-permute-done.31 = bf16[72,2688]{1,0:T(8,128)(2,1)S(1)} collective-permute-done((bf16[72,2688]{1,0:T(8,128)(2,1)S(1)}, bf16[72,2688]{1,0:T(8,128)(2,1)S(1)}, u32[]{:S(2)}, u32[]{:S(2)}) %collective-permute-start.31) | collective-permute-done | bytes 387104 | tf_op jit(solution)/shard_map/ppermute | solution.py:211
  317.6 8.1 %collective-permute-done.32 = bf16[72,2688]{1,0:T(8,128)(2,1)S(1)} collective-permute-done((bf16[72,2688]{1,0:T(8,128)(2,1)S(1)}, bf16[72,2688]{1,0:T(8,128)(2,1)S(1)}, u32[]{:S(2)}, u32[]{:S(2)}) %collective-permute-start.32) | collective-permute-done | bytes 387104 | tf_op jit(solution)/shard_map/ppermute | solution.py:211
  327.1 1.8 collective-permute-done.34
  328.9 17.8 %collective-permute-done.64 = bf16[128,2688]{1,0:T(8,128)(2,1)S(1)} collective-permute-done((bf16[128,2688]{1,0:T(8,128)(2,1)S(1)}, bf16[128,2688]{1,0:T(8,128)(2,1)S(1)}, u32[]{:S(2)}, u32[]{:S(2)}) %collective-permute-start.64) | collective-permute-done | bytes 688160 | tf_op jit(solution)/shard_map/ppermute | solution.py:219
  (237 shorter events, 89.8 us)
Async XLA Ops:
  1.0 7.6 %collective-permute-start = (bf16[16,3072]{1,0:T(8,128)(2,1)S(1)}, bf16[16,3072]{1,0:T(8,128)(2,1)S(1)}, u32[]{:S(2)}, u32[]{:S(2)}) collective-permute-start(bf16[16,3072]{1,0:T(8,128)(2,1)S(1)} %slice.237), channel_id=1, source_target_pairs={{0,1},{1,2},{2,3},{3,4},{4,5},{5,6},{6,7},{7,8},{8,9},{9,10},{10,1... | collective-permute-start | bytes 294920 | tf_op jit(solution)/shard_map/ppermute | solution.py:214
  3.3 86.7 %collective-permute-start.18 = (bf16[512,2688]{1,0:T(8,128)(2,1)}, bf16[512,2688]{1,0:T(8,128)(2,1)}, u32[]{:S(2)}, u32[]{:S(2)}) collective-permute-start(bf16[512,2688]{1,0:T(8,128)(2,1)} %param.19), channel_id=1, source_target_pairs={{0,1},{1,0},{2,3},{3,2},{4,5},{5,4},{6,7},{7,6},{8,9},{9,8},{10,11... | collective-permute-start | bytes 8257544 | tf_op jit(solution)/shard_map/ppermute | solution.py:211
  17.7 39.5 %collective-permute-start.19 = (bf16[128,2688]{1,0:T(8,128)(2,1)}, bf16[128,2688]{1,0:T(8,128)(2,1)}, u32[]{:S(2)}, u32[]{:S(2)}) collective-permute-start(bf16[128,2688]{1,0:T(8,128)(2,1)} %get-tuple-element.43), channel_id=1, source_target_pairs={{0,2},{1,3},{2,0},{3,1},{4,6},{5,7},{6,4},{7,5},{8,10},{9,11},{10,... | collective-permute-start | bytes 2064392 | tf_op jit(solution)/shard_map/ppermute | solution.py:211
  22.0 9.2 %collective-permute-start.10 = (bf16[80,256]{1,0:T(8,128)(2,1)S(1)}, bf16[80,256]{1,0:T(8,128)(2,1)S(1)}, u32[]{:S(2)}, u32[]{:S(2)}) collective-permute-start(bf16[80,256]{1,0:T(8,128)(2,1)S(1)} %shard_map.129), channel_id=1, source_target_pairs={{0,24},{1,25},{2,26},{3,27},{4,28},{5,29},{6,30},{7,31}} | collective-permute-start | bytes 122888 | tf_op jit(solution)/shard_map/ppermute | solution.py:214
  35.0 25.1 %collective-permute-start.23 = (bf16[128,2688]{1,0:T(8,128)(2,1)}, bf16[128,2688]{1,0:T(8,128)(2,1)}, u32[]{:S(2)}, u32[]{:S(2)}) collective-permute-start(bf16[128,2688]{1,0:T(8,128)(2,1)} %get-tuple-element.44), channel_id=1, source_target_pairs={{0,2},{1,3},{2,0},{3,1},{4,6},{5,7},{6,4},{7,5},{8,10},{9,11},{10,... | collective-permute-start | bytes 2064392 | tf_op jit(solution)/shard_map/ppermute | solution.py:211
  41.0 14.2 %collective-permute-start.16 = (bf16[64,256]{1,0:T(8,128)(2,1)S(1)}, bf16[64,256]{1,0:T(8,128)(2,1)S(1)}, u32[]{:S(2)}, u32[]{:S(2)}) collective-permute-start(bf16[64,256]{1,0:T(8,128)(2,1)S(1)} %get-tuple-element.41), channel_id=1, source_target_pairs={{0,6},{1,7},{2,4},{3,5},{4,2},{5,3},{6,0},{7,1},{8,14},{9,15},{10,... | collective-permute-start | bytes 98312 | tf_op jit(solution)/shard_map/ppermute | solution.py:211
  44.1 11.1 %collective-permute-start.17 = (bf16[64,256]{1,0:T(8,128)(2,1)S(1)}, bf16[64,256]{1,0:T(8,128)(2,1)S(1)}, u32[]{:S(2)}, u32[]{:S(2)}) collective-permute-start(bf16[64,256]{1,0:T(8,128)(2,1)S(1)} %get-tuple-element.42), channel_id=1, source_target_pairs={{0,7},{1,6},{2,5},{3,4},{4,3},{5,2},{6,1},{7,0},{8,15},{9,14},{10,... | collective-permute-start | bytes 98312 | tf_op jit(solution)/shard_map/ppermute | solution.py:211
  57.2 18.6 %collective-permute-start.21 = (bf16[128,2688]{1,0:T(8,128)(2,1)}, bf16[128,2688]{1,0:T(8,128)(2,1)S(1)}, u32[]{:S(2)}, u32[]{:S(2)}) collective-permute-start(bf16[128,2688]{1,0:T(8,128)(2,1)} %collective-permute-done.19), channel_id=1, source_target_pairs={{0,4},{1,5},{2,6},{3,7},{4,0},{5,1},{6,2},{7,3},{8,12},{9,13},{10,... | collective-permute-start | bytes 2064392 | tf_op jit(solution)/shard_map/ppermute | solution.py:211
  60.1 32.4 %collective-permute-start.20 = (bf16[128,2688]{1,0:T(8,128)(2,1)}, bf16[128,2688]{1,0:T(8,128)(2,1)S(1)}, u32[]{:S(2)}, u32[]{:S(2)}) collective-permute-start(bf16[128,2688]{1,0:T(8,128)(2,1)} %collective-permute-done.19), channel_id=1, source_target_pairs={{0,1},{1,0},{2,3},{3,2},{4,5},{5,4},{6,7},{7,6},{8,9},{9,8},{10,11... | collective-permute-start | bytes 2064392 | tf_op jit(solution)/shard_map/ppermute | solution.py:211
  60.2 29.5 %collective-permute-start.25 = (bf16[128,2688]{1,0:T(8,128)(2,1)}, bf16[128,2688]{1,0:T(8,128)(2,1)S(1)}, u32[]{:S(2)}, u32[]{:S(2)}) collective-permute-start(bf16[128,2688]{1,0:T(8,128)(2,1)} %collective-permute-done.23), channel_id=1, source_target_pairs={{0,4},{1,5},{2,6},{3,7},{4,0},{5,1},{6,2},{7,3},{8,12},{9,13},{10,... | collective-permute-start | bytes 2064392 | tf_op jit(solution)/shard_map/ppermute | solution.py:211
  61.8 31.5 %collective-permute-start.24 = (bf16[128,2688]{1,0:T(8,128)(2,1)}, bf16[128,2688]{1,0:T(8,128)(2,1)S(1)}, u32[]{:S(2)}, u32[]{:S(2)}) collective-permute-start(bf16[128,2688]{1,0:T(8,128)(2,1)} %collective-permute-done.23), channel_id=1, source_target_pairs={{0,1},{1,0},{2,3},{3,2},{4,5},{5,4},{6,7},{7,6},{8,9},{9,8},{10,11... | collective-permute-start | bytes 2064392 | tf_op jit(solution)/shard_map/ppermute | solution.py:211
  75.7 17.1 %collective-permute-start.22 = (bf16[128,2688]{1,0:T(8,128)(2,1)S(1)}, bf16[128,2688]{1,0:T(8,128)(2,1)S(1)}, u32[]{:S(2)}, u32[]{:S(2)}) collective-permute-start(bf16[128,2688]{1,0:T(8,128)(2,1)S(1)} %collective-permute-done.21), channel_id=1, source_target_pairs={{0,1},{1,0},{2,3},{3,2},{4,5},{5,4},{6,7},{7,6},{8,9},{9,8},{10,11... | collective-permute-start | bytes 2064392 | tf_op jit(solution)/shard_map/ppermute | solution.py:211
  94.6 20.5 %collective-permute-start.35 = (bf16[128,2816]{1,0:T(8,128)(2,1)S(1)}, bf16[128,2816]{1,0:T(8,128)(2,1)}, u32[]{:S(2)}, u32[]{:S(2)}) collective-permute-start(bf16[128,2816]{1,0:T(8,128)(2,1)S(1)} %pad_maximum_fusion.4), channel_id=1, source_target_pairs={{0,8},{1,9},{2,10},{3,11},{4,12},{5,13},{6,14},{7,15},{8,16},{9,17... | collective-permute-start | bytes 2162696 | tf_op jit(solution)/shard_map/ppermute | solution.py:219
  95.6 20.7 %collective-permute-start.27 = (bf16[128,2816]{1,0:T(8,128)(2,1)S(1)}, bf16[128,2816]{1,0:T(8,128)(2,1)S(1)}, u32[]{:S(2)}, u32[]{:S(2)}) collective-permute-start(bf16[128,2816]{1,0:T(8,128)(2,1)S(1)} %pad_maximum_fusion.4), channel_id=1, source_target_pairs={{0,1},{1,0},{2,3},{3,2},{4,5},{5,4},{6,7},{7,6},{8,9},{9,8},{10,11... | collective-permute-start | bytes 2162696 | tf_op jit(solution)/shard_map/ppermute | solution.py:211
  115.1 19.9 %collective-permute-start.36 = (bf16[128,2816]{1,0:T(8,128)(2,1)}, bf16[128,2816]{1,0:T(8,128)(2,1)}, u32[]{:S(2)}, u32[]{:S(2)}) collective-permute-start(bf16[128,2816]{1,0:T(8,128)(2,1)} %collective-permute-done.35), channel_id=1, source_target_pairs={{0,8},{1,9},{2,10},{3,11},{4,12},{5,13},{6,14},{7,15},{8,16},{9,17... | collective-permute-start | bytes 2162696 | tf_op jit(solution)/shard_map/ppermute | solution.py:219
  115.1 19.9 %collective-permute-start.54 = (bf16[128,2816]{1,0:T(8,128)(2,1)}, bf16[128,2816]{1,0:T(8,128)(2,1)}, u32[]{:S(2)}, u32[]{:S(2)}) collective-permute-start(bf16[128,2816]{1,0:T(8,128)(2,1)} %collective-permute-done.35), channel_id=1, source_target_pairs={{0,1},{1,0},{2,3},{3,2},{4,5},{5,4},{6,7},{7,6},{8,9},{9,8},{10,11... | collective-permute-start | bytes 2162696 | tf_op jit(solution)/shard_map/ppermute | solution.py:211
  135.0 7.7 %collective-permute-start.46 = (bf16[128,2816]{1,0:T(8,128)(2,1)}, bf16[128,2816]{1,0:T(8,128)(2,1)}, u32[]{:S(2)}, u32[]{:S(2)}) collective-permute-start(bf16[128,2816]{1,0:T(8,128)(2,1)} %collective-permute-done.36), channel_id=1, source_target_pairs={{0,1},{1,0},{2,3},{3,2},{4,5},{5,4},{6,7},{7,6},{8,9},{9,8},{10,11... | collective-permute-start | bytes 2162696 | tf_op jit(solution)/shard_map/ppermute | solution.py:211
  141.5 20.7 %collective-permute-start.37 = (bf16[128,2816]{1,0:T(8,128)(2,1)}, bf16[128,2816]{1,0:T(8,128)(2,1)}, u32[]{:S(2)}, u32[]{:S(2)}) collective-permute-start(bf16[128,2816]{1,0:T(8,128)(2,1)} %collective-permute-done.36), channel_id=1, source_target_pairs={{0,8},{1,9},{2,10},{3,11},{4,12},{5,13},{6,14},{7,15},{8,16},{9,17... | collective-permute-start | bytes 2162696 | tf_op jit(solution)/shard_map/ppermute | solution.py:219
  174.2 11.8 %collective-permute-start.55 = (bf16[72,2688]{1,0:T(8,128)(2,1)S(1)}, bf16[72,2688]{1,0:T(8,128)(2,1)S(1)}, u32[]{:S(2)}, u32[]{:S(2)}) collective-permute-start(bf16[72,2688]{1,0:T(8,128)(2,1)S(1)} %get-tuple-element.52), channel_id=1, source_target_pairs={{0,2},{1,3},{2,0},{3,1},{4,6},{5,7},{6,4},{7,5},{8,10},{9,11},{10,... | collective-permute-start | bytes 1161224 | tf_op jit(solution)/shard_map/ppermute | solution.py:211
  175.7 20.1 %collective-permute-start.56 = (bf16[72,2688]{1,0:T(8,128)(2,1)S(1)}, bf16[72,2688]{1,0:T(8,128)(2,1)S(1)}, u32[]{:S(2)}, u32[]{:S(2)}) collective-permute-start(bf16[72,2688]{1,0:T(8,128)(2,1)S(1)} %get-tuple-element.51), channel_id=1, source_target_pairs={{0,4},{1,5},{2,6},{3,7},{4,0},{5,1},{6,2},{7,3},{8,12},{9,13},{10,... | collective-permute-start | bytes 1161224 | tf_op jit(solution)/shard_map/ppermute | solution.py:211
  176.1 20.3 %collective-permute-start.57 = (bf16[72,2688]{1,0:T(8,128)(2,1)S(1)}, bf16[72,2688]{1,0:T(8,128)(2,1)S(1)}, u32[]{:S(2)}, u32[]{:S(2)}) collective-permute-start(bf16[72,2688]{1,0:T(8,128)(2,1)S(1)} %get-tuple-element.50), channel_id=1, source_target_pairs={{0,6},{1,7},{2,4},{3,5},{4,2},{5,3},{6,0},{7,1},{8,14},{9,15},{10,... | collective-permute-start | bytes 1161224 | tf_op jit(solution)/shard_map/ppermute | solution.py:211
  178.5 24.2 %collective-permute-start.47 = (bf16[72,2688]{1,0:T(8,128)(2,1)S(1)}, bf16[72,2688]{1,0:T(8,128)(2,1)S(1)}, u32[]{:S(2)}, u32[]{:S(2)}) collective-permute-start(bf16[72,2688]{1,0:T(8,128)(2,1)S(1)} %get-tuple-element.60), channel_id=1, source_target_pairs={{0,2},{1,3},{2,0},{3,1},{4,6},{5,7},{6,4},{7,5},{8,10},{9,11},{10,... | collective-permute-start | bytes 1161224 | tf_op jit(solution)/shard_map/ppermute | solution.py:211
  179.9 32.4 %collective-permute-start.48 = (bf16[72,2688]{1,0:T(8,128)(2,1)S(1)}, bf16[72,2688]{1,0:T(8,128)(2,1)S(1)}, u32[]{:S(2)}, u32[]{:S(2)}) collective-permute-start(bf16[72,2688]{1,0:T(8,128)(2,1)S(1)} %get-tuple-element.59), channel_id=1, source_target_pairs={{0,4},{1,5},{2,6},{3,7},{4,0},{5,1},{6,2},{7,3},{8,12},{9,13},{10,... | collective-permute-start | bytes 1161224 | tf_op jit(solution)/shard_map/ppermute | solution.py:211
  186.1 27.0 %collective-permute-start.49 = (bf16[72,2688]{1,0:T(8,128)(2,1)S(1)}, bf16[72,2688]{1,0:T(8,128)(2,1)S(1)}, u32[]{:S(2)}, u32[]{:S(2)}) collective-permute-start(bf16[72,2688]{1,0:T(8,128)(2,1)S(1)} %get-tuple-element.58), channel_id=1, source_target_pairs={{0,6},{1,7},{2,4},{3,5},{4,2},{5,3},{6,0},{7,1},{8,14},{9,15},{10,... | collective-permute-start | bytes 1161224 | tf_op jit(solution)/shard_map/ppermute | solution.py:211
  195.8 23.6 %collective-permute-start.39 = (bf16[72,2688]{1,0:T(8,128)(2,1)S(1)}, bf16[72,2688]{1,0:T(8,128)(2,1)S(1)}, u32[]{:S(2)}, u32[]{:S(2)}) collective-permute-start(bf16[72,2688]{1,0:T(8,128)(2,1)S(1)} %get-tuple-element.68), channel_id=1, source_target_pairs={{0,2},{1,3},{2,0},{3,1},{4,6},{5,7},{6,4},{7,5},{8,10},{9,11},{10,... | collective-permute-start | bytes 1161224 | tf_op jit(solution)/shard_map/ppermute | solution.py:211
  196.4 32.5 %collective-permute-start.40 = (bf16[72,2688]{1,0:T(8,128)(2,1)S(1)}, bf16[72,2688]{1,0:T(8,128)(2,1)S(1)}, u32[]{:S(2)}, u32[]{:S(2)}) collective-permute-start(bf16[72,2688]{1,0:T(8,128)(2,1)S(1)} %get-tuple-element.67), channel_id=1, source_target_pairs={{0,4},{1,5},{2,6},{3,7},{4,0},{5,1},{6,2},{7,3},{8,12},{9,13},{10,... | collective-permute-start | bytes 1161224 | tf_op jit(solution)/shard_map/ppermute | solution.py:211
  202.7 26.9 %collective-permute-start.41 = (bf16[72,2688]{1,0:T(8,128)(2,1)S(1)}, bf16[72,2688]{1,0:T(8,128)(2,1)S(1)}, u32[]{:S(2)}, u32[]{:S(2)}) collective-permute-start(bf16[72,2688]{1,0:T(8,128)(2,1)S(1)} %get-tuple-element.66), channel_id=1, source_target_pairs={{0,6},{1,7},{2,4},{3,5},{4,2},{5,3},{6,0},{7,1},{8,14},{9,15},{10,... | collective-permute-start | bytes 1161224 | tf_op jit(solution)/shard_map/ppermute | solution.py:211
  212.4 54.9 %collective-permute-start.28 = (bf16[72,2688]{1,0:T(8,128)(2,1)S(1)}, bf16[72,2688]{1,0:T(8,128)(2,1)S(1)}, u32[]{:S(2)}, u32[]{:S(2)}) collective-permute-start(bf16[72,2688]{1,0:T(8,128)(2,1)S(1)} %get-tuple-element.76), channel_id=1, source_target_pairs={{0,2},{1,3},{2,0},{3,1},{4,6},{5,7},{6,4},{7,5},{8,10},{9,11},{10,... | collective-permute-start | bytes 1161224 | tf_op jit(solution)/shard_map/ppermute | solution.py:211
  213.0 55.9 %collective-permute-start.29 = (bf16[72,2688]{1,0:T(8,128)(2,1)S(1)}, bf16[72,2688]{1,0:T(8,128)(2,1)S(1)}, u32[]{:S(2)}, u32[]{:S(2)}) collective-permute-start(bf16[72,2688]{1,0:T(8,128)(2,1)S(1)} %get-tuple-element.75), channel_id=1, source_target_pairs={{0,4},{1,5},{2,6},{3,7},{4,0},{5,1},{6,2},{7,3},{8,12},{9,13},{10,... | collective-permute-start | bytes 1161224 | tf_op jit(solution)/shard_map/ppermute | solution.py:211
  219.4 50.2 %collective-permute-start.30 = (bf16[72,2688]{1,0:T(8,128)(2,1)S(1)}, bf16[72,2688]{1,0:T(8,128)(2,1)S(1)}, u32[]{:S(2)}, u32[]{:S(2)}) collective-permute-start(bf16[72,2688]{1,0:T(8,128)(2,1)S(1)} %get-tuple-element.74), channel_id=1, source_target_pairs={{0,6},{1,7},{2,4},{3,5},{4,2},{5,3},{6,0},{7,1},{8,14},{9,15},{10,... | collective-permute-start | bytes 1161224 | tf_op jit(solution)/shard_map/ppermute | solution.py:211
  229.0 23.3 %collective-permute-start.58 = (bf16[72,2688]{1,0:T(8,128)(2,1)S(1)}, bf16[72,2688]{1,0:T(8,128)(2,1)S(1)}, u32[]{:S(2)}, u32[]{:S(2)}) collective-permute-start(bf16[72,2688]{1,0:T(8,128)(2,1)S(1)} %get-tuple-element.48), channel_id=1, source_target_pairs={{0,2},{1,3},{2,0},{3,1},{4,6},{5,7},{6,4},{7,5},{8,10},{9,11},{10,... | collective-permute-start | bytes 1161224 | tf_op jit(solution)/shard_map/ppermute | solution.py:211
  229.6 24.0 %collective-permute-start.59 = (bf16[72,2688]{1,0:T(8,128)(2,1)S(1)}, bf16[72,2688]{1,0:T(8,128)(2,1)S(1)}, u32[]{:S(2)}, u32[]{:S(2)}) collective-permute-start(bf16[72,2688]{1,0:T(8,128)(2,1)S(1)} %get-tuple-element.47), channel_id=1, source_target_pairs={{0,4},{1,5},{2,6},{3,7},{4,0},{5,1},{6,2},{7,3},{8,12},{9,13},{10,... | collective-permute-start | bytes 1161224 | tf_op jit(solution)/shard_map/ppermute | solution.py:211
  252.2 12.8 %collective-permute-start.60 = (bf16[72,2688]{1,0:T(8,128)(2,1)S(1)}, bf16[72,2688]{1,0:T(8,128)(2,1)S(1)}, u32[]{:S(2)}, u32[]{:S(2)}) collective-permute-start(bf16[72,2688]{1,0:T(8,128)(2,1)S(1)} %get-tuple-element.46), channel_id=1, source_target_pairs={{0,6},{1,7},{2,4},{3,5},{4,2},{5,3},{6,0},{7,1},{8,14},{9,15},{10,... | collective-permute-start | bytes 1161224 | tf_op jit(solution)/shard_map/ppermute | solution.py:211
  253.6 19.5 %collective-permute-start.50 = (bf16[72,2688]{1,0:T(8,128)(2,1)S(1)}, bf16[72,2688]{1,0:T(8,128)(2,1)S(1)}, u32[]{:S(2)}, u32[]{:S(2)}) collective-permute-start(bf16[72,2688]{1,0:T(8,128)(2,1)S(1)} %get-tuple-element.56), channel_id=1, source_target_pairs={{0,2},{1,3},{2,0},{3,1},{4,6},{5,7},{6,4},{7,5},{8,10},{9,11},{10,... | collective-permute-start | bytes 1161224 | tf_op jit(solution)/shard_map/ppermute | solution.py:211
  265.0 18.0 %collective-permute-start.51 = (bf16[72,2688]{1,0:T(8,128)(2,1)S(1)}, bf16[72,2688]{1,0:T(8,128)(2,1)S(1)}, u32[]{:S(2)}, u32[]{:S(2)}) collective-permute-start(bf16[72,2688]{1,0:T(8,128)(2,1)S(1)} %get-tuple-element.55), channel_id=1, source_target_pairs={{0,4},{1,5},{2,6},{3,7},{4,0},{5,1},{6,2},{7,3},{8,12},{9,13},{10,... | collective-permute-start | bytes 1161224 | tf_op jit(solution)/shard_map/ppermute | solution.py:211
  267.2 17.0 %collective-permute-start.52 = (bf16[72,2688]{1,0:T(8,128)(2,1)S(1)}, bf16[72,2688]{1,0:T(8,128)(2,1)S(1)}, u32[]{:S(2)}, u32[]{:S(2)}) collective-permute-start(bf16[72,2688]{1,0:T(8,128)(2,1)S(1)} %get-tuple-element.54), channel_id=1, source_target_pairs={{0,6},{1,7},{2,4},{3,5},{4,2},{5,3},{6,0},{7,1},{8,14},{9,15},{10,... | collective-permute-start | bytes 1161224 | tf_op jit(solution)/shard_map/ppermute | solution.py:211
  268.9 20.8 %collective-permute-start.42 = (bf16[72,2688]{1,0:T(8,128)(2,1)S(1)}, bf16[72,2688]{1,0:T(8,128)(2,1)S(1)}, u32[]{:S(2)}, u32[]{:S(2)}) collective-permute-start(bf16[72,2688]{1,0:T(8,128)(2,1)S(1)} %get-tuple-element.64), channel_id=1, source_target_pairs={{0,2},{1,3},{2,0},{3,1},{4,6},{5,7},{6,4},{7,5},{8,10},{9,11},{10,... | collective-permute-start | bytes 1161224 | tf_op jit(solution)/shard_map/ppermute | solution.py:211
  269.6 15.8 %collective-permute-start.61 = (bf16[128,2688]{1,0:T(8,128)(2,1)S(1)}, bf16[128,2688]{1,0:T(8,128)(2,1)S(1)}, u32[]{:S(2)}, u32[]{:S(2)}) collective-permute-start(bf16[128,2688]{1,0:T(8,128)(2,1)S(1)} %slice.447), channel_id=1, source_target_pairs={{0,1},{1,0},{2,3},{3,2},{4,5},{5,4},{6,7},{7,6},{8,9},{9,8},{10,11... | collective-permute-start | bytes 2064392 | tf_op jit(solution)/shard_map/ppermute | solution.py:211
  273.1 25.3 %collective-permute-start.43 = (bf16[72,2688]{1,0:T(8,128)(2,1)S(1)}, bf16[72,2688]{1,0:T(8,128)(2,1)S(1)}, u32[]{:S(2)}, u32[]{:S(2)}) collective-permute-start(bf16[72,2688]{1,0:T(8,128)(2,1)S(1)} %get-tuple-element.63), channel_id=1, source_target_pairs={{0,4},{1,5},{2,6},{3,7},{4,0},{5,1},{6,2},{7,3},{8,12},{9,13},{10,... | collective-permute-start | bytes 1161224 | tf_op jit(solution)/shard_map/ppermute | solution.py:211
  283.0 15.3 %collective-permute-start.44 = (bf16[72,2688]{1,0:T(8,128)(2,1)S(1)}, bf16[72,2688]{1,0:T(8,128)(2,1)S(1)}, u32[]{:S(2)}, u32[]{:S(2)}) collective-permute-start(bf16[72,2688]{1,0:T(8,128)(2,1)S(1)} %get-tuple-element.62), channel_id=1, source_target_pairs={{0,6},{1,7},{2,4},{3,5},{4,2},{5,3},{6,0},{7,1},{8,14},{9,15},{10,... | collective-permute-start | bytes 1161224 | tf_op jit(solution)/shard_map/ppermute | solution.py:211
  285.3 14.1 %collective-permute-start.53 = (bf16[128,2688]{1,0:T(8,128)(2,1)S(1)}, bf16[128,2688]{1,0:T(8,128)(2,1)S(1)}, u32[]{:S(2)}, u32[]{:S(2)}) collective-permute-start(bf16[128,2688]{1,0:T(8,128)(2,1)S(1)} %slice.448), channel_id=1, source_target_pairs={{0,1},{1,0},{2,3},{3,2},{4,5},{5,4},{6,7},{7,6},{8,9},{9,8},{10,11... | collective-permute-start | bytes 2064392 | tf_op jit(solution)/shard_map/ppermute | solution.py:211
  285.5 19.7 %collective-permute-start.62 = (bf16[128,2688]{1,0:T(8,128)(2,1)S(1)}, bf16[128,2688]{1,0:T(8,128)(2,1)S(1)}, u32[]{:S(2)}, u32[]{:S(2)}) collective-permute-start(bf16[128,2688]{1,0:T(8,128)(2,1)S(1)} %fusion.94), channel_id=1, source_target_pairs={{0,8},{1,9},{2,10},{3,11},{4,12},{5,13},{6,14},{7,15},{8,16},{9,17... | collective-permute-start | bytes 2064392 | tf_op jit(solution)/shard_map/ppermute | solution.py:219
  299.4 27.4 %collective-permute-start.45 = (bf16[128,2688]{1,0:T(8,128)(2,1)S(1)}, bf16[128,2688]{1,0:T(8,128)(2,1)S(1)}, u32[]{:S(2)}, u32[]{:S(2)}) collective-permute-start(bf16[128,2688]{1,0:T(8,128)(2,1)S(1)} %slice.449), channel_id=1, source_target_pairs={{0,1},{1,0},{2,3},{3,2},{4,5},{5,4},{6,7},{7,6},{8,9},{9,8},{10,11... | collective-permute-start | bytes 2064392 | tf_op jit(solution)/shard_map/ppermute | solution.py:211
  305.4 21.4 %collective-permute-start.63 = (bf16[128,2688]{1,0:T(8,128)(2,1)S(1)}, bf16[128,2688]{1,0:T(8,128)(2,1)S(1)}, u32[]{:S(2)}, u32[]{:S(2)}) collective-permute-start(bf16[128,2688]{1,0:T(8,128)(2,1)S(1)} %fusion.97), channel_id=1, source_target_pairs={{0,8},{1,9},{2,10},{3,11},{4,12},{5,13},{6,14},{7,15},{8,16},{9,17... | collective-permute-start | bytes 2064392 | tf_op jit(solution)/shard_map/ppermute | solution.py:219
  305.6 12.0 %collective-permute-start.31 = (bf16[72,2688]{1,0:T(8,128)(2,1)S(1)}, bf16[72,2688]{1,0:T(8,128)(2,1)S(1)}, u32[]{:S(2)}, u32[]{:S(2)}) collective-permute-start(bf16[72,2688]{1,0:T(8,128)(2,1)S(1)} %get-tuple-element.72), channel_id=1, source_target_pairs={{0,2},{1,3},{2,0},{3,1},{4,6},{5,7},{6,4},{7,5},{8,10},{9,11},{10,... | collective-permute-start | bytes 1161224 | tf_op jit(solution)/shard_map/ppermute | solution.py:211
  307.1 18.6 %collective-permute-start.32 = (bf16[72,2688]{1,0:T(8,128)(2,1)S(1)}, bf16[72,2688]{1,0:T(8,128)(2,1)S(1)}, u32[]{:S(2)}, u32[]{:S(2)}) collective-permute-start(bf16[72,2688]{1,0:T(8,128)(2,1)S(1)} %get-tuple-element.71), channel_id=1, source_target_pairs={{0,4},{1,5},{2,6},{3,7},{4,0},{5,1},{6,2},{7,3},{8,12},{9,13},{10,... | collective-permute-start | bytes 1161224 | tf_op jit(solution)/shard_map/ppermute | solution.py:211
  307.9 17.8 %collective-permute-start.33 = (bf16[72,2688]{1,0:T(8,128)(2,1)S(1)}, bf16[72,2688]{1,0:T(8,128)(2,1)S(1)}, u32[]{:S(2)}, u32[]{:S(2)}) collective-permute-start(bf16[72,2688]{1,0:T(8,128)(2,1)S(1)} %get-tuple-element.70), channel_id=1, source_target_pairs={{0,6},{1,7},{2,4},{3,5},{4,2},{5,3},{6,0},{7,1},{8,14},{9,15},{10,... | collective-permute-start | bytes 1161224 | tf_op jit(solution)/shard_map/ppermute | solution.py:211
  327.0 19.7 %collective-permute-start.64 = (bf16[128,2688]{1,0:T(8,128)(2,1)S(1)}, bf16[128,2688]{1,0:T(8,128)(2,1)S(1)}, u32[]{:S(2)}, u32[]{:S(2)}) collective-permute-start(bf16[128,2688]{1,0:T(8,128)(2,1)S(1)} %fusion.100), channel_id=1, source_target_pairs={{0,8},{1,9},{2,10},{3,11},{4,12},{5,13},{6,14},{7,15},{8,16},{9,17... | collective-permute-start | bytes 2064392 | tf_op jit(solution)/shard_map/ppermute | solution.py:219
  (42 other events, 262.8 us)

commit v2 on v1

--- a/solution.py
+++ b/solution.py
@@ -145,9 +145,10 @@
             out_ref[:, cols] = dot(mixing, act_ref[:, cols], ((1,), (0,)))
 
 
-def norm_kernel(plane, r_ref, act_ref, cumt_ref, inside_ref, z_ref, gain_ref, *rest):
-    incoming, out_ref, scr = rest[:plane], rest[plane], rest[plane + 1]
-    r = r_ref[0]
+def norm_kernel(plane, n_grp, r_ref, act_ref, cumt_ref, inside_ref, z_ref, gain_ref, *rest):
+    incoming, outs = rest[:plane], rest[plane : plane + n_grp // 2]
+    scr, mix = rest[-2], rest[-1]
+    r, grp = r_ref[0], r_ref[1]
     for m in range(plane):
         scr[r ^ m] = incoming[m][...]
     inner = z_ref.shape[1]
@@ -155,6 +156,7 @@
     per_group = heads // G
     width = inner // G
     head_size = inner // heads
+    per_shard = G // n_grp
     reach = jnp.exp(cumt_ref[...])
     for g in range(G):
         cols = slice(g * width, (g + 1) * width)
@@ -164,7 +166,51 @@
         ssm = inside_ref[:, cols] + far * spread_lanes([reach[:, h : h + 1] for h in hs], head_size)
         gated = ssm * silu(z_ref[:, cols].astype(f32))
         square = jnp.mean(gated * gated, axis=1, keepdims=True)
-        out_ref[g] = (gated * lax.rsqrt(square + EPS) * gain_ref[:, cols]).astype(bf16)
+        mix[((g // per_shard) ^ grp) * per_shard + g % per_shard] = (
+            gated * lax.rsqrt(square + EPS) * gain_ref[:, cols]
+        ).astype(bf16)
+    for j in range(G):
+        k, at = j // (2 * per_shard), j % (2 * per_shard)
+        outs[k][:, at * width : (at + 1) * width] = mix[j]
+
+
+def dispatch_kernel(plane, devices, capacity, pieces, at_ref, own_ref, *rest):
+    pair_refs, outs, weigh_ref = rest[:pieces], rest[pieces:-1], rest[-1]
+    length, model = own_ref.shape[0], outs[0].shape[1]
+    rows = outs[0].shape[0]
+    lanes = len(outs) * rows
+    device = lax.broadcasted_iota(jnp.int32, (devices, lanes), 0)
+    lane = lax.broadcasted_iota(jnp.int32, (devices, lanes), 1)
+    wanted = jnp.zeros((devices, lanes), jnp.int32)
+    start = lax.broadcasted_iota(jnp.int32, (length, lanes), 1)
+    for k in range(len(outs)):
+        inside = (lane >= k * rows) & (lane < (k + 1) * rows)
+        wanted = jnp.where(inside, at_ref[1] + (at_ref[0] ^ (2 * k)), wanted)
+    place = start
+    for k in range(1, len(outs)):
+        place = jnp.where(start >= k * rows, start - k * rows, place)
+    place = place.astype(f32)
+    select = (device == wanted).astype(f32).astype(bf16)
+    total = None
+    first = 0
+    for ref in (own_ref,) + pair_refs:
+        b, count = (0 if first < length else 1), ref.shape[0]
+        slot = dot(ref[:, model : model + devices], select, ((1,), (0,)))
+        gate = dot(ref[:, model + devices : model + 2 * devices], select, ((1,), (0,))) + dot(
+            ref[:, model + 2 * devices : model + 3 * devices], select, ((1,), (0,))
+        )
+        hit = (slot >= 0.0) & (slot + float(b * capacity) == place[:count])
+        weigh_ref[first : first + count, :] = jnp.where(hit, gate, 0.0).astype(bf16)
+        take = jnp.where(hit, 1.0, 0.0).astype(bf16)
+        part = dot(take, ref[:, :model], ((0,), (0,)))
+        total = part if total is None else total + part
+        first += count
+    for k in range(len(outs)):
+        outs[k][...] = total[k * rows : (k + 1) * rows].astype(bf16)
+
+
+def after(x, *others):
+    return lax.optimization_barrier((x,) + others)[0]
 
 
 def call(kernel, out_shape, scratch=(), flops=0, moved=0):
@@ -228,17 +274,11 @@
 
     previous = onward(conv_input[length - halo :], 1)
 
-    per_shard = out_weight.shape[0] // width
-    half = out_weight.shape[0] // 2
-    side = lax.div(r, n_grp)
-    mine_half = lax.dynamic_slice_in_dim(out_weight, side * half, half, 0)
     grp = lax.axis_index("grp")
-    cuts = [mine_half[: half // 2], mine_half[half // 2 :]]
-    by_x = [swap(c, 2) for c in cuts]
-    by_y = [swap(c, n_grp) for c in by_x]
-    own_pair = swap(out_weight, 1)
-    by_x_pair = [swap(c, 1) for c in by_x]
-    by_y_pair = [swap(c, 1) for c in by_y]
+    rows_own = out_weight
+    rows_pair = swap(out_weight, 1)
+    shard = out_weight.shape[0]
+    groups_shard = shard // width
 
     shapes = jax.ShapeDtypeStruct
     chunk = shapes((N + DEC, width), bf16)
@@ -284,31 +324,27 @@
         cost_estimate=pl.CostEstimate(flops=1000000, bytes_accessed=2000000, transcendentals=0),
     )(rs, *chunks, *earlier)
     incoming = [entering[0]] + [swap(entering[m], m) for m in range(1, plane)]
-    mixed = pl.pallas_call(
-        functools.partial(norm_kernel, plane),
-        out_shape=shapes((G, length, width), bf16),
+    split = pl.pallas_call(
+        functools.partial(norm_kernel, plane, n_grp),
+        out_shape=[shapes((length, 2 * shard), bf16)] * (n_grp // 2),
         in_specs=[smem] + [vm] * (5 + plane),
-        scratch_shapes=[pltpu.VMEM((G, N, width), bf16)],
+        scratch_shapes=[
+            pltpu.VMEM((G, N, width), bf16),
+            pltpu.VMEM((n_grp * groups_shard, length, width), bf16),
+        ],
         compiler_params=pltpu.CompilerParams(vmem_limit_bytes=VMEM_LIMIT),
         cost_estimate=pl.CostEstimate(flops=40000000, bytes_accessed=6000000, transcendentals=0),
-    )(rs, active, cumt, inside, z_stream, norm_gain[None, :], *incoming)
-
-    flat = mixed.transpose(1, 0, 2).reshape(length, inner)
-    shard = out_weight.shape[0]
-
-    def project(rows, start):
-        part = lax.dynamic_slice_in_dim(flat, start, rows.shape[0], 1)
-        return jnp.dot(part, rows, preferred_element_type=f32)
-
-    other = 1 - side
-    quarter = half // 2
-    total = hidden.astype(f32)
-    total = total + project(out_weight, grp * shard) + project(own_pair, (grp ^ 1) * shard)
-    for k in range(2):
-        total = total + project(by_x[k], (grp ^ 2) * shard + side * half + k * quarter)
-        total = total + project(by_x_pair[k], (grp ^ 3) * shard + side * half + k * quarter)
-        total = total + project(by_y[k], (grp ^ 2) * shard + other * half + k * quarter)
-        total = total + project(by_y_pair[k], (grp ^ 3) * shard + other * half + k * quarter)
+    )(jnp.stack([r, grp]).astype(jnp.int32), active, cumt, inside, z_stream, norm_gain[None, :], *incoming)
+
+    def project(part):
+        return jnp.dot(part[:, :shard], rows_own, preferred_element_type=f32) + jnp.dot(
+            part[:, shard:], rows_pair, preferred_element_type=f32
+        )
+
+    fars = [swap(split[k], 2 * k) for k in range(1, n_grp // 2)]
+    total = hidden.astype(f32) + project(split[0])
+    for k in range(1, n_grp // 2):
+        total = total + swap(project(fars[k - 1]).astype(bf16), 2 * k).astype(f32)
     residual_one = total.astype(bf16)
     moe_in = token_norm(residual_one, moe_gain)
 
@@ -334,37 +370,29 @@
     up_local = up_weight[0]
     down_local = down_weight[0]
     hops = list(range(0, plane, 2))
-    two = 2 * capacity
-
-    def serve(block):
-        both = jnp.concatenate([block, swap(block, 1)], axis=0)
-        here = both[:, model:]
-        ours = lax.dynamic_slice(
-            jnp.stack([here[:, :devices], here[:, devices : 2 * devices], here[:, 2 * devices : 3 * devices]]),
-            (0, 0, place * plane),
-            (3, 2 * length, plane),
-        ).astype(f32)
-        column = [lax.dynamic_slice_in_dim(ours, r ^ m, 1, 2) for m in hops]
-        column = jnp.concatenate(column, axis=2)
-        slot = jnp.where(column[0] < 0, -1.0, column[0])
-        late = (lax.broadcasted_iota(jnp.int32, slot.shape, 0) >= length) & (slot >= 0)
-        slot = slot + jnp.where(late, float(capacity), 0.0)
-        gate = column[1] + column[2]
-        wanted = slot[:, :, None] == jnp.arange(two, dtype=f32)[None, None, :]
-        take = wanted.astype(bf16).reshape(2 * length, len(hops) * two)
-        weigh = (
-            jnp.where(wanted, gate[:, :, None], 0.0).astype(bf16).reshape(2 * length, len(hops) * two)
-        )
-        sent = dot(take, both[:, :model], ((0,), (0,))).astype(bf16)
-        sent = [sent[k * two : (k + 1) * two] for k in range(len(hops))]
-        arrived = [sent[0]] + [swap(sent[k], hops[k]) for k in range(1, len(hops))]
-        return weigh, arrived
+    two = -(-2 * capacity // 8) * 8
+
+    at = jnp.stack([r, place * plane]).astype(jnp.int32)
+
+    def serve(block, pair):
+        out = pl.pallas_call(
+            functools.partial(dispatch_kernel, plane, devices, capacity, len(pair)),
+            out_shape=[shapes((two, model), bf16)] * len(hops)
+            + [shapes((2 * length, len(hops) * two), bf16)],
+            in_specs=[smem, vm] + [vm] * len(pair),
+            compiler_params=pltpu.CompilerParams(vmem_limit_bytes=VMEM_LIMIT),
+            cost_estimate=pl.CostEstimate(flops=0, bytes_accessed=0, transcendentals=0),
+        )(at, block, *pair)
+        sent = out[:-1]
+        return out[-1], [sent[0]] + [swap(sent[k], hops[k]) for k in range(1, len(hops))], sent
 
     def work(arrived):
         rows = jnp.concatenate(arrived, axis=0)
         up = jnp.dot(rows, up_local, preferred_element_type=f32)
         squared = jnp.square(jax.nn.relu(up)).astype(bf16)
-        result = jnp.dot(squared, down_local, preferred_element_type=f32).astype(bf16)
+        return jnp.dot(squared, down_local, preferred_element_type=f32).astype(bf16)
+
+    def send_back(result):
         parts = [result[k * two : (k + 1) * two] for k in range(len(hops))]
         return [parts[0]] + [swap(parts[k], hops[k]) for k in range(1, len(hops))]
 
@@ -373,14 +401,29 @@
         return part[:length] + swap(part[length:].astype(bf16), 1).astype(f32)
 
     block = jnp.concatenate([moe_in, meta], axis=1)
-    blocks = [block]
-    for _ in range(outer - 1):
-        blocks.append(turn(blocks[-1]))
-    served = [serve(b) for b in blocks]
-    returned = [work(s[1]) for s in served]
+    weighs, results, returned = {}, {}, {}
+    arrived = {}
+    for step in range(outer):
+        pair = [swap(block[: length // 2], 1), swap(block[length // 2 :], 1)]
+        if step >= 2:
+            pair[0] = after(pair[0], results[step - 2])
+        weighs[step], arrived[step], sent = serve(block, pair)
+        if step + 1 < outer:
+            block = turn(after(block, weighs[step]))
+        if step >= 1:
+            results[step - 1] = work(arrived[step - 1])
+            if step >= 2:
+                returned[step - 1] = send_back(results[step - 1])
+    results[outer - 1] = work(arrived[outer - 1])
+    if outer > 1:
+        returned[outer - 1] = send_back(results[outer - 1])
+    returned[0] = send_back(after(results[0], results[outer - 1]))
     carried = None
     for step in list(range(1, outer)) + [0]:
-        part = gather_up(served[step][0], returned[step])
+        back = returned[step]
+        if carried is not None and step == 0:
+            back = [after(back[0], carried)] + back[1:]
+        part = gather_up(weighs[step], back)
         if carried is not None:
             part = part + carried.astype(f32)
         if step:

time: 349 us -> 265 us (0.76)
  waiting for transfers between devices: 207 us -> 151 us
  local copies, waits for them, and re-layouts: 33 us -> 4.74 us
  Pallas kernels: 5.51 us -> 15.6 us
  other arithmetic: 7.16 us -> 2.47 us
    ppermute x6, waiting for transfers between devices: 69.3 us -> 33 us  [turn(): lax.ppermute(x, AXES, [(d, (d + plane) % devices) for d in range(devices)])]
    ppermute x55 -> x53, waiting for transfers between devices: 136 us -> 115 us  [swap(): return lax.ppermute(x, AXES, [(d, d ^ m) for d in range(devices)])]
    another operation x15 -> x0, local copies, waits for them, and re-layouts: 17.5 us -> none  [serve(): jnp.stack([here[:, :devices], here[:, devices:2 * devices], here[:, 2 * d...]
    pallas_call x1 -> x5, Pallas kernels: 1.67 us -> 11.7 us  [the longest x4 9.4 us: serve(): pl.pallas_call(functools.partial(dispatch_kernel, plane, devices, capacit...]
    unnamed x54 -> x42, local copies, waits for them, and re-layouts: 7.49 us -> 2.75 us
    dot_general x18 -> x8, matrix products: 20 us -> 15.8 us  [the longest x4 7.62 us: work(): return jnp.dot(squared, down_local, preferred_element_type=f32).astype(bf16)]
    ppermute x55 -> x53, starting transfers between devices: 49.8 us -> 47.8 us  [swap(): return lax.ppermute(x, AXES, [(d, d ^ m) for d in range(devices)])]
  transfers between devices with their start and end apart: 65 -> 63, of which waited for: 28 -> 34; matrix products, arithmetic and copies ran while one was open for 16% -> 10% of each run, Pallas kernels for 2% -> 5%
where the time goes in v2:
time: 265 us; the launch traced here: 264 us
  waiting for transfers between devices  151 us (57%)
  starting transfers between devices  59.9 us (23%)
  matrix products  29.7 us (11%)
  Pallas kernels  15.6 us (6%)
  local copies, waits for them, and re-layouts  4.74 us (2%)
    ppermute x53, waiting for transfers between devices, swap(): return lax.ppermute(x, AXES, [(d, d ^ m) for d in range(devices)])  115 us
    ppermute x53, starting transfers between devices, swap(): return lax.ppermute(x, AXES, [(d, d ^ m) for d in range(devices)])  47.8 us
    ppermute x6, waiting for transfers between devices, turn(): lax.ppermute(x, AXES, [(d, (d + plane) % devices) for d in range(devices)])  33 us
    ppermute x4, starting transfers between devices, onward(): lax.ppermute(x, AXES, [(d, d + by) for d in range(devices) if d + by < de...  11.4 us
    dot_general x4, matrix products, work(): up = jnp.dot(rows, up_local, preferred_element_type=f32)  10.3 us
    pallas_call x4, Pallas kernels, serve(): pl.pallas_call(functools.partial(dispatch_kernel, plane, devices, capacit...  9.4 us
    dot_general x4, matrix products, work(): return jnp.dot(squared, down_local, preferred_element_type=f32).astype(bf16)  7.62 us
  transfers between devices with their start and end apart: 63, of which 34 were waited for; matrix products, arithmetic and copies ran while one was open for 10% of the time, Pallas kernels for 5%

profile of v2, /device:TPU:0, one launch (start us, length us, event | category | flops | bytes accessed | tf_op | source)
XLA Modules:
  0.0 264.4 jit_solution(698514664140442781)
XLA Ops:
  1.4 2.0 collective-permute-start
  3.3 2.0 collective-permute-done.prev_ref
  8.0 2.0 shard_map.127
  10.0 2.3 collective-permute-start.1
  12.2 2.4 collective-permute-start.2
  14.7 2.7 %collective-permute-start.4 = (bf16[80,256]{1,0:T(8,128)(2,1)S(1)}, bf16[80,256]{1,0:T(8,128)(2,1)S(1)}, u32[]{:S(2)}, u32[]{:S(2)}) collective-permute-start(bf16[80,256]{1,0:T(8,128)(2,1)S(1)} %get-tuple-element.60), channel_id=1, source_target_pairs={{0,4},{1,5},{2,6},{3,7},{4,0},{5,1},{6,2},{7,3},{8,12},{9,13},{10,... | collective-permute-start | bytes 122888 | tf_op jit(solution)/shard_map/ppermute | solution.py:257
  17.3 2.2 collective-permute-start.6
  22.3 1.9 collective-permute-done.7.rest_7_
  24.3 5.7 %collective-permute-start.10 = (bf16[80,256]{1,0:T(8,128)(2,1)S(1)}, bf16[80,256]{1,0:T(8,128)(2,1)S(1)}, u32[]{:S(2)}, u32[]{:S(2)}) collective-permute-start(bf16[80,256]{1,0:T(8,128)(2,1)S(1)} %shard_map.129), channel_id=1, source_target_pairs={{0,24},{1,25},{2,26},{3,27},{4,28},{5,29},{6,30},{7,31}} | collective-permute-start | bytes 122888 | tf_op jit(solution)/shard_map/ppermute | solution.py:260
  31.3 2.5 collective-permute-start.9
  39.6 2.4 collective-permute-start.16
  44.4 2.1 collective-permute-done.17.rest_7_
  46.5 2.3 shard_map.131
  49.3 7.8 %collective-permute-done.19 = bf16[128,1024]{1,0:T(8,128)(2,1)S(1)} collective-permute-done((bf16[128,1024]{1,0:T(8,128)(2,1)S(1)}, bf16[128,1024]{1,0:T(8,128)(2,1)S(1)}, u32[]{:S(2)}, u32[]{:S(2)}) %collective-permute-start.19) | collective-permute-done | bytes 262176 | tf_op jit(solution)/shard_map/ppermute | solution.py:257
  57.1 2.3 fusion.164
  61.4 2.4 fusion.167
  63.8 13.9 %collective-permute-done.20 = bf16[128,2688]{1,0:T(8,128)(2,1)} collective-permute-done((bf16[128,2688]{1,0:T(8,128)(2,1)}, bf16[128,2688]{1,0:T(8,128)(2,1)}, u32[]{:S(2)}, u32[]{:S(2)}) %collective-permute-start.20) | collective-permute-done | bytes 688160 | tf_op jit(solution)/shard_map/ppermute | solution.py:257
  77.7 2.0 multiply_reduce_fusion
  82.3 2.4 shard_map.132
  86.5 2.0 collective-permute-start.25
  88.4 16.4 %collective-permute-done.26.own_ref = bf16[128,2816]{1,0:T(8,128)(2,1)S(1)} collective-permute-done((bf16[128,2816]{1,0:T(8,128)(2,1)S(1)}, bf16[128,2816]{1,0:T(8,128)(2,1)S(1)}, u32[]{:S(2)}, u32[]{:S(2)}) %collective-permute-start.26) | collective-permute-done | bytes 720928 | tf_op jit(solution)/shard_map/ppermute | solution.py:265
  107.1 2.3 shard_map.133
  111.1 2.0 collective-permute-start.36
  113.1 1.9 fusion.156
  115.0 6.3 %collective-permute-done.34 = bf16[72,2688]{1,0:T(8,128)(2,1)S(1)} collective-permute-done((bf16[72,2688]{1,0:T(8,128)(2,1)S(1)}, bf16[72,2688]{1,0:T(8,128)(2,1)S(1)}, u32[]{:S(2)}, u32[]{:S(2)}) %collective-permute-start.34) | collective-permute-done | bytes 387104 | tf_op jit(solution)/shard_map/ppermute | solution.py:257
  121.4 7.6 %collective-permute-done.35 = bf16[72,2688]{1,0:T(8,128)(2,1)S(1)} collective-permute-done((bf16[72,2688]{1,0:T(8,128)(2,1)S(1)}, bf16[72,2688]{1,0:T(8,128)(2,1)S(1)}, u32[]{:S(2)}, u32[]{:S(2)}) %collective-permute-start.35) | collective-permute-done | bytes 387104 | tf_op jit(solution)/shard_map/ppermute | solution.py:257
  129.0 1.9 fusion.151
  131.0 1.9 fusion.19
  133.0 1.7 collective-permute-start.52
  137.2 1.9 fusion.16
  139.1 2.4 shard_map.134
  141.5 1.7 collective-permute-start.45
  146.6 7.4 %collective-permute-done.54 = bf16[72,2688]{1,0:T(8,128)(2,1)S(1)} collective-permute-done((bf16[72,2688]{1,0:T(8,128)(2,1)S(1)}, bf16[72,2688]{1,0:T(8,128)(2,1)S(1)}, u32[]{:S(2)}, u32[]{:S(2)}) %collective-permute-start.54) | collective-permute-done | bytes 387104 | tf_op jit(solution)/shard_map/ppermute | solution.py:257
  155.4 6.2 %collective-permute-done.45 = bf16[72,2688]{1,0:T(8,128)(2,1)S(1)} collective-permute-done((bf16[72,2688]{1,0:T(8,128)(2,1)S(1)}, bf16[72,2688]{1,0:T(8,128)(2,1)S(1)}, u32[]{:S(2)}, u32[]{:S(2)}) %collective-permute-start.45) | collective-permute-done | bytes 387104 | tf_op jit(solution)/shard_map/ppermute | solution.py:257
  162.1 6.9 %collective-permute-done.47 = bf16[72,2688]{1,0:T(8,128)(2,1)S(1)} collective-permute-done((bf16[72,2688]{1,0:T(8,128)(2,1)S(1)}, bf16[72,2688]{1,0:T(8,128)(2,1)S(1)}, u32[]{:S(2)}, u32[]{:S(2)}) %collective-permute-start.47) | collective-permute-done | bytes 387104 | tf_op jit(solution)/shard_map/ppermute | solution.py:257
  169.0 4.6 %fusion.141 = bf16[288,1024]{1,0:T(8,128)(2,1)S(1)} fusion(bf16[1,2688,1024]{2,1,0:T(8,128)(2,1)} %param.24, bf16[72,2688]{1,0:T(8,128)(2,1)S(1)} %collective-permute-done.47, bf16[72,2688]{1,0:T(8,128)(2,1)S(1)} %collective-permute-done.46, bf16[72,2688]{1,0:T(8,128)(2,1)S(1)} %collective-permute-done.45, bf16[72,2688]{1,0:T(8,128)(2,1)S(1)} %get-tuple-element.96), kind=kOutput, calls=%fused_computation.113 | convolution fusion | flops 1592524800 | bytes 7643136 | tf_op jit(solution)/shard_map/dot_general | solution.py:391
  173.6 1.9 fusion.25
  179.8 2.3 shard_map.135
  184.5 3.1 %collective-permute-done.48 = bf16[72,2688]{1,0:T(8,128)(2,1)S(1)} collective-permute-done((bf16[72,2688]{1,0:T(8,128)(2,1)S(1)}, bf16[72,2688]{1,0:T(8,128)(2,1)S(1)}, u32[]{:S(2)}, u32[]{:S(2)}) %collective-permute-start.48) | collective-permute-done | bytes 387104 | tf_op jit(solution)/shard_map/ppermute | solution.py:257
  187.8 9.6 %collective-permute-done.49 = bf16[72,2688]{1,0:T(8,128)(2,1)S(1)} collective-permute-done((bf16[72,2688]{1,0:T(8,128)(2,1)S(1)}, bf16[72,2688]{1,0:T(8,128)(2,1)S(1)}, u32[]{:S(2)}, u32[]{:S(2)}) %collective-permute-start.49) | collective-permute-done | bytes 387104 | tf_op jit(solution)/shard_map/ppermute | solution.py:257
  198.4 5.8 %collective-permute-done.38 = bf16[72,2688]{1,0:T(8,128)(2,1)S(1)} collective-permute-done((bf16[72,2688]{1,0:T(8,128)(2,1)S(1)}, bf16[72,2688]{1,0:T(8,128)(2,1)S(1)}, u32[]{:S(2)}, u32[]{:S(2)}) %collective-permute-start.38) | collective-permute-done | bytes 387104 | tf_op jit(solution)/shard_map/ppermute | solution.py:257
  204.3 8.8 %collective-permute-done.39 = bf16[72,2688]{1,0:T(8,128)(2,1)S(1)} collective-permute-done((bf16[72,2688]{1,0:T(8,128)(2,1)S(1)}, bf16[72,2688]{1,0:T(8,128)(2,1)S(1)}, u32[]{:S(2)}, u32[]{:S(2)}) %collective-permute-start.39) | collective-permute-done | bytes 387104 | tf_op jit(solution)/shard_map/ppermute | solution.py:257
  213.1 1.9 fusion.146
  215.0 1.9 fusion.22
  220.9 8.1 %collective-permute-done.41 = bf16[72,2688]{1,0:T(8,128)(2,1)S(1)} collective-permute-done((bf16[72,2688]{1,0:T(8,128)(2,1)S(1)}, bf16[72,2688]{1,0:T(8,128)(2,1)S(1)}, u32[]{:S(2)}, u32[]{:S(2)}) %collective-permute-start.41) | collective-permute-done | bytes 387104 | tf_op jit(solution)/shard_map/ppermute | solution.py:257
  229.9 6.5 %collective-permute-done.43 = bf16[72,2688]{1,0:T(8,128)(2,1)S(1)} collective-permute-done((bf16[72,2688]{1,0:T(8,128)(2,1)S(1)}, bf16[72,2688]{1,0:T(8,128)(2,1)S(1)}, u32[]{:S(2)}, u32[]{:S(2)}) %collective-permute-start.43) | collective-permute-done | bytes 387104 | tf_op jit(solution)/shard_map/ppermute | solution.py:257
  243.6 15.6 %collective-permute-done.58 = bf16[128,2688]{1,0:T(8,128)(2,1)S(1)} collective-permute-done((bf16[128,2688]{1,0:T(8,128)(2,1)S(1)}, bf16[128,2688]{1,0:T(8,128)(2,1)S(1)}, u32[]{:S(2)}, u32[]{:S(2)}) %collective-permute-start.58) | collective-permute-done | bytes 688160 | tf_op jit(solution)/shard_map/ppermute | solution.py:265
  261.1 2.1 collective-permute-done.62
  (180 shorter events, 57.9 us)
Async XLA Ops:
  0.0 57.1 %collective-permute-start.18 = (bf16[512,2688]{1,0:T(8,128)(2,1)}, bf16[512,2688]{1,0:T(8,128)(2,1)}, u32[]{:S(2)}, u32[]{:S(2)}) collective-permute-start(bf16[512,2688]{1,0:T(8,128)(2,1)} %param.19), channel_id=1, source_target_pairs={{0,1},{1,0},{2,3},{3,2},{4,5},{5,4},{6,7},{7,6},{8,9},{9,8},{10,11... | collective-permute-start | bytes 8257544 | tf_op jit(solution)/shard_map/ppermute | solution.py:257
  10.0 7.4 %collective-permute-start.1 = (bf16[80,256]{1,0:T(8,128)(2,1)S(1)}, bf16[80,256]{1,0:T(8,128)(2,1)S(1)}, u32[]{:S(2)}, u32[]{:S(2)}) collective-permute-start(bf16[80,256]{1,0:T(8,128)(2,1)S(1)} %get-tuple-element.57), channel_id=1, source_target_pairs={{0,1},{1,0},{2,3},{3,2},{4,5},{5,4},{6,7},{7,6},{8,9},{9,8},{10,11... | collective-permute-start | bytes 122888 | tf_op jit(solution)/shard_map/ppermute | solution.py:257
  12.2 5.1 %collective-permute-start.2 = (bf16[80,256]{1,0:T(8,128)(2,1)S(1)}, bf16[80,256]{1,0:T(8,128)(2,1)S(1)}, u32[]{:S(2)}, u32[]{:S(2)}) collective-permute-start(bf16[80,256]{1,0:T(8,128)(2,1)S(1)} %get-tuple-element.58), channel_id=1, source_target_pairs={{0,2},{1,3},{2,0},{3,1},{4,6},{5,7},{6,4},{7,5},{8,10},{9,11},{10,... | collective-permute-start | bytes 122888 | tf_op jit(solution)/shard_map/ppermute | solution.py:257
  14.6 5.0 %collective-permute-start.3 = (bf16[80,256]{1,0:T(8,128)(2,1)S(1)}, bf16[80,256]{1,0:T(8,128)(2,1)S(1)}, u32[]{:S(2)}, u32[]{:S(2)}) collective-permute-start(bf16[80,256]{1,0:T(8,128)(2,1)S(1)} %get-tuple-element.59), channel_id=1, source_target_pairs={{0,3},{1,2},{2,1},{3,0},{4,7},{5,6},{6,5},{7,4},{8,11},{9,10},{10,... | collective-permute-start | bytes 122888 | tf_op jit(solution)/shard_map/ppermute | solution.py:257
  14.7 5.9 %collective-permute-start.4 = (bf16[80,256]{1,0:T(8,128)(2,1)S(1)}, bf16[80,256]{1,0:T(8,128)(2,1)S(1)}, u32[]{:S(2)}, u32[]{:S(2)}) collective-permute-start(bf16[80,256]{1,0:T(8,128)(2,1)S(1)} %get-tuple-element.60), channel_id=1, source_target_pairs={{0,4},{1,5},{2,6},{3,7},{4,0},{5,1},{6,2},{7,3},{8,12},{9,13},{10,... | collective-permute-start | bytes 122888 | tf_op jit(solution)/shard_map/ppermute | solution.py:257
  17.3 5.0 %collective-permute-start.6 = (bf16[80,256]{1,0:T(8,128)(2,1)S(1)}, bf16[80,256]{1,0:T(8,128)(2,1)S(1)}, u32[]{:S(2)}, u32[]{:S(2)}) collective-permute-start(bf16[80,256]{1,0:T(8,128)(2,1)S(1)} %get-tuple-element.62), channel_id=1, source_target_pairs={{0,6},{1,7},{2,4},{3,5},{4,2},{5,3},{6,0},{7,1},{8,14},{9,15},{10,... | collective-permute-start | bytes 122888 | tf_op jit(solution)/shard_map/ppermute | solution.py:257
  19.6 4.6 %collective-permute-start.7 = (bf16[80,256]{1,0:T(8,128)(2,1)S(1)}, bf16[80,256]{1,0:T(8,128)(2,1)S(1)}, u32[]{:S(2)}, u32[]{:S(2)}) collective-permute-start(bf16[80,256]{1,0:T(8,128)(2,1)S(1)} %get-tuple-element.63), channel_id=1, source_target_pairs={{0,7},{1,6},{2,5},{3,4},{4,3},{5,2},{6,1},{7,0},{8,15},{9,14},{10,... | collective-permute-start | bytes 122888 | tf_op jit(solution)/shard_map/ppermute | solution.py:257
  24.3 9.5 %collective-permute-start.10 = (bf16[80,256]{1,0:T(8,128)(2,1)S(1)}, bf16[80,256]{1,0:T(8,128)(2,1)S(1)}, u32[]{:S(2)}, u32[]{:S(2)}) collective-permute-start(bf16[80,256]{1,0:T(8,128)(2,1)S(1)} %shard_map.129), channel_id=1, source_target_pairs={{0,24},{1,25},{2,26},{3,27},{4,28},{5,29},{6,30},{7,31}} | collective-permute-start | bytes 122888 | tf_op jit(solution)/shard_map/ppermute | solution.py:260
  31.3 4.1 %collective-permute-start.9 = (bf16[80,256]{1,0:T(8,128)(2,1)S(1)}, bf16[80,256]{1,0:T(8,128)(2,1)S(1)}, u32[]{:S(2)}, u32[]{:S(2)}) collective-permute-start(bf16[80,256]{1,0:T(8,128)(2,1)S(1)} %shard_map.129), channel_id=1, source_target_pairs={{0,16},{1,17},{2,18},{3,19},{4,20},{5,21},{6,22},{7,23},{8,24},{9,... | collective-permute-start | bytes 122888 | tf_op jit(solution)/shard_map/ppermute | solution.py:260
  37.2 4.8 %collective-permute-start.13 = (bf16[64,256]{1,0:T(8,128)(2,1)S(1)}, bf16[64,256]{1,0:T(8,128)(2,1)S(1)}, u32[]{:S(2)}, u32[]{:S(2)}) collective-permute-start(bf16[64,256]{1,0:T(8,128)(2,1)S(1)} %get-tuple-element.67), channel_id=1, source_target_pairs={{0,3},{1,2},{2,1},{3,0},{4,7},{5,6},{6,5},{7,4},{8,11},{9,10},{10,... | collective-permute-start | bytes 98312 | tf_op jit(solution)/shard_map/ppermute | solution.py:257
  37.6 6.2 %collective-permute-start.14 = (bf16[64,256]{1,0:T(8,128)(2,1)S(1)}, bf16[64,256]{1,0:T(8,128)(2,1)S(1)}, u32[]{:S(2)}, u32[]{:S(2)}) collective-permute-start(bf16[64,256]{1,0:T(8,128)(2,1)S(1)} %get-tuple-element.68), channel_id=1, source_target_pairs={{0,4},{1,5},{2,6},{3,7},{4,0},{5,1},{6,2},{7,3},{8,12},{9,13},{10,... | collective-permute-start | bytes 98312 | tf_op jit(solution)/shard_map/ppermute | solution.py:257
  38.7 5.1 %collective-permute-start.15 = (bf16[64,256]{1,0:T(8,128)(2,1)S(1)}, bf16[64,256]{1,0:T(8,128)(2,1)S(1)}, u32[]{:S(2)}, u32[]{:S(2)}) collective-permute-start(bf16[64,256]{1,0:T(8,128)(2,1)S(1)} %get-tuple-element.69), channel_id=1, source_target_pairs={{0,5},{1,4},{2,7},{3,6},{4,1},{5,0},{6,3},{7,2},{8,13},{9,12},{10,... | collective-permute-start | bytes 98312 | tf_op jit(solution)/shard_map/ppermute | solution.py:257
  39.6 4.8 %collective-permute-start.16 = (bf16[64,256]{1,0:T(8,128)(2,1)S(1)}, bf16[64,256]{1,0:T(8,128)(2,1)S(1)}, u32[]{:S(2)}, u32[]{:S(2)}) collective-permute-start(bf16[64,256]{1,0:T(8,128)(2,1)S(1)} %get-tuple-element.70), channel_id=1, source_target_pairs={{0,6},{1,7},{2,4},{3,5},{4,2},{5,3},{6,0},{7,1},{8,14},{9,15},{10,... | collective-permute-start | bytes 98312 | tf_op jit(solution)/shard_map/ppermute | solution.py:257
  42.0 4.5 %collective-permute-start.17 = (bf16[64,256]{1,0:T(8,128)(2,1)S(1)}, bf16[64,256]{1,0:T(8,128)(2,1)S(1)}, u32[]{:S(2)}, u32[]{:S(2)}) collective-permute-start(bf16[64,256]{1,0:T(8,128)(2,1)S(1)} %get-tuple-element.71), channel_id=1, source_target_pairs={{0,7},{1,6},{2,5},{3,4},{4,3},{5,2},{6,1},{7,0},{8,15},{9,14},{10,... | collective-permute-start | bytes 98312 | tf_op jit(solution)/shard_map/ppermute | solution.py:257
  48.8 8.3 %collective-permute-start.19 = (bf16[128,1024]{1,0:T(8,128)(2,1)S(1)}, bf16[128,1024]{1,0:T(8,128)(2,1)S(1)}, u32[]{:S(2)}, u32[]{:S(2)}) collective-permute-start(bf16[128,1024]{1,0:T(8,128)(2,1)S(1)} %get-tuple-element.73), channel_id=1, source_target_pairs={{0,2},{1,3},{2,0},{3,1},{4,6},{5,7},{6,4},{7,5},{8,10},{9,11},{10,... | collective-permute-start | bytes 786440 | tf_op jit(solution)/shard_map/ppermute | solution.py:257
  60.9 16.8 %collective-permute-start.20 = (bf16[128,2688]{1,0:T(8,128)(2,1)}, bf16[128,2688]{1,0:T(8,128)(2,1)}, u32[]{:S(2)}, u32[]{:S(2)}) collective-permute-start(bf16[128,2688]{1,0:T(8,128)(2,1)} %fusion.32), channel_id=1, source_target_pairs={{0,2},{1,3},{2,0},{3,1},{4,6},{5,7},{6,4},{7,5},{8,10},{9,11},{10,... | collective-permute-start | bytes 2064392 | tf_op jit(solution)/shard_map/ppermute | solution.py:257
  84.6 20.2 %collective-permute-start.26 = (bf16[128,2816]{1,0:T(8,128)(2,1)S(1)}, bf16[128,2816]{1,0:T(8,128)(2,1)S(1)}, u32[]{:S(2)}, u32[]{:S(2)}) collective-permute-start(bf16[128,2816]{1,0:T(8,128)(2,1)S(1)} %pad_maximum_fusion.own_ref), channel_id=1, source_target_pairs={{0,8},{1,9},{2,10},{3,11},{4,12},{5,13},{6,14},{7,15},{8,16},{9,17... | collective-permute-start | bytes 2162696 | tf_op jit(solution)/shard_map/ppermute | solution.py:265
  84.9 26.2 %collective-permute-start.23 = (bf16[72,2688]{1,0:T(8,128)(2,1)S(1)}, bf16[72,2688]{1,0:T(8,128)(2,1)S(1)}, u32[]{:S(2)}, u32[]{:S(2)}) collective-permute-start(bf16[72,2688]{1,0:T(8,128)(2,1)S(1)} %get-tuple-element.76), channel_id=1, source_target_pairs={{0,2},{1,3},{2,0},{3,1},{4,6},{5,7},{6,4},{7,5},{8,10},{9,11},{10,... | collective-permute-start | bytes 1161224 | tf_op jit(solution)/shard_map/ppermute | solution.py:257
  85.4 27.7 %collective-permute-start.24 = (bf16[72,2688]{1,0:T(8,128)(2,1)S(1)}, bf16[72,2688]{1,0:T(8,128)(2,1)S(1)}, u32[]{:S(2)}, u32[]{:S(2)}) collective-permute-start(bf16[72,2688]{1,0:T(8,128)(2,1)S(1)} %get-tuple-element.77), channel_id=1, source_target_pairs={{0,4},{1,5},{2,6},{3,7},{4,0},{5,1},{6,2},{7,3},{8,12},{9,13},{10,... | collective-permute-start | bytes 1161224 | tf_op jit(solution)/shard_map/ppermute | solution.py:257
  86.5 26.6 %collective-permute-start.25 = (bf16[72,2688]{1,0:T(8,128)(2,1)S(1)}, bf16[72,2688]{1,0:T(8,128)(2,1)S(1)}, u32[]{:S(2)}, u32[]{:S(2)}) collective-permute-start(bf16[72,2688]{1,0:T(8,128)(2,1)S(1)} %get-tuple-element.78), channel_id=1, source_target_pairs={{0,6},{1,7},{2,4},{3,5},{4,2},{5,3},{6,0},{7,1},{8,14},{9,15},{10,... | collective-permute-start | bytes 1161224 | tf_op jit(solution)/shard_map/ppermute | solution.py:257
  109.5 11.9 %collective-permute-start.34 = (bf16[72,2688]{1,0:T(8,128)(2,1)S(1)}, bf16[72,2688]{1,0:T(8,128)(2,1)S(1)}, u32[]{:S(2)}, u32[]{:S(2)}) collective-permute-start(bf16[72,2688]{1,0:T(8,128)(2,1)S(1)} %get-tuple-element.86), channel_id=1, source_target_pairs={{0,2},{1,3},{2,0},{3,1},{4,6},{5,7},{6,4},{7,5},{8,10},{9,11},{10,... | collective-permute-start | bytes 1161224 | tf_op jit(solution)/shard_map/ppermute | solution.py:257
  110.0 19.0 %collective-permute-start.35 = (bf16[72,2688]{1,0:T(8,128)(2,1)S(1)}, bf16[72,2688]{1,0:T(8,128)(2,1)S(1)}, u32[]{:S(2)}, u32[]{:S(2)}) collective-permute-start(bf16[72,2688]{1,0:T(8,128)(2,1)S(1)} %get-tuple-element.87), channel_id=1, source_target_pairs={{0,4},{1,5},{2,6},{3,7},{4,0},{5,1},{6,2},{7,3},{8,12},{9,13},{10,... | collective-permute-start | bytes 1161224 | tf_op jit(solution)/shard_map/ppermute | solution.py:257
  111.1 18.0 %collective-permute-start.36 = (bf16[72,2688]{1,0:T(8,128)(2,1)S(1)}, bf16[72,2688]{1,0:T(8,128)(2,1)S(1)}, u32[]{:S(2)}, u32[]{:S(2)}) collective-permute-start(bf16[72,2688]{1,0:T(8,128)(2,1)S(1)} %get-tuple-element.88), channel_id=1, source_target_pairs={{0,6},{1,7},{2,4},{3,5},{4,2},{5,3},{6,0},{7,1},{8,14},{9,15},{10,... | collective-permute-start | bytes 1161224 | tf_op jit(solution)/shard_map/ppermute | solution.py:257
  115.0 21.6 %collective-permute-start.29 = (bf16[128,2816]{1,0:T(8,128)(2,1)S(1)}, bf16[128,2816]{1,0:T(8,128)(2,1)S(1)}, u32[]{:S(2)}, u32[]{:S(2)}) collective-permute-start(bf16[128,2816]{1,0:T(8,128)(2,1)S(1)} %collective-permute-done.26.own_ref), channel_id=1, source_target_pairs={{0,8},{1,9},{2,10},{3,11},{4,12},{5,13},{6,14},{7,15},{8,16},{9,17... | collective-permute-start | bytes 2162696 | tf_op jit(solution)/shard_map/ppermute | solution.py:265
  133.0 12.0 %collective-permute-start.52 = (bf16[72,2688]{1,0:T(8,128)(2,1)S(1)}, bf16[72,2688]{1,0:T(8,128)(2,1)S(1)}, u32[]{:S(2)}, u32[]{:S(2)}) collective-permute-start(bf16[72,2688]{1,0:T(8,128)(2,1)S(1)} %get-tuple-element.104), channel_id=1, source_target_pairs={{0,2},{1,3},{2,0},{3,1},{4,6},{5,7},{6,4},{7,5},{8,10},{9,11},{10,... | collective-permute-start | bytes 1161224 | tf_op jit(solution)/shard_map/ppermute | solution.py:257
  134.7 12.0 %collective-permute-start.53 = (bf16[72,2688]{1,0:T(8,128)(2,1)S(1)}, bf16[72,2688]{1,0:T(8,128)(2,1)S(1)}, u32[]{:S(2)}, u32[]{:S(2)}) collective-permute-start(bf16[72,2688]{1,0:T(8,128)(2,1)S(1)} %get-tuple-element.103), channel_id=1, source_target_pairs={{0,4},{1,5},{2,6},{3,7},{4,0},{5,1},{6,2},{7,3},{8,12},{9,13},{10,... | collective-permute-start | bytes 1161224 | tf_op jit(solution)/shard_map/ppermute | solution.py:257
  135.3 18.8 %collective-permute-start.54 = (bf16[72,2688]{1,0:T(8,128)(2,1)S(1)}, bf16[72,2688]{1,0:T(8,128)(2,1)S(1)}, u32[]{:S(2)}, u32[]{:S(2)}) collective-permute-start(bf16[72,2688]{1,0:T(8,128)(2,1)S(1)} %get-tuple-element.102), channel_id=1, source_target_pairs={{0,6},{1,7},{2,4},{3,5},{4,2},{5,3},{6,0},{7,1},{8,14},{9,15},{10,... | collective-permute-start | bytes 1161224 | tf_op jit(solution)/shard_map/ppermute | solution.py:257
  141.5 20.2 %collective-permute-start.45 = (bf16[72,2688]{1,0:T(8,128)(2,1)S(1)}, bf16[72,2688]{1,0:T(8,128)(2,1)S(1)}, u32[]{:S(2)}, u32[]{:S(2)}) collective-permute-start(bf16[72,2688]{1,0:T(8,128)(2,1)S(1)} %get-tuple-element.97), channel_id=1, source_target_pairs={{0,2},{1,3},{2,0},{3,1},{4,6},{5,7},{6,4},{7,5},{8,10},{9,11},{10,... | collective-permute-start | bytes 1161224 | tf_op jit(solution)/shard_map/ppermute | solution.py:257
  143.2 18.9 %collective-permute-start.46 = (bf16[72,2688]{1,0:T(8,128)(2,1)S(1)}, bf16[72,2688]{1,0:T(8,128)(2,1)S(1)}, u32[]{:S(2)}, u32[]{:S(2)}) collective-permute-start(bf16[72,2688]{1,0:T(8,128)(2,1)S(1)} %get-tuple-element.98), channel_id=1, source_target_pairs={{0,4},{1,5},{2,6},{3,7},{4,0},{5,1},{6,2},{7,3},{8,12},{9,13},{10,... | collective-permute-start | bytes 1161224 | tf_op jit(solution)/shard_map/ppermute | solution.py:257
  145.0 24.0 %collective-permute-start.47 = (bf16[72,2688]{1,0:T(8,128)(2,1)S(1)}, bf16[72,2688]{1,0:T(8,128)(2,1)S(1)}, u32[]{:S(2)}, u32[]{:S(2)}) collective-permute-start(bf16[72,2688]{1,0:T(8,128)(2,1)S(1)} %get-tuple-element.99), channel_id=1, source_target_pairs={{0,6},{1,7},{2,4},{3,5},{4,2},{5,3},{6,0},{7,1},{8,14},{9,15},{10,... | collective-permute-start | bytes 1161224 | tf_op jit(solution)/shard_map/ppermute | solution.py:257
  155.1 28.6 %collective-permute-start.55 = (bf16[128,2688]{1,0:T(8,128)(2,1)S(1)}, bf16[128,2688]{1,0:T(8,128)(2,1)S(1)}, u32[]{:S(2)}, u32[]{:S(2)}) collective-permute-start(bf16[128,2688]{1,0:T(8,128)(2,1)S(1)} %slice.229), channel_id=1, source_target_pairs={{0,1},{1,0},{2,3},{3,2},{4,5},{5,4},{6,7},{7,6},{8,9},{9,8},{10,11... | collective-permute-start | bytes 2064392 | tf_op jit(solution)/shard_map/ppermute | solution.py:257
  155.2 21.4 %collective-permute-start.32 = (bf16[128,2816]{1,0:T(8,128)(2,1)S(1)}, bf16[128,2816]{1,0:T(8,128)(2,1)S(1)}, u32[]{:S(2)}, u32[]{:S(2)}) collective-permute-start(bf16[128,2816]{1,0:T(8,128)(2,1)S(1)} %collective-permute-done.29.own_ref), channel_id=1, source_target_pairs={{0,8},{1,9},{2,10},{3,11},{4,12},{5,13},{6,14},{7,15},{8,16},{9,17... | collective-permute-start | bytes 2162696 | tf_op jit(solution)/shard_map/ppermute | solution.py:265
  175.6 12.0 %collective-permute-start.48 = (bf16[72,2688]{1,0:T(8,128)(2,1)S(1)}, bf16[72,2688]{1,0:T(8,128)(2,1)S(1)}, u32[]{:S(2)}, u32[]{:S(2)}) collective-permute-start(bf16[72,2688]{1,0:T(8,128)(2,1)S(1)} %get-tuple-element.108), channel_id=1, source_target_pairs={{0,2},{1,3},{2,0},{3,1},{4,6},{5,7},{6,4},{7,5},{8,10},{9,11},{10,... | collective-permute-start | bytes 1161224 | tf_op jit(solution)/shard_map/ppermute | solution.py:257
  177.2 20.1 %collective-permute-start.49 = (bf16[72,2688]{1,0:T(8,128)(2,1)S(1)}, bf16[72,2688]{1,0:T(8,128)(2,1)S(1)}, u32[]{:S(2)}, u32[]{:S(2)}) collective-permute-start(bf16[72,2688]{1,0:T(8,128)(2,1)S(1)} %get-tuple-element.107), channel_id=1, source_target_pairs={{0,4},{1,5},{2,6},{3,7},{4,0},{5,1},{6,2},{7,3},{8,12},{9,13},{10,... | collective-permute-start | bytes 1161224 | tf_op jit(solution)/shard_map/ppermute | solution.py:257
  178.6 18.8 %collective-permute-start.50 = (bf16[72,2688]{1,0:T(8,128)(2,1)S(1)}, bf16[72,2688]{1,0:T(8,128)(2,1)S(1)}, u32[]{:S(2)}, u32[]{:S(2)}) collective-permute-start(bf16[72,2688]{1,0:T(8,128)(2,1)S(1)} %get-tuple-element.106), channel_id=1, source_target_pairs={{0,6},{1,7},{2,4},{3,5},{4,2},{5,3},{6,0},{7,1},{8,14},{9,15},{10,... | collective-permute-start | bytes 1161224 | tf_op jit(solution)/shard_map/ppermute | solution.py:257
  182.2 22.1 %collective-permute-start.38 = (bf16[72,2688]{1,0:T(8,128)(2,1)S(1)}, bf16[72,2688]{1,0:T(8,128)(2,1)S(1)}, u32[]{:S(2)}, u32[]{:S(2)}) collective-permute-start(bf16[72,2688]{1,0:T(8,128)(2,1)S(1)} %get-tuple-element.91), channel_id=1, source_target_pairs={{0,2},{1,3},{2,0},{3,1},{4,6},{5,7},{6,4},{7,5},{8,10},{9,11},{10,... | collective-permute-start | bytes 1161224 | tf_op jit(solution)/shard_map/ppermute | solution.py:257
  183.7 29.4 %collective-permute-start.39 = (bf16[72,2688]{1,0:T(8,128)(2,1)S(1)}, bf16[72,2688]{1,0:T(8,128)(2,1)S(1)}, u32[]{:S(2)}, u32[]{:S(2)}) collective-permute-start(bf16[72,2688]{1,0:T(8,128)(2,1)S(1)} %get-tuple-element.92), channel_id=1, source_target_pairs={{0,4},{1,5},{2,6},{3,7},{4,0},{5,1},{6,2},{7,3},{8,12},{9,13},{10,... | collective-permute-start | bytes 1161224 | tf_op jit(solution)/shard_map/ppermute | solution.py:257
  187.6 25.4 %collective-permute-start.40 = (bf16[72,2688]{1,0:T(8,128)(2,1)S(1)}, bf16[72,2688]{1,0:T(8,128)(2,1)S(1)}, u32[]{:S(2)}, u32[]{:S(2)}) collective-permute-start(bf16[72,2688]{1,0:T(8,128)(2,1)S(1)} %get-tuple-element.93), channel_id=1, source_target_pairs={{0,6},{1,7},{2,4},{3,5},{4,2},{5,3},{6,0},{7,1},{8,14},{9,15},{10,... | collective-permute-start | bytes 1161224 | tf_op jit(solution)/shard_map/ppermute | solution.py:257
  197.3 23.3 %collective-permute-start.56 = (bf16[128,2688]{1,0:T(8,128)(2,1)S(1)}, bf16[128,2688]{1,0:T(8,128)(2,1)S(1)}, u32[]{:S(2)}, u32[]{:S(2)}) collective-permute-start(bf16[128,2688]{1,0:T(8,128)(2,1)S(1)} %fusion.96), channel_id=1, source_target_pairs={{0,8},{1,9},{2,10},{3,11},{4,12},{5,13},{6,14},{7,15},{8,16},{9,17... | collective-permute-start | bytes 2064392 | tf_op jit(solution)/shard_map/ppermute | solution.py:265
  198.3 22.3 %collective-permute-start.51 = (bf16[128,2688]{1,0:T(8,128)(2,1)S(1)}, bf16[128,2688]{1,0:T(8,128)(2,1)S(1)}, u32[]{:S(2)}, u32[]{:S(2)}) collective-permute-start(bf16[128,2688]{1,0:T(8,128)(2,1)S(1)} %slice.230), channel_id=1, source_target_pairs={{0,1},{1,0},{2,3},{3,2},{4,5},{5,4},{6,7},{7,6},{8,9},{9,8},{10,11... | collective-permute-start | bytes 2064392 | tf_op jit(solution)/shard_map/ppermute | solution.py:257
  217.0 12.0 %collective-permute-start.41 = (bf16[72,2688]{1,0:T(8,128)(2,1)S(1)}, bf16[72,2688]{1,0:T(8,128)(2,1)S(1)}, u32[]{:S(2)}, u32[]{:S(2)}) collective-permute-start(bf16[72,2688]{1,0:T(8,128)(2,1)S(1)} %get-tuple-element.112), channel_id=1, source_target_pairs={{0,2},{1,3},{2,0},{3,1},{4,6},{5,7},{6,4},{7,5},{8,10},{9,11},{10,... | collective-permute-start | bytes 1161224 | tf_op jit(solution)/shard_map/ppermute | solution.py:257
  218.3 11.7 %collective-permute-start.42 = (bf16[72,2688]{1,0:T(8,128)(2,1)S(1)}, bf16[72,2688]{1,0:T(8,128)(2,1)S(1)}, u32[]{:S(2)}, u32[]{:S(2)}) collective-permute-start(bf16[72,2688]{1,0:T(8,128)(2,1)S(1)} %get-tuple-element.111), channel_id=1, source_target_pairs={{0,4},{1,5},{2,6},{3,7},{4,0},{5,1},{6,2},{7,3},{8,12},{9,13},{10,... | collective-permute-start | bytes 1161224 | tf_op jit(solution)/shard_map/ppermute | solution.py:257
  219.0 17.4 %collective-permute-start.43 = (bf16[72,2688]{1,0:T(8,128)(2,1)S(1)}, bf16[72,2688]{1,0:T(8,128)(2,1)S(1)}, u32[]{:S(2)}, u32[]{:S(2)}) collective-permute-start(bf16[72,2688]{1,0:T(8,128)(2,1)S(1)} %get-tuple-element.110), channel_id=1, source_target_pairs={{0,6},{1,7},{2,4},{3,5},{4,2},{5,3},{6,0},{7,1},{8,14},{9,15},{10,... | collective-permute-start | bytes 1161224 | tf_op jit(solution)/shard_map/ppermute | solution.py:257
  220.9 17.6 %collective-permute-start.57 = (bf16[128,2688]{1,0:T(8,128)(2,1)S(1)}, bf16[128,2688]{1,0:T(8,128)(2,1)S(1)}, u32[]{:S(2)}, u32[]{:S(2)}) collective-permute-start(bf16[128,2688]{1,0:T(8,128)(2,1)S(1)} %fusion.98), channel_id=1, source_target_pairs={{0,8},{1,9},{2,10},{3,11},{4,12},{5,13},{6,14},{7,15},{8,16},{9,17... | collective-permute-start | bytes 2064392 | tf_op jit(solution)/shard_map/ppermute | solution.py:265
  239.9 19.3 %collective-permute-start.58 = (bf16[128,2688]{1,0:T(8,128)(2,1)S(1)}, bf16[128,2688]{1,0:T(8,128)(2,1)S(1)}, u32[]{:S(2)}, u32[]{:S(2)}) collective-permute-start(bf16[128,2688]{1,0:T(8,128)(2,1)S(1)} %fusion.100), channel_id=1, source_target_pairs={{0,8},{1,9},{2,10},{3,11},{4,12},{5,13},{6,14},{7,15},{8,16},{9,17... | collective-permute-start | bytes 2064392 | tf_op jit(solution)/shard_map/ppermute | solution.py:265
  240.0 19.1 %collective-permute-start.59 = (bf16[72,2688]{1,0:T(8,128)(2,1)S(1)}, bf16[72,2688]{1,0:T(8,128)(2,1)S(1)}, u32[]{:S(2)}, u32[]{:S(2)}) collective-permute-start(bf16[72,2688]{1,0:T(8,128)(2,1)S(1)} %get-tuple-element.116), channel_id=1, source_target_pairs={{0,2},{1,3},{2,0},{3,1},{4,6},{5,7},{6,4},{7,5},{8,10},{9,11},{10,... | collective-permute-start | bytes 1161224 | tf_op jit(solution)/shard_map/ppermute | solution.py:257
  241.0 19.0 %collective-permute-start.60 = (bf16[72,2688]{1,0:T(8,128)(2,1)S(1)}, bf16[72,2688]{1,0:T(8,128)(2,1)S(1)}, u32[]{:S(2)}, u32[]{:S(2)}) collective-permute-start(bf16[72,2688]{1,0:T(8,128)(2,1)S(1)} %get-tuple-element.115), channel_id=1, source_target_pairs={{0,4},{1,5},{2,6},{3,7},{4,0},{5,1},{6,2},{7,3},{8,12},{9,13},{10,... | collective-permute-start | bytes 1161224 | tf_op jit(solution)/shard_map/ppermute | solution.py:257
  242.4 17.7 %collective-permute-start.61 = (bf16[72,2688]{1,0:T(8,128)(2,1)S(1)}, bf16[72,2688]{1,0:T(8,128)(2,1)S(1)}, u32[]{:S(2)}, u32[]{:S(2)}) collective-permute-start(bf16[72,2688]{1,0:T(8,128)(2,1)S(1)} %get-tuple-element.114), channel_id=1, source_target_pairs={{0,6},{1,7},{2,4},{3,5},{4,2},{5,3},{6,0},{7,1},{8,14},{9,15},{10,... | collective-permute-start | bytes 1161224 | tf_op jit(solution)/shard_map/ppermute | solution.py:257
  (36 other events, 422.0 us)

commit v3 on v2

v3 whole, which is shorter than its diff:
```python
import functools

import jax
import jax.numpy as jnp
from jax import lax
from jax.experimental import pallas as pl
from jax.experimental.pallas import tpu as pltpu
from jax.sharding import PartitionSpec as P

AXES = ("seq", "grp")
N = 64
G = 8
EPS = 1e-05
DEC = 16
VMEM_LIMIT = 24 * 1024 * 1024
f32 = jnp.float32
bf16 = jnp.bfloat16


def dot(a, b, contract, precision=None):
    return lax.dot_general(
        a, b, ((contract[0], contract[1]), ((), ())), preferred_element_type=f32, precision=precision
    )


def spread_lanes(columns, width):
    count = len(columns)
    rows = columns[0].shape[0]
    lane = lax.broadcasted_iota(jnp.int32, (rows, count * width), 1)
    out = jnp.broadcast_to(columns[-1], (rows, count * width))
    for j in range(count - 2, -1, -1):
        out = jnp.where(lane < (j + 1) * width, columns[j], out)
    return out


def split_decay(d):
    whole = jnp.floor(d)
    part = d - whole
    coarse = jnp.floor(part * 256.0) * (1.0 / 256.0)
    fine = part - coarse
    row = lax.broadcasted_iota(jnp.int32, (DEC, d.shape[1]), 0)
    rows = jnp.where(row == 0, whole, jnp.where(row == 1, coarse, jnp.where(row == 2, fine, 0.0)))
    return rows.astype(bf16)


def join_decay(rows):
    return jnp.sum(rows.astype(f32), axis=0, keepdims=True)


def silu(x):
    return x * (1.0 / (1.0 + jnp.exp(-x)))


def columns(blocks, inner, keys, c, width, which):
    start, first = 0, 0
    for extent in (inner, keys, keys):
        size = extent // blocks
        if c < first + size:
            return pl.ds(pl.multiple_of(start + which * size + (c - first), width), width)
        start, first = start + extent, first + size


def pick_kernel(blocks, inner, width, at_ref, x_ref, tail_ref, *outs):
    half = at_ref[1]
    length, channels = x_ref.shape
    keys = (channels - inner) // 2
    tail_ref[...] = x_ref[length - tail_ref.shape[0] :, :]
    for b in range(1, blocks):
        for c in range(0, channels // blocks, width):
            outs[b - 1][:, c : c + width] = x_ref[
                :, columns(blocks, inner, keys, c, width, half ^ b)
            ]


def running(ld):
    length = ld.shape[1]
    low = (
        lax.broadcasted_iota(jnp.int32, (length, length), 0)
        >= lax.broadcasted_iota(jnp.int32, (length, length), 1)
    ).astype(f32)
    return (
        dot(ld, low, ((1,), (1,)), lax.Precision.HIGHEST),
        dot(low, ld, ((1,), (1,)), lax.Precision.HIGHEST),
    )


def start_kernel(members, blocks, at_ref, cw_ref, z_ref, *rest):
    xs, prevs, lds = rest[:blocks], rest[blocks : 2 * blocks], rest[2 * blocks : 3 * blocks]
    rest = rest[3 * blocks :]
    acts, outs, scr = rest[:blocks], rest[blocks : blocks + members], rest[-1]
    z_outs = rest[blocks + members : -1]
    member, half = at_ref[0], at_ref[1]
    length = xs[0].shape[0]
    channels = xs[0].shape[1] // blocks
    heads = lds[0].shape[0] // blocks
    count = scr.shape[0]
    per_group = heads // count
    inner = channels - 2 * count * N
    width = inner // count
    head_size = width // per_group
    halo, taps = prevs[0].shape[0], cw_ref.shape[0]
    for b in range(blocks):
        ld = lds[b][pl.ds(pl.multiple_of(half * heads, heads), heads), :]
        cumt = running(ld)[1]
        last = cumt[length - 1 : length, :]
        to_end = jnp.exp(last - cumt)
        act_ref = acts[b]
        for c in range(0, channels, width):
            cols = slice(c, c + width)
            at = columns(blocks, inner * blocks, count * N * blocks, c, width, half)
            padded = jnp.concatenate(
                [prevs[b][:, at], xs[b][:, cols if b else at]], axis=0
            ).astype(f32)
            first = halo - taps + 1
            total = cw_ref[0:1, at] * padded[first : first + length]
            for k in range(1, taps):
                total = total + cw_ref[k : k + 1, at] * padded[first + k : first + k + length]
            act_ref[:, cols] = silu(total).astype(bf16)
        slot = half ^ b
        for g in range(count):
            v = act_ref[:, g * width : (g + 1) * width].astype(f32)
            ik = act_ref[:, inner + g * N : inner + (g + 1) * N]
            hs = range(g * per_group, (g + 1) * per_group)
            weighted = (v * spread_lanes([to_end[:, h : h + 1] for h in hs], head_size)).astype(bf16)
            scr[g, slot, :N, :] = dot(ik, weighted, ((0,), (0,))).astype(bf16)
            scr[g, slot, N:, :] = split_decay(
                spread_lanes([last[:, h : h + 1] for h in hs], head_size)
            )
    for m in range(members):
        outs[m][...] = scr[member ^ m]
    for b in range(1, blocks):
        for c in range(0, inner, width):
            at = pl.ds(pl.multiple_of((half ^ b) * inner + c, width), width)
            z_outs[b - 1][:, c : c + width] = z_ref[:, at]


def in_order(members, blocks, member, chunks, scr):
    for m in range(members):
        who = member ^ m
        for k in range(blocks):
            scr[(who >> 1) * 2 * blocks + 2 * k + (who & 1)] = chunks[m][k]


def plane_kernel(members, blocks, at_ref, *rest):
    chunks, out, scr = rest[:members], rest[members], rest[members + 1]
    in_order(members, blocks, at_ref[0], chunks, scr)
    state = jnp.zeros((N, out.shape[1]), f32)
    total = jnp.zeros((1, out.shape[1]), f32)
    for s in range(members * blocks):
        decay = join_decay(scr[s, N:, :])
        state = jnp.exp(decay) * state + scr[s, :N, :].astype(f32)
        total = total + decay
    out[:N, :] = state.astype(bf16)
    out[N:, :] = split_decay(total)


def pair_kernel(stage, at_ref, own_ref, other_ref, out_ref):
    later = ((at_ref[3] >> stage) & 1) == 1
    own, other = own_ref[:N, :].astype(f32), other_ref[:N, :].astype(f32)
    own_decay, other_decay = join_decay(own_ref[N:, :]), join_decay(other_ref[N:, :])
    first, second = jnp.where(later, other, own), jnp.where(later, own, other)
    out_ref[:N, :] = (jnp.exp(jnp.where(later, own_decay, other_decay)) * first + second).astype(bf16)
    out_ref[N:, :] = split_decay(own_decay + other_decay)


def enter_kernel(members, blocks, stages, at_ref, scr, *rest):
    earlier, outs, inc = rest[:stages], rest[stages : stages + members], rest[-1]
    member = at_ref[0]
    state = jnp.zeros((N, scr.shape[2]), f32)
    for stage in range(stages - 1, -1, -1):
        e = earlier[stage]
        joined = jnp.exp(join_decay(e[N:, :])) * state + e[:N, :].astype(f32)
        state = jnp.where(((at_ref[3] >> stage) & 1) == 1, joined, state)
    for s in range(members * blocks):
        inc[s] = state.astype(bf16)
        state = jnp.exp(join_decay(scr[s, N:, :])) * state + scr[s, :N, :].astype(f32)
    for m in range(members):
        who = member ^ m
        for k in range(blocks):
            outs[m][k] = inc[(who >> 1) * 2 * blocks + 2 * k + (who & 1)]


def inside_kernel(count, blocks, at_ref, *refs):
    acts, lds, outs = (refs[k * blocks : (k + 1) * blocks] for k in range(3))
    length, channels = acts[0].shape
    heads = lds[0].shape[0] // blocks
    per_group = heads // count
    inner = channels - 2 * count * N
    head_size = inner // heads
    causal = lax.broadcasted_iota(jnp.int32, (length, length), 0) >= lax.broadcasted_iota(
        jnp.int32, (length, length), 1
    )
    for b in range(blocks):
        act_ref, out_ref = acts[b], outs[b]
        cum, cumt = running(lds[b][pl.ds(pl.multiple_of(at_ref[1] * heads, heads), heads), :])
        for g in range(count):
            ik = act_ref[:, inner + g * N : inner + (g + 1) * N]
            ok = act_ref[:, inner + (count + g) * N : inner + (count + g + 1) * N]
            meet = jnp.where(causal, dot(ok, ik, ((1,), (1,))), 0.0)
            for h in range(g * per_group, (g + 1) * per_group):
                gap = jnp.where(causal, cumt[:, h : h + 1] - cum[h : h + 1, :], 0.0)
                mixing = (jnp.exp(gap) * meet).astype(bf16)
                cols = slice(h * head_size, (h + 1) * head_size)
                out_ref[:, cols] = dot(mixing, act_ref[:, cols], ((1,), (0,)))


def norm_kernel(members, blocks, b, at_ref, gain_ref, act_ref, ld_ref, inside_ref, z_ref, *rest):
    incoming, own_ref, pair_ref = rest[:members], rest[members], rest[members + 1]
    out_ref, scr, mix = rest[-3], rest[-2], rest[-1]
    member, half, core = at_ref[0], at_ref[1], at_ref[2]
    for m in range(members):
        scr[member ^ m] = incoming[m][...]
    inner = z_ref.shape[1] if b else z_ref.shape[1] // blocks
    heads = ld_ref.shape[0] // blocks
    count = scr.shape[0]
    per_group = heads // count
    width = inner // count
    head_size = inner // heads
    shard = count // 2
    reach = jnp.exp(running(ld_ref[pl.ds(pl.multiple_of(half * heads, heads), heads), :])[1])
    slot = half ^ b
    for g in range(count):
        cols = slice(g * width, (g + 1) * width)
        ok = act_ref[:, inner + (count + g) * N : inner + (count + g + 1) * N]
        hs = range(g * per_group, (g + 1) * per_group)
        far = dot(ok, scr[g, slot], ((1,), (0,)))
        ssm = inside_ref[:, cols] + far * spread_lanes([reach[:, h : h + 1] for h in hs], head_size)
        at = pl.ds(pl.multiple_of(half * inner + g * width, width), width)
        gated = ssm * silu(z_ref[:, cols if b else at].astype(f32))
        square = jnp.mean(gated * gated, axis=1, keepdims=True)
        mix[((g // shard) ^ core) * shard + g % shard] = (
            gated * lax.rsqrt(square + EPS) * gain_ref[:, at]
        ).astype(bf16)
    model = out_ref.shape[1]
    tile = 384 if model % 384 == 0 else model
    for c in range(0, model, tile):
        total = None
        for g in range(count):
            rows = (own_ref, pair_ref)[g // shard]
            at = (g % shard) * width
            part = dot(mix[g], rows[at : at + width, c : c + tile], ((1,), (0,)))
            total = part if total is None else total + part
        out_ref[:, c : c + tile] = total.astype(out_ref.dtype)


def token_kernel(blocks, gain_ref, hidden_ref, own_ref, meta_ref, *rest):
    others, residual_ref, block_ref = rest[: blocks - 1], rest[blocks - 1], rest[blocks]
    model = hidden_ref.shape[1]
    total = hidden_ref[...].astype(f32) + own_ref[...]
    for other in others:
        total = total + other[...].astype(f32)
    residual = total.astype(bf16)
    residual_ref[...] = residual
    wide = residual.astype(f32)
    square = jnp.mean(wide * wide, axis=1, keepdims=True)
    block_ref[:, :model] = (wide * lax.rsqrt(square + EPS) * gain_ref[...]).astype(bf16)
    block_ref[:, model:] = meta_ref[...]


def dispatch_kernel(plane, devices, capacity, pieces, at_ref, own_ref, *rest):
    pair_refs, outs, weigh_ref = rest[:pieces], rest[pieces:-1], rest[-1]
    length, model = own_ref.shape[0], outs[0].shape[1]
    rows = outs[0].shape[0]
    lanes = len(outs) * rows
    device = lax.broadcasted_iota(jnp.int32, (devices, lanes), 0)
    lane = lax.broadcasted_iota(jnp.int32, (devices, lanes), 1)
    wanted = jnp.zeros((devices, lanes), jnp.int32)
    start = lax.broadcasted_iota(jnp.int32, (length, lanes), 1)
    for k in range(len(outs)):
        inside = (lane >= k * rows) & (lane < (k + 1) * rows)
        wanted = jnp.where(inside, at_ref[1] + (at_ref[0] ^ (2 * k)), wanted)
    place = start
    for k in range(1, len(outs)):
        place = jnp.where(start >= k * rows, start - k * rows, place)
    place = place.astype(f32)
    select = (device == wanted).astype(f32).astype(bf16)
    total = None
    first = 0
    for ref in (own_ref,) + pair_refs:
        b, count = (0 if first < length else 1), ref.shape[0]
        slot = dot(ref[:, model : model + devices], select, ((1,), (0,)))
        gate = dot(ref[:, model + devices : model + 2 * devices], select, ((1,), (0,))) + dot(
            ref[:, model + 2 * devices : model + 3 * devices], select, ((1,), (0,))
        )
        hit = (slot >= 0.0) & (slot + float(b * capacity) == place[:count])
        weigh_ref[first : first + count, :] = jnp.where(hit, gate, 0.0).astype(bf16)
        take = jnp.where(hit, 1.0, 0.0).astype(bf16)
        part = dot(take, ref[:, :model], ((0,), (0,)))
        total = part if total is None else total + part
        first += count
    for k in range(len(outs)):
        outs[k][...] = total[k * rows : (k + 1) * rows].astype(bf16)


def after(x, *others):
    return lax.optimization_barrier((x,) + others)[0]


def local(
    hidden,
    conv_input,
    z_stream,
    log_decay,
    conv_weight,
    norm_gain,
    out_weight,
    moe_gain,
    routes,
    gate_weights,
    expert_home,
    up_weight,
    down_weight,
):
    n_grp = lax.axis_size("grp")
    devices = lax.axis_size("seq") * n_grp
    plane = 2 * n_grp
    outer = devices // plane
    me = lax.axis_index("seq") * n_grp + lax.axis_index("grp")
    r = lax.rem(me, plane)
    place = lax.div(me, plane)

    def swap(x, m):
        return lax.ppermute(x, AXES, [(d, d ^ m) for d in range(devices)])

    def onward(x, by):
        return lax.ppermute(
            x, AXES, [(d, d + by) for d in range(devices) if d + by < devices]
        )

    def turn(x):
        return lax.ppermute(x, AXES, [(d, (d + plane) % devices) for d in range(devices)])

    length, channels = conv_input.shape
    inner = z_stream.shape[1]
    width = inner // G
    model = hidden.shape[1]
    smem = pl.BlockSpec(memory_space=pltpu.SMEM)
    halo = 16

    blocks = n_grp // 2
    members = plane // blocks
    grp = lax.axis_index("grp")
    half = lax.div(grp, 2)
    core = lax.rem(grp, 2)
    member = lax.div(r, n_grp) * 2 + core
    at_member = jnp.stack([member, half, core, place]).astype(jnp.int32)
    count = G // blocks

    def onward_to(x, by, m):
        return lax.ppermute(
            x, AXES, [(d, (d + by) ^ m) for d in range(devices) if d + by < devices]
        )

    shapes = jax.ShapeDtypeStruct
    vm = pl.BlockSpec(memory_space=pltpu.VMEM)
    wide = channels // blocks
    chunk = (N + DEC, width)

    def kernel_call(kernel, inputs, outs, scratch=(), flops=0, moved=0, scalars=True):
        return pl.pallas_call(
            kernel,
            out_shape=outs,
            in_specs=([smem] if scalars else []) + [vm] * (len(inputs) - (1 if scalars else 0)),
            scratch_shapes=list(scratch),
            compiler_params=pltpu.CompilerParams(vmem_limit_bytes=VMEM_LIMIT),
            cost_estimate=pl.CostEstimate(flops=flops, bytes_accessed=moved, transcendentals=0),
        )(*inputs)

    picked = kernel_call(
        functools.partial(pick_kernel, blocks, inner, width),
        [at_member, conv_input],
        [shapes((halo, channels), bf16)] + [shapes((length, wide), bf16)] * (blocks - 1),
    )
    tail = picked[0]
    xs, prevs, lds = [conv_input], [onward_to(tail, 1, 0)], [log_decay]
    for b in range(1, blocks):
        xs.append(swap(picked[b], 2 * b))
        prevs.append(onward_to(tail, 1, 2 * b))
        lds.append(swap(log_decay, 2 * b))

    rows_own = out_weight
    rows_pair = swap(out_weight, 1)
    shard = out_weight.shape[0]

    first = kernel_call(
        functools.partial(start_kernel, members, blocks),
        [at_member, conv_weight, z_stream] + xs + prevs + lds,
        [shapes((length, wide), bf16)] * blocks
        + [shapes((blocks,) + chunk, bf16)] * members
        + [shapes((length, inner // blocks), bf16)] * (blocks - 1),
        [pltpu.VMEM((count, blocks) + chunk, bf16)],
        50000000,
        8000000,
    )
    acts = first[:blocks]
    sends = first[blocks : blocks + members]
    zs = [z_stream] + [swap(first[blocks + members + b - 1], 2 * b) for b in range(1, blocks)]
    mask = [(m >> 1) * n_grp + (m & 1) for m in range(members)]
    chunks = [sends[0]] + [swap(sends[m], mask[m]) for m in range(1, members)]
    inside = kernel_call(
        functools.partial(inside_kernel, count, blocks),
        [at_member] + list(acts) + lds,
        [shapes((length, inner // blocks), f32)] * blocks,
        (),
        100000000,
        15000000,
    )
    whole, ordered = kernel_call(
        functools.partial(plane_kernel, members, blocks),
        [at_member] + chunks,
        [shapes(chunk, bf16), shapes((plane,) + chunk, bf16)],
    )
    earlier, stage = [], 0
    while (1 << stage) < outer:
        earlier.append(swap(whole, plane << stage))
        stage += 1
        if (1 << stage) < outer:
            whole = kernel_call(
                functools.partial(pair_kernel, stage - 1),
                [at_member, whole, earlier[-1]],
                shapes(chunk, bf16),
            )
    entering = kernel_call(
        functools.partial(enter_kernel, members, blocks, stage),
        [at_member, ordered] + earlier,
        [shapes((blocks, N, width), bf16)] * members,
        [pltpu.VMEM((plane, N, width), bf16)],
        1000000,
        2000000,
    )
    incoming = [entering[0]] + [swap(entering[m], mask[m]) for m in range(1, members)]
    def project(b):
        return kernel_call(
            functools.partial(norm_kernel, members, blocks, b),
            [at_member, norm_gain[None, :], acts[b], lds[b], inside[b], zs[b]]
            + incoming
            + [rows_own, rows_pair],
            shapes((length, model), bf16 if b else f32),
            [pltpu.VMEM((count, blocks, N, width), bf16), pltpu.VMEM((count, length, width), bf16)],
            800000000,
            8000000,
        )

    others = [swap(project(b), 2 * b) for b in range(1, blocks)]
    mine = project(0)

    top_count = routes.shape[1]
    capacity = max(2, 3 * length * top_count // (2 * devices))
    experts = expert_home.shape[0]
    picked = routes[:, :, None] == jnp.arange(experts, dtype=jnp.int32)[None, None, :]
    target = jnp.sum(jnp.where(picked, expert_home[None, None, :], 0), axis=2)
    at_device = target[:, :, None] == jnp.arange(devices, dtype=jnp.int32)[None, None, :]
    chosen = jnp.any(at_device, axis=1)
    gates = jnp.sum(jnp.where(at_device, gate_weights[:, :, None], 0.0), axis=1)
    before = (
        lax.broadcasted_iota(jnp.int32, (length, length), 0)
        > lax.broadcasted_iota(jnp.int32, (length, length), 1)
    ).astype(bf16)
    rank = jnp.dot(before, chosen.astype(bf16), preferred_element_type=f32)
    slots = jnp.where(chosen, rank, -1.0)
    gate_high = jnp.floor(gates * 128.0) * (1.0 / 128.0)
    meta = jnp.concatenate([slots, gate_high, gates - gate_high], axis=1).astype(bf16)
    extra = -(-3 * devices // 128) * 128
    meta = jnp.pad(meta, ((0, 0), (0, extra - 3 * devices)))

    up_local = up_weight[0]
    down_local = down_weight[0]
    hops = list(range(0, plane, 2))
    two = -(-2 * capacity // 8) * 8

    at = jnp.stack([r, place * plane]).astype(jnp.int32)

    def serve(block, pair):
        out = pl.pallas_call(
            functools.partial(dispatch_kernel, plane, devices, capacity, len(pair)),
            out_shape=[shapes((two, model), bf16)] * len(hops)
            + [shapes((2 * length, len(hops) * two), bf16)],
            in_specs=[smem, vm] + [vm] * len(pair),
            compiler_params=pltpu.CompilerParams(vmem_limit_bytes=VMEM_LIMIT),
            cost_estimate=pl.CostEstimate(flops=0, bytes_accessed=0, transcendentals=0),
        )(at, block, *pair)
        sent = out[:-1]
        return out[-1], [sent[0]] + [swap(sent[k], hops[k]) for k in range(1, len(hops))], sent

    def work(arrived):
        rows = jnp.concatenate(arrived, axis=0)
        up = jnp.dot(rows, up_local, preferred_element_type=f32)
        squared = jnp.square(jax.nn.relu(up)).astype(bf16)
        return jnp.dot(squared, down_local, preferred_element_type=f32).astype(bf16)

    def send_back(result):
        parts = [result[k * two : (k + 1) * two] for k in range(len(hops))]
        return [parts[0]] + [swap(parts[k], hops[k]) for k in range(1, len(hops))]

    def gather_up(weigh, returned):
        part = jnp.dot(weigh, jnp.concatenate(returned, axis=0), preferred_element_type=f32)
        return part[:length] + swap(part[length:].astype(bf16), 1).astype(f32)

    residual_one, block = kernel_call(
        functools.partial(token_kernel, blocks),
        [moe_gain[None, :], hidden, mine, meta] + others,
        [shapes((length, model), bf16), shapes((length, model + extra), bf16)],
        scalars=False,
    )
    weighs, results, returned = {}, {}, {}
    arrived = {}
    for step in range(outer):
        pair = [swap(block[: length // 2], 1), swap(block[length // 2 :], 1)]
        if step >= 2:
            pair[0] = after(pair[0], results[step - 2])
        weighs[step], arrived[step], sent = serve(block, pair)
        if step + 1 < outer:
            block = turn(after(block, weighs[step]))
        if step >= 1:
            results[step - 1] = work(arrived[step - 1])
            if step >= 2:
                returned[step - 1] = send_back(results[step - 1])
    results[outer - 1] = work(arrived[outer - 1])
    if outer > 1:
        returned[outer - 1] = send_back(results[outer - 1])
    returned[0] = send_back(after(results[0], results[outer - 1]))
    carried = None
    for step in list(range(1, outer)) + [0]:
        back = returned[step]
        if carried is not None and step == 0:
            back = [after(back[0], carried)] + back[1:]
        part = gather_up(weighs[step], back)
        if carried is not None:
            part = part + carried.astype(f32)
        if step:
            carried = turn(part.astype(bf16))
    return (residual_one.astype(f32) + part).astype(bf16)


def solution(mesh):
    placed = (
        P(AXES, None),
        P(AXES, None),
        P(AXES, None),
        P(None, AXES),
        P(),
        P(),
        P("grp", None),
        P(),
        P(AXES, None),
        P(AXES, None),
        P(),
        P(AXES, None, None),
        P(AXES, None, None),
    )
    return jax.shard_map(local, mesh=mesh, in_specs=placed, out_specs=P(AXES, None), check_vma=False)
```

time: 265 us -> 256 us (0.966)
  waiting for transfers between devices: 151 us -> 132 us
  Pallas kernels: 15.6 us -> 27.1 us
  local copies, waits for them, and re-layouts: 4.74 us -> 12.6 us
  matrix products: 29.7 us -> 22.3 us
  starting transfers between devices: 59.9 us -> 55.4 us
    ppermute x53 -> x49, waiting for transfers between devices: 115 us -> 97.6 us  [swap(): return lax.ppermute(x, AXES, [(d, d ^ m) for d in range(devices)])]
    pallas_call x5 -> x9, Pallas kernels: 6.17 us -> 17.7 us  [kernel_call(): pl.pallas_call(kernel, out_shape=outs, in_specs=([smem] if scalars else [...]
    dot_general x4 -> x0, matrix products: 8.16 us -> none  [the longest x2 4.72 us: project(): jnp.dot(part[:, shard:], rows_pair, preferred_element_type=f32)]
    unnamed x42, local copies, waits for them, and re-layouts: 2.75 us -> 8.13 us
    ppermute x4 -> x2, starting transfers between devices: 11.4 us -> 6.51 us  [onward_to(): lax.ppermute(x, AXES, [(d, d + by ^ m) for d in range(devices) if d + by...]
    ppermute x4 -> x2, waiting for transfers between devices: 3.63 us -> 0.01 us  [onward_to(): lax.ppermute(x, AXES, [(d, d + by ^ m) for d in range(devices) if d + by...]
    ppermute x53 -> x49, starting transfers between devices: 47.8 us -> 46.4 us  [swap(): return lax.ppermute(x, AXES, [(d, d ^ m) for d in range(devices)])]
  transfers between devices with their start and end apart: 63 -> 57, of which waited for: 34 -> 30; matrix products, arithmetic and copies ran while one was open for 10% -> 11% of each run, Pallas kernels for 5% -> 7%
where the time goes in v3:
time: 256 us; the launch traced here: 255 us
  waiting for transfers between devices  132 us (52%)
  starting transfers between devices  55.4 us (22%)
  Pallas kernels  27.1 us (11%)
  matrix products  22.3 us (9%)
  local copies, waits for them, and re-layouts  12.6 us (5%)
  other arithmetic  4.92 us (2%)
    ppermute x49, waiting for transfers between devices, swap(): return lax.ppermute(x, AXES, [(d, d ^ m) for d in range(devices)])  97.6 us
    ppermute x49, starting transfers between devices, swap(): return lax.ppermute(x, AXES, [(d, d ^ m) for d in range(devices)])  46.4 us
    ppermute x6, waiting for transfers between devices, turn(): lax.ppermute(x, AXES, [(d, (d + plane) % devices) for d in range(devices)])  34.5 us
    pallas_call x9, Pallas kernels, kernel_call(): pl.pallas_call(kernel, out_shape=outs, in_specs=([smem] if scalars else [...  17.7 us
    dot_general x4, matrix products, work(): up = jnp.dot(rows, up_local, preferred_element_type=f32)  10.4 us
    pallas_call x4, Pallas kernels, serve(): pl.pallas_call(functools.partial(dispatch_kernel, plane, devices, capacit...  9.4 us
    unnamed x42, local copies, waits for them, and re-layouts  8.13 us
    dot_general x4, matrix products, work(): return jnp.dot(squared, down_local, preferred_element_type=f32).astype(bf16)  7.46 us
  transfers between devices with their start and end apart: 57, of which 30 were waited for; matrix products, arithmetic and copies ran while one was open for 11% of the time, Pallas kernels for 7%

profile of v3, /device:TPU:0, one launch (start us, length us, event | category | flops | bytes accessed | tf_op | source)
XLA Modules:
  0.0 255.0 jit_solution(876508098645783258)
XLA Ops:
  2.5 2.4 collective-permute-start
  5.0 2.1 collective-permute-start.1
  7.0 4.4 %collective-permute-start.2 = (bf16[16,3072]{1,0:T(8,128)(2,1)S(1)}, bf16[16,3072]{1,0:T(8,128)(2,1)S(1)}, u32[]{:S(2)}, u32[]{:S(2)}) collective-permute-start(bf16[16,3072]{1,0:T(8,128)(2,1)S(1)} %get-tuple-element.52), channel_id=1, source_target_pairs={{0,3},{1,0},{2,1},{3,6},{4,7},{5,4},{6,5},{7,10},{8,11},{9,8},{10,... | collective-permute-start | bytes 294920 | tf_op jit(solution)/shard_map/ppermute | solution.py:350
  11.6 5.6 %collective-permute-done.3.rest_5_.refs_3_.ld_ref = f32[32,128]{1,0:T(8,128)S(1)} collective-permute-done((f32[32,128]{1,0:T(8,128)}, f32[32,128]{1,0:T(8,128)S(1)}, u32[]{:S(2)}, u32[]{:S(2)}) %collective-permute-start.3) | collective-permute-done | bytes 16416 | tf_op jit(solution)/shard_map/ppermute | solution.py:323
  19.7 2.7 %shard_map.128 = (bf16[128,1536]{1,0:T(8,128)(2,1)S(1)}, bf16[128,1536]{1,0:T(8,128)(2,1)S(1)}, bf16[2,80,256]{2,1,0:T(8,128)(2,1)S(1)}, bf16[2,80,256]{2,1,0:T(...) custom-call(s32[4]{0:T(128)S(1)} %pad_add_fusion.at_ref, ...), custom_call_target="tpu_custom_call" | custom-call | flops 50000000 | bytes 8000000 | tf_op jit(solution)/shard_map/pallas_call | solution.py:360
  24.3 3.4 %collective-permute-done.5.rest_2_ = bf16[2,80,256]{2,1,0:T(8,128)(2,1)S(1)} collective-permute-done((bf16[2,80,256]{2,1,0:T(8,128)(2,1)S(1)}, bf16[2,80,256]{2,1,0:T(8,128)(2,1)S(1)}, u32[]{:S(2)}, u32[]{:S(2)}) %collective-permute-start.5) | collective-permute-done | bytes 81952 | tf_op jit(solution)/shard_map/ppermute | solution.py:323
  29.3 2.1 collective-permute-start.7
  31.4 1.5 collective-permute-start.13
  33.9 3.1 %collective-permute-start.8 = (bf16[80,256]{1,0:T(8,128)(2,1)S(1)}, bf16[80,256]{1,0:T(8,128)(2,1)S(1)}, u32[]{:S(2)}, u32[]{:S(2)}) collective-permute-start(bf16[80,256]{1,0:T(8,128)(2,1)S(1)} %shard_map.131), channel_id=1, source_target_pairs={{0,16},{1,17},{2,18},{3,19},{4,20},{5,21},{6,22},{7,23},{8,24},{9,... | collective-permute-start | bytes 122888 | tf_op jit(solution)/shard_map/ppermute | solution.py:323
  42.5 2.7 %shard_map.129 = (f32[128,1024]{1,0:T(8,128)S(1)}, f32[128,1024]{1,0:T(8,128)S(1)}) custom-call(s32[4]{0:T(128)S(1)} %pad_add_fusion.at_ref, bf16[128,1536]{1,0:T(8,128)(2,1)S(1)} %get-tuple-element.53.refs_0_.act_ref, bf16[128,1536]{1,0:T(8,128)(2,1)S(1)} %get-tuple-element.54.refs_1_.act_ref, f32[32,128]{1,0:T(8,128)S(1)} %copy-done.9, ...), custom_call_target="tpu_custom_call" | custom-call | flops 100000000 | bytes 15000000 | tf_op jit(solution)/shard_map/pallas_call | solution.py:360
  46.1 4.6 %shard_map.134 = bf16[128,2688]{1,0:T(8,128)(2,1)} custom-call(s32[4]{0:T(128)S(1)} %pad_add_fusion.at_ref, f32[1,2048]{1,0:T(1,128)S(1)} %bitcast.66, bf16[128,1536]{1,0:T(8,128)(2,1)S(1)} %get-tuple-element.54.refs_1_.act_ref, f32[32,128]{1,0:T(8,128)S(1)} %collective-permute-done.3.rest_5_.refs_3_.ld_ref, f32[128,1024]{1,0:T(8,128)S(1)} %get-tuple-element.66.inside_ref, ...), custom_call_target="tpu_custom_call" | custom-call | flops 800000000 | bytes 8000000 | tf_op jit(solution)/shard_map/pallas_call | solution.py:360
  50.6 1.8 collective-permute-start.14
  61.8 3.7 %shard_map.133.own_ref = f32[128,2688]{1,0:T(8,128)S(1)} custom-call(s32[4]{0:T(128)S(1)} %copy-done.13, f32[1,2048]{1,0:T(1,128)S(1)} %bitcast.67, bf16[128,1536]{1,0:T(8,128)(2,1)S(1)} %copy-done.5, f32[32,128]{1,0:T(8,128)S(1)} %copy-done.10, f32[128,1024]{1,0:T(8,128)S(1)} %copy-done.8, bf16[128,2048]{1,0:T(8,128)(2,1)S(1)} %copy-done.3, ...), custom_call_target="tpu_custom_call" | custom-call | flops 800000000 | bytes 8000000 | tf_op jit(solution)/shard_map/pallas_call | solution.py:360
  65.5 2.9 %collective-permute-done.14.rest_0_ = bf16[128,2688]{1,0:T(8,128)(2,1)} collective-permute-done((bf16[128,2688]{1,0:T(8,128)(2,1)}, bf16[128,2688]{1,0:T(8,128)(2,1)}, u32[]{:S(2)}, u32[]{:S(2)}) %collective-permute-start.14) | collective-permute-done | bytes 688160 | tf_op jit(solution)/shard_map/ppermute | solution.py:323
  68.4 1.6 shard_map.135
  72.3 2.4 shard_map.136
  74.7 2.1 collective-permute-start.20
  76.7 1.5 collective-permute-start.17
  80.2 15.3 %collective-permute-done.20.own_ref = bf16[128,2816]{1,0:T(8,128)(2,1)S(1)} collective-permute-done((bf16[128,2816]{1,0:T(8,128)(2,1)S(1)}, bf16[128,2816]{1,0:T(8,128)(2,1)S(1)}, u32[]{:S(2)}, u32[]{:S(2)}) %collective-permute-start.20) | collective-permute-done | bytes 720928 | tf_op jit(solution)/shard_map/ppermute | solution.py:331
  97.8 2.3 shard_map.137
  100.2 1.6 collective-permute-start.28
  103.7 4.7 %fusion.151 = bf16[288,1024]{1,0:T(8,128)(2,1)S(1)} fusion(bf16[1,2688,1024]{2,1,0:T(8,128)(2,1)} %param.24, bf16[72,2688]{1,0:T(8,128)(2,1)S(1)} %collective-permute-done.19, bf16[72,2688]{1,0:T(8,128)(2,1)S(1)} %collective-permute-done.18, bf16[72,2688]{1,0:T(8,128)(2,1)S(1)} %collective-permute-done.17, bf16[72,2688]{1,0:T(8,128)(2,1)S(1)} %get-tuple-element.71), kind=kOutput, calls=%fused_computation.107 | convolution fusion | flops 1592524800 | bytes 7643136 | tf_op jit(solution)/shard_map/dot_general | solution.py:487
  108.5 3.6 %collective-permute-done.28 = bf16[72,2688]{1,0:T(8,128)(2,1)S(1)} collective-permute-done((bf16[72,2688]{1,0:T(8,128)(2,1)S(1)}, bf16[72,2688]{1,0:T(8,128)(2,1)S(1)}, u32[]{:S(2)}, u32[]{:S(2)}) %collective-permute-start.28) | collective-permute-done | bytes 387104 | tf_op jit(solution)/shard_map/ppermute | solution.py:323
  112.1 8.7 %collective-permute-done.29 = bf16[72,2688]{1,0:T(8,128)(2,1)S(1)} collective-permute-done((bf16[72,2688]{1,0:T(8,128)(2,1)S(1)}, bf16[72,2688]{1,0:T(8,128)(2,1)S(1)}, u32[]{:S(2)}, u32[]{:S(2)}) %collective-permute-start.29) | collective-permute-done | bytes 387104 | tf_op jit(solution)/shard_map/ppermute | solution.py:323
  120.8 1.9 fusion.146
  122.7 1.9 fusion.19
  126.7 1.6 collective-permute-start.48
  128.9 1.8 fusion.16
  130.8 2.4 shard_map.138
  138.0 7.1 %collective-permute-done.47 = bf16[72,2688]{1,0:T(8,128)(2,1)S(1)} collective-permute-done((bf16[72,2688]{1,0:T(8,128)(2,1)S(1)}, bf16[72,2688]{1,0:T(8,128)(2,1)S(1)}, u32[]{:S(2)}, u32[]{:S(2)}) %collective-permute-start.47) | collective-permute-done | bytes 387104 | tf_op jit(solution)/shard_map/ppermute | solution.py:323
  147.2 6.2 %collective-permute-done.39 = bf16[72,2688]{1,0:T(8,128)(2,1)S(1)} collective-permute-done((bf16[72,2688]{1,0:T(8,128)(2,1)S(1)}, bf16[72,2688]{1,0:T(8,128)(2,1)S(1)}, u32[]{:S(2)}, u32[]{:S(2)}) %collective-permute-start.39) | collective-permute-done | bytes 387104 | tf_op jit(solution)/shard_map/ppermute | solution.py:323
  153.3 7.3 %collective-permute-done.40 = bf16[72,2688]{1,0:T(8,128)(2,1)S(1)} collective-permute-done((bf16[72,2688]{1,0:T(8,128)(2,1)S(1)}, bf16[72,2688]{1,0:T(8,128)(2,1)S(1)}, u32[]{:S(2)}, u32[]{:S(2)}) %collective-permute-start.40) | collective-permute-done | bytes 387104 | tf_op jit(solution)/shard_map/ppermute | solution.py:323
  160.7 1.9 fusion.136
  162.6 1.9 fusion.25
  165.2 2.0 collective-permute-done.26.own_ref
  170.2 2.3 shard_map.139
  175.0 2.1 collective-permute-start.34
  177.2 10.8 %collective-permute-done.43 = bf16[72,2688]{1,0:T(8,128)(2,1)S(1)} collective-permute-done((bf16[72,2688]{1,0:T(8,128)(2,1)S(1)}, bf16[72,2688]{1,0:T(8,128)(2,1)S(1)}, u32[]{:S(2)}, u32[]{:S(2)}) %collective-permute-start.43) | collective-permute-done | bytes 387104 | tf_op jit(solution)/shard_map/ppermute | solution.py:323
  189.9 13.8 %collective-permute-done.33 = bf16[72,2688]{1,0:T(8,128)(2,1)S(1)} collective-permute-done((bf16[72,2688]{1,0:T(8,128)(2,1)S(1)}, bf16[72,2688]{1,0:T(8,128)(2,1)S(1)}, u32[]{:S(2)}, u32[]{:S(2)}) %collective-permute-start.33) | collective-permute-done | bytes 387104 | tf_op jit(solution)/shard_map/ppermute | solution.py:323
  203.7 1.9 fusion.141
  205.7 1.9 fusion.22
  209.5 1.8 collective-permute-start.37
  211.5 8.1 %collective-permute-done.35 = bf16[72,2688]{1,0:T(8,128)(2,1)S(1)} collective-permute-done((bf16[72,2688]{1,0:T(8,128)(2,1)S(1)}, bf16[72,2688]{1,0:T(8,128)(2,1)S(1)}, u32[]{:S(2)}, u32[]{:S(2)}) %collective-permute-start.35) | collective-permute-done | bytes 387104 | tf_op jit(solution)/shard_map/ppermute | solution.py:323
  219.7 6.8 %collective-permute-done.36 = bf16[72,2688]{1,0:T(8,128)(2,1)S(1)} collective-permute-done((bf16[72,2688]{1,0:T(8,128)(2,1)S(1)}, bf16[72,2688]{1,0:T(8,128)(2,1)S(1)}, u32[]{:S(2)}, u32[]{:S(2)}) %collective-permute-start.36) | collective-permute-done | bytes 387104 | tf_op jit(solution)/shard_map/ppermute | solution.py:323
  227.5 1.6 collective-permute-done.51
  230.0 1.6 collective-permute-start.53
  233.5 15.6 %collective-permute-done.52 = bf16[128,2688]{1,0:T(8,128)(2,1)S(1)} collective-permute-done((bf16[128,2688]{1,0:T(8,128)(2,1)S(1)}, bf16[128,2688]{1,0:T(8,128)(2,1)S(1)}, u32[]{:S(2)}, u32[]{:S(2)}) %collective-permute-start.52) | collective-permute-done | bytes 688160 | tf_op jit(solution)/shard_map/ppermute | solution.py:331
  251.6 2.1 collective-permute-done.56
  (162 shorter events, 61.5 us)
Async XLA Ops:
  0.0 46.0 %collective-permute-start.12 = (bf16[512,2688]{1,0:T(8,128)(2,1)}, bf16[512,2688]{1,0:T(8,128)(2,1)}, u32[]{:S(2)}, u32[]{:S(2)}) collective-permute-start(bf16[512,2688]{1,0:T(8,128)(2,1)} %rest_4_.5), channel_id=1, source_target_pairs={{0,1},{1,0},{2,3},{3,2},{4,5},{5,4},{6,7},{7,6},{8,9},{9,8},{10,11... | collective-permute-start | bytes 8257544 | tf_op jit(solution)/shard_map/ppermute | solution.py:323
  2.5 14.6 %collective-permute-start = (bf16[128,1536]{1,0:T(8,128)(2,1)S(1)}, bf16[128,1536]{1,0:T(8,128)(2,1)S(1)}, u32[]{:S(2)}, u32[]{:S(2)}) collective-permute-start(bf16[128,1536]{1,0:T(8,128)(2,1)S(1)} %get-tuple-element.51), channel_id=1, source_target_pairs={{0,2},{1,3},{2,0},{3,1},{4,6},{5,7},{6,4},{7,5},{8,10},{9,11},{10,... | collective-permute-start | bytes 1179656 | tf_op jit(solution)/shard_map/ppermute | solution.py:323
  5.0 12.2 %collective-permute-start.1 = (bf16[16,3072]{1,0:T(8,128)(2,1)S(1)}, bf16[16,3072]{1,0:T(8,128)(2,1)S(1)}, u32[]{:S(2)}, u32[]{:S(2)}) collective-permute-start(bf16[16,3072]{1,0:T(8,128)(2,1)S(1)} %get-tuple-element.52), channel_id=1, source_target_pairs={{0,1},{1,2},{2,3},{3,4},{4,5},{5,6},{6,7},{7,8},{8,9},{9,10},{10,1... | collective-permute-start | bytes 294920 | tf_op jit(solution)/shard_map/ppermute | solution.py:350
  7.0 10.1 %collective-permute-start.2 = (bf16[16,3072]{1,0:T(8,128)(2,1)S(1)}, bf16[16,3072]{1,0:T(8,128)(2,1)S(1)}, u32[]{:S(2)}, u32[]{:S(2)}) collective-permute-start(bf16[16,3072]{1,0:T(8,128)(2,1)S(1)} %get-tuple-element.52), channel_id=1, source_target_pairs={{0,3},{1,0},{2,1},{3,6},{4,7},{5,4},{6,5},{7,10},{8,11},{9,8},{10,... | collective-permute-start | bytes 294920 | tf_op jit(solution)/shard_map/ppermute | solution.py:350
  11.5 5.6 %collective-permute-start.3 = (f32[32,128]{1,0:T(8,128)}, f32[32,128]{1,0:T(8,128)S(1)}, u32[]{:S(2)}, u32[]{:S(2)}) collective-permute-start(f32[32,128]{1,0:T(8,128)} %ld_ref.1), channel_id=1, source_target_pairs={{0,2},{1,3},{2,0},{3,1},{4,6},{5,7},{6,4},{7,5},{8,10},{9,11},{10,... | collective-permute-start | bytes 49160 | tf_op jit(solution)/shard_map/ppermute | solution.py:323
  22.5 5.3 %collective-permute-start.5 = (bf16[2,80,256]{2,1,0:T(8,128)(2,1)S(1)}, bf16[2,80,256]{2,1,0:T(8,128)(2,1)S(1)}, u32[]{:S(2)}, u32[]{:S(2)}) collective-permute-start(bf16[2,80,256]{2,1,0:T(8,128)(2,1)S(1)} %get-tuple-element.58), channel_id=1, source_target_pairs={{0,4},{1,5},{2,6},{3,7},{4,0},{5,1},{6,2},{7,3},{8,12},{9,13},{10,... | collective-permute-start | bytes 245768 | tf_op jit(solution)/shard_map/ppermute | solution.py:323
  23.4 5.3 %collective-permute-start.6 = (bf16[2,80,256]{2,1,0:T(8,128)(2,1)S(1)}, bf16[2,80,256]{2,1,0:T(8,128)(2,1)S(1)}, u32[]{:S(2)}, u32[]{:S(2)}) collective-permute-start(bf16[2,80,256]{2,1,0:T(8,128)(2,1)S(1)} %get-tuple-element.59), channel_id=1, source_target_pairs={{0,5},{1,4},{2,7},{3,6},{4,1},{5,0},{6,3},{7,2},{8,13},{9,12},{10,... | collective-permute-start | bytes 245768 | tf_op jit(solution)/shard_map/ppermute | solution.py:323
  29.3 4.1 %collective-permute-start.7 = (bf16[80,256]{1,0:T(8,128)(2,1)S(1)}, bf16[80,256]{1,0:T(8,128)(2,1)S(1)}, u32[]{:S(2)}, u32[]{:S(2)}) collective-permute-start(bf16[80,256]{1,0:T(8,128)(2,1)S(1)} %get-tuple-element.61.own_ref), channel_id=1, source_target_pairs={{0,8},{1,9},{2,10},{3,11},{4,12},{5,13},{6,14},{7,15},{8,0},{9,1},... | collective-permute-start | bytes 122888 | tf_op jit(solution)/shard_map/ppermute | solution.py:323
  31.4 14.7 %collective-permute-start.13 = (bf16[128,1024]{1,0:T(8,128)(2,1)S(1)}, bf16[128,1024]{1,0:T(8,128)(2,1)S(1)}, u32[]{:S(2)}, u32[]{:S(2)}) collective-permute-start(bf16[128,1024]{1,0:T(8,128)(2,1)S(1)} %get-tuple-element.67), channel_id=1, source_target_pairs={{0,2},{1,3},{2,0},{3,1},{4,6},{5,7},{6,4},{7,5},{8,10},{9,11},{10,... | collective-permute-start | bytes 786440 | tf_op jit(solution)/shard_map/ppermute | solution.py:323
  33.9 5.1 %collective-permute-start.8 = (bf16[80,256]{1,0:T(8,128)(2,1)S(1)}, bf16[80,256]{1,0:T(8,128)(2,1)S(1)}, u32[]{:S(2)}, u32[]{:S(2)}) collective-permute-start(bf16[80,256]{1,0:T(8,128)(2,1)S(1)} %shard_map.131), channel_id=1, source_target_pairs={{0,16},{1,17},{2,18},{3,19},{4,20},{5,21},{6,22},{7,23},{8,24},{9,... | collective-permute-start | bytes 122888 | tf_op jit(solution)/shard_map/ppermute | solution.py:323
  39.7 6.3 %collective-permute-start.10 = (bf16[2,64,256]{2,1,0:T(8,128)(2,1)S(1)}, bf16[2,64,256]{2,1,0:T(8,128)(2,1)S(1)}, u32[]{:S(2)}, u32[]{:S(2)}) collective-permute-start(bf16[2,64,256]{2,1,0:T(8,128)(2,1)S(1)} %get-tuple-element.64), channel_id=1, source_target_pairs={{0,4},{1,5},{2,6},{3,7},{4,0},{5,1},{6,2},{7,3},{8,12},{9,13},{10,... | collective-permute-start | bytes 196616 | tf_op jit(solution)/shard_map/ppermute | solution.py:323
  41.1 4.9 %collective-permute-start.11 = (bf16[2,64,256]{2,1,0:T(8,128)(2,1)S(1)}, bf16[2,64,256]{2,1,0:T(8,128)(2,1)S(1)}, u32[]{:S(2)}, u32[]{:S(2)}) collective-permute-start(bf16[2,64,256]{2,1,0:T(8,128)(2,1)S(1)} %get-tuple-element.65), channel_id=1, source_target_pairs={{0,5},{1,4},{2,7},{3,6},{4,1},{5,0},{6,3},{7,2},{8,13},{9,12},{10,... | collective-permute-start | bytes 196616 | tf_op jit(solution)/shard_map/ppermute | solution.py:323
  41.1 4.9 %collective-permute-start.9 = (bf16[2,64,256]{2,1,0:T(8,128)(2,1)S(1)}, bf16[2,64,256]{2,1,0:T(8,128)(2,1)S(1)}, u32[]{:S(2)}, u32[]{:S(2)}) collective-permute-start(bf16[2,64,256]{2,1,0:T(8,128)(2,1)S(1)} %get-tuple-element.63), channel_id=1, source_target_pairs={{0,1},{1,0},{2,3},{3,2},{4,5},{5,4},{6,7},{7,6},{8,9},{9,8},{10,11... | collective-permute-start | bytes 196616 | tf_op jit(solution)/shard_map/ppermute | solution.py:323
  50.6 17.7 %collective-permute-start.14 = (bf16[128,2688]{1,0:T(8,128)(2,1)}, bf16[128,2688]{1,0:T(8,128)(2,1)}, u32[]{:S(2)}, u32[]{:S(2)}) collective-permute-start(bf16[128,2688]{1,0:T(8,128)(2,1)} %shard_map.134), channel_id=1, source_target_pairs={{0,2},{1,3},{2,0},{3,1},{4,6},{5,7},{6,4},{7,5},{8,10},{9,11},{10,... | collective-permute-start | bytes 2064392 | tf_op jit(solution)/shard_map/ppermute | solution.py:323
  74.7 20.8 %collective-permute-start.20 = (bf16[128,2816]{1,0:T(8,128)(2,1)S(1)}, bf16[128,2816]{1,0:T(8,128)(2,1)S(1)}, u32[]{:S(2)}, u32[]{:S(2)}) collective-permute-start(bf16[128,2816]{1,0:T(8,128)(2,1)S(1)} %get-tuple-element.75.own_ref), channel_id=1, source_target_pairs={{0,8},{1,9},{2,10},{3,11},{4,12},{5,13},{6,14},{7,15},{8,16},{9,17... | collective-permute-start | bytes 2162696 | tf_op jit(solution)/shard_map/ppermute | solution.py:331
  76.7 26.4 %collective-permute-start.17 = (bf16[72,2688]{1,0:T(8,128)(2,1)S(1)}, bf16[72,2688]{1,0:T(8,128)(2,1)S(1)}, u32[]{:S(2)}, u32[]{:S(2)}) collective-permute-start(bf16[72,2688]{1,0:T(8,128)(2,1)S(1)} %get-tuple-element.72), channel_id=1, source_target_pairs={{0,2},{1,3},{2,0},{3,1},{4,6},{5,7},{6,4},{7,5},{8,10},{9,11},{10,... | collective-permute-start | bytes 1161224 | tf_op jit(solution)/shard_map/ppermute | solution.py:323
  78.2 25.5 %collective-permute-start.18 = (bf16[72,2688]{1,0:T(8,128)(2,1)S(1)}, bf16[72,2688]{1,0:T(8,128)(2,1)S(1)}, u32[]{:S(2)}, u32[]{:S(2)}) collective-permute-start(bf16[72,2688]{1,0:T(8,128)(2,1)S(1)} %get-tuple-element.73), channel_id=1, source_target_pairs={{0,4},{1,5},{2,6},{3,7},{4,0},{5,1},{6,2},{7,3},{8,12},{9,13},{10,... | collective-permute-start | bytes 1161224 | tf_op jit(solution)/shard_map/ppermute | solution.py:323
  79.6 24.2 %collective-permute-start.19 = (bf16[72,2688]{1,0:T(8,128)(2,1)S(1)}, bf16[72,2688]{1,0:T(8,128)(2,1)S(1)}, u32[]{:S(2)}, u32[]{:S(2)}) collective-permute-start(bf16[72,2688]{1,0:T(8,128)(2,1)S(1)} %get-tuple-element.74), channel_id=1, source_target_pairs={{0,6},{1,7},{2,4},{3,5},{4,2},{5,3},{6,0},{7,1},{8,14},{9,15},{10,... | collective-permute-start | bytes 1161224 | tf_op jit(solution)/shard_map/ppermute | solution.py:323
  100.2 11.9 %collective-permute-start.28 = (bf16[72,2688]{1,0:T(8,128)(2,1)S(1)}, bf16[72,2688]{1,0:T(8,128)(2,1)S(1)}, u32[]{:S(2)}, u32[]{:S(2)}) collective-permute-start(bf16[72,2688]{1,0:T(8,128)(2,1)S(1)} %get-tuple-element.82), channel_id=1, source_target_pairs={{0,2},{1,3},{2,0},{3,1},{4,6},{5,7},{6,4},{7,5},{8,10},{9,11},{10,... | collective-permute-start | bytes 1161224 | tf_op jit(solution)/shard_map/ppermute | solution.py:323
  101.7 19.0 %collective-permute-start.29 = (bf16[72,2688]{1,0:T(8,128)(2,1)S(1)}, bf16[72,2688]{1,0:T(8,128)(2,1)S(1)}, u32[]{:S(2)}, u32[]{:S(2)}) collective-permute-start(bf16[72,2688]{1,0:T(8,128)(2,1)S(1)} %get-tuple-element.83), channel_id=1, source_target_pairs={{0,4},{1,5},{2,6},{3,7},{4,0},{5,1},{6,2},{7,3},{8,12},{9,13},{10,... | collective-permute-start | bytes 1161224 | tf_op jit(solution)/shard_map/ppermute | solution.py:323
  103.1 17.7 %collective-permute-start.30 = (bf16[72,2688]{1,0:T(8,128)(2,1)S(1)}, bf16[72,2688]{1,0:T(8,128)(2,1)S(1)}, u32[]{:S(2)}, u32[]{:S(2)}) collective-permute-start(bf16[72,2688]{1,0:T(8,128)(2,1)S(1)} %get-tuple-element.84), channel_id=1, source_target_pairs={{0,6},{1,7},{2,4},{3,5},{4,2},{5,3},{6,0},{7,1},{8,14},{9,15},{10,... | collective-permute-start | bytes 1161224 | tf_op jit(solution)/shard_map/ppermute | solution.py:323
  108.4 19.9 %collective-permute-start.23 = (bf16[128,2816]{1,0:T(8,128)(2,1)S(1)}, bf16[128,2816]{1,0:T(8,128)(2,1)S(1)}, u32[]{:S(2)}, u32[]{:S(2)}) collective-permute-start(bf16[128,2816]{1,0:T(8,128)(2,1)S(1)} %collective-permute-done.20.own_ref), channel_id=1, source_target_pairs={{0,8},{1,9},{2,10},{3,11},{4,12},{5,13},{6,14},{7,15},{8,16},{9,17... | collective-permute-start | bytes 2162696 | tf_op jit(solution)/shard_map/ppermute | solution.py:331
  124.7 12.0 %collective-permute-start.46 = (bf16[72,2688]{1,0:T(8,128)(2,1)S(1)}, bf16[72,2688]{1,0:T(8,128)(2,1)S(1)}, u32[]{:S(2)}, u32[]{:S(2)}) collective-permute-start(bf16[72,2688]{1,0:T(8,128)(2,1)S(1)} %get-tuple-element.100), channel_id=1, source_target_pairs={{0,2},{1,3},{2,0},{3,1},{4,6},{5,7},{6,4},{7,5},{8,10},{9,11},{10,... | collective-permute-start | bytes 1161224 | tf_op jit(solution)/shard_map/ppermute | solution.py:323
  125.9 19.3 %collective-permute-start.47 = (bf16[72,2688]{1,0:T(8,128)(2,1)S(1)}, bf16[72,2688]{1,0:T(8,128)(2,1)S(1)}, u32[]{:S(2)}, u32[]{:S(2)}) collective-permute-start(bf16[72,2688]{1,0:T(8,128)(2,1)S(1)} %get-tuple-element.99), channel_id=1, source_target_pairs={{0,4},{1,5},{2,6},{3,7},{4,0},{5,1},{6,2},{7,3},{8,12},{9,13},{10,... | collective-permute-start | bytes 1161224 | tf_op jit(solution)/shard_map/ppermute | solution.py:323
  126.7 19.2 %collective-permute-start.48 = (bf16[72,2688]{1,0:T(8,128)(2,1)S(1)}, bf16[72,2688]{1,0:T(8,128)(2,1)S(1)}, u32[]{:S(2)}, u32[]{:S(2)}) collective-permute-start(bf16[72,2688]{1,0:T(8,128)(2,1)S(1)} %get-tuple-element.98), channel_id=1, source_target_pairs={{0,6},{1,7},{2,4},{3,5},{4,2},{5,3},{6,0},{7,1},{8,14},{9,15},{10,... | collective-permute-start | bytes 1161224 | tf_op jit(solution)/shard_map/ppermute | solution.py:323
  128.3 2.4 collective-permute-start.24
  133.1 20.2 %collective-permute-start.39 = (bf16[72,2688]{1,0:T(8,128)(2,1)S(1)}, bf16[72,2688]{1,0:T(8,128)(2,1)S(1)}, u32[]{:S(2)}, u32[]{:S(2)}) collective-permute-start(bf16[72,2688]{1,0:T(8,128)(2,1)S(1)} %get-tuple-element.93), channel_id=1, source_target_pairs={{0,2},{1,3},{2,0},{3,1},{4,6},{5,7},{6,4},{7,5},{8,10},{9,11},{10,... | collective-permute-start | bytes 1161224 | tf_op jit(solution)/shard_map/ppermute | solution.py:323
  134.3 26.4 %collective-permute-start.40 = (bf16[72,2688]{1,0:T(8,128)(2,1)S(1)}, bf16[72,2688]{1,0:T(8,128)(2,1)S(1)}, u32[]{:S(2)}, u32[]{:S(2)}) collective-permute-start(bf16[72,2688]{1,0:T(8,128)(2,1)S(1)} %get-tuple-element.94), channel_id=1, source_target_pairs={{0,4},{1,5},{2,6},{3,7},{4,0},{5,1},{6,2},{7,3},{8,12},{9,13},{10,... | collective-permute-start | bytes 1161224 | tf_op jit(solution)/shard_map/ppermute | solution.py:323
  136.7 24.0 %collective-permute-start.41 = (bf16[72,2688]{1,0:T(8,128)(2,1)S(1)}, bf16[72,2688]{1,0:T(8,128)(2,1)S(1)}, u32[]{:S(2)}, u32[]{:S(2)}) collective-permute-start(bf16[72,2688]{1,0:T(8,128)(2,1)S(1)} %get-tuple-element.95), channel_id=1, source_target_pairs={{0,6},{1,7},{2,4},{3,5},{4,2},{5,3},{6,0},{7,1},{8,14},{9,15},{10,... | collective-permute-start | bytes 1161224 | tf_op jit(solution)/shard_map/ppermute | solution.py:323
  146.8 27.0 %collective-permute-start.49 = (bf16[128,2688]{1,0:T(8,128)(2,1)S(1)}, bf16[128,2688]{1,0:T(8,128)(2,1)S(1)}, u32[]{:S(2)}, u32[]{:S(2)}) collective-permute-start(bf16[128,2688]{1,0:T(8,128)(2,1)S(1)} %slice.183), channel_id=1, source_target_pairs={{0,1},{1,0},{2,3},{3,2},{4,5},{5,4},{6,7},{7,6},{8,9},{9,8},{10,11... | collective-permute-start | bytes 2064392 | tf_op jit(solution)/shard_map/ppermute | solution.py:323
  146.9 20.3 %collective-permute-start.26 = (bf16[128,2816]{1,0:T(8,128)(2,1)S(1)}, bf16[128,2816]{1,0:T(8,128)(2,1)S(1)}, u32[]{:S(2)}, u32[]{:S(2)}) collective-permute-start(bf16[128,2816]{1,0:T(8,128)(2,1)S(1)} %collective-permute-done.23.own_ref), channel_id=1, source_target_pairs={{0,8},{1,9},{2,10},{3,11},{4,12},{5,13},{6,14},{7,15},{8,16},{9,17... | collective-permute-start | bytes 2162696 | tf_op jit(solution)/shard_map/ppermute | solution.py:331
  164.6 10.4 %collective-permute-start.42 = (bf16[72,2688]{1,0:T(8,128)(2,1)S(1)}, bf16[72,2688]{1,0:T(8,128)(2,1)S(1)}, u32[]{:S(2)}, u32[]{:S(2)}) collective-permute-start(bf16[72,2688]{1,0:T(8,128)(2,1)S(1)} %get-tuple-element.104), channel_id=1, source_target_pairs={{0,2},{1,3},{2,0},{3,1},{4,6},{5,7},{6,4},{7,5},{8,10},{9,11},{10,... | collective-permute-start | bytes 1161224 | tf_op jit(solution)/shard_map/ppermute | solution.py:323
  167.4 2.8 %collective-permute-start.31 = (bf16[64,2816]{1,0:T(8,128)(2,1)S(1)}, bf16[64,2816]{1,0:T(8,128)(2,1)S(1)}, u32[]{:S(2)}, u32[]{:S(2)}) collective-permute-start(bf16[64,2816]{1,0:T(8,128)(2,1)S(1)} %get-tuple-element.113), channel_id=1, source_target_pairs={{0,1},{1,0},{2,3},{3,2},{4,5},{5,4},{6,7},{7,6},{8,9},{9,8},{10,11... | collective-permute-start | bytes 1081352 | tf_op jit(solution)/shard_map/ppermute | solution.py:323
  167.9 20.1 %collective-permute-start.43 = (bf16[72,2688]{1,0:T(8,128)(2,1)S(1)}, bf16[72,2688]{1,0:T(8,128)(2,1)S(1)}, u32[]{:S(2)}, u32[]{:S(2)}) collective-permute-start(bf16[72,2688]{1,0:T(8,128)(2,1)S(1)} %get-tuple-element.103), channel_id=1, source_target_pairs={{0,4},{1,5},{2,6},{3,7},{4,0},{5,1},{6,2},{7,3},{8,12},{9,13},{10,... | collective-permute-start | bytes 1161224 | tf_op jit(solution)/shard_map/ppermute | solution.py:323
  169.0 19.0 %collective-permute-start.44 = (bf16[72,2688]{1,0:T(8,128)(2,1)S(1)}, bf16[72,2688]{1,0:T(8,128)(2,1)S(1)}, u32[]{:S(2)}, u32[]{:S(2)}) collective-permute-start(bf16[72,2688]{1,0:T(8,128)(2,1)S(1)} %get-tuple-element.102), channel_id=1, source_target_pairs={{0,6},{1,7},{2,4},{3,5},{4,2},{5,3},{6,0},{7,1},{8,14},{9,15},{10,... | collective-permute-start | bytes 1161224 | tf_op jit(solution)/shard_map/ppermute | solution.py:323
  172.6 17.3 %collective-permute-start.32 = (bf16[72,2688]{1,0:T(8,128)(2,1)S(1)}, bf16[72,2688]{1,0:T(8,128)(2,1)S(1)}, u32[]{:S(2)}, u32[]{:S(2)}) collective-permute-start(bf16[72,2688]{1,0:T(8,128)(2,1)S(1)} %get-tuple-element.87), channel_id=1, source_target_pairs={{0,2},{1,3},{2,0},{3,1},{4,6},{5,7},{6,4},{7,5},{8,10},{9,11},{10,... | collective-permute-start | bytes 1161224 | tf_op jit(solution)/shard_map/ppermute | solution.py:323
  173.8 29.9 %collective-permute-start.33 = (bf16[72,2688]{1,0:T(8,128)(2,1)S(1)}, bf16[72,2688]{1,0:T(8,128)(2,1)S(1)}, u32[]{:S(2)}, u32[]{:S(2)}) collective-permute-start(bf16[72,2688]{1,0:T(8,128)(2,1)S(1)} %get-tuple-element.88), channel_id=1, source_target_pairs={{0,4},{1,5},{2,6},{3,7},{4,0},{5,1},{6,2},{7,3},{8,12},{9,13},{10,... | collective-permute-start | bytes 1161224 | tf_op jit(solution)/shard_map/ppermute | solution.py:323
  175.0 28.8 %collective-permute-start.34 = (bf16[72,2688]{1,0:T(8,128)(2,1)S(1)}, bf16[72,2688]{1,0:T(8,128)(2,1)S(1)}, u32[]{:S(2)}, u32[]{:S(2)}) collective-permute-start(bf16[72,2688]{1,0:T(8,128)(2,1)S(1)} %get-tuple-element.89), channel_id=1, source_target_pairs={{0,6},{1,7},{2,4},{3,5},{4,2},{5,3},{6,0},{7,1},{8,14},{9,15},{10,... | collective-permute-start | bytes 1161224 | tf_op jit(solution)/shard_map/ppermute | solution.py:323
  188.0 23.2 %collective-permute-start.50 = (bf16[128,2688]{1,0:T(8,128)(2,1)S(1)}, bf16[128,2688]{1,0:T(8,128)(2,1)S(1)}, u32[]{:S(2)}, u32[]{:S(2)}) collective-permute-start(bf16[128,2688]{1,0:T(8,128)(2,1)S(1)} %fusion.91), channel_id=1, source_target_pairs={{0,8},{1,9},{2,10},{3,11},{4,12},{5,13},{6,14},{7,15},{8,16},{9,17... | collective-permute-start | bytes 2064392 | tf_op jit(solution)/shard_map/ppermute | solution.py:331
  189.0 22.2 %collective-permute-start.45 = (bf16[128,2688]{1,0:T(8,128)(2,1)S(1)}, bf16[128,2688]{1,0:T(8,128)(2,1)S(1)}, u32[]{:S(2)}, u32[]{:S(2)}) collective-permute-start(bf16[128,2688]{1,0:T(8,128)(2,1)S(1)} %slice.184), channel_id=1, source_target_pairs={{0,1},{1,0},{2,3},{3,2},{4,5},{5,4},{6,7},{7,6},{8,9},{9,8},{10,11... | collective-permute-start | bytes 2064392 | tf_op jit(solution)/shard_map/ppermute | solution.py:323
  207.7 12.0 %collective-permute-start.35 = (bf16[72,2688]{1,0:T(8,128)(2,1)S(1)}, bf16[72,2688]{1,0:T(8,128)(2,1)S(1)}, u32[]{:S(2)}, u32[]{:S(2)}) collective-permute-start(bf16[72,2688]{1,0:T(8,128)(2,1)S(1)} %get-tuple-element.108), channel_id=1, source_target_pairs={{0,2},{1,3},{2,0},{3,1},{4,6},{5,7},{6,4},{7,5},{8,10},{9,11},{10,... | collective-permute-start | bytes 1161224 | tf_op jit(solution)/shard_map/ppermute | solution.py:323
  208.3 18.1 %collective-permute-start.36 = (bf16[72,2688]{1,0:T(8,128)(2,1)S(1)}, bf16[72,2688]{1,0:T(8,128)(2,1)S(1)}, u32[]{:S(2)}, u32[]{:S(2)}) collective-permute-start(bf16[72,2688]{1,0:T(8,128)(2,1)S(1)} %get-tuple-element.107), channel_id=1, source_target_pairs={{0,4},{1,5},{2,6},{3,7},{4,0},{5,1},{6,2},{7,3},{8,12},{9,13},{10,... | collective-permute-start | bytes 1161224 | tf_op jit(solution)/shard_map/ppermute | solution.py:323
  209.5 16.9 %collective-permute-start.37 = (bf16[72,2688]{1,0:T(8,128)(2,1)S(1)}, bf16[72,2688]{1,0:T(8,128)(2,1)S(1)}, u32[]{:S(2)}, u32[]{:S(2)}) collective-permute-start(bf16[72,2688]{1,0:T(8,128)(2,1)S(1)} %get-tuple-element.106), channel_id=1, source_target_pairs={{0,6},{1,7},{2,4},{3,5},{4,2},{5,3},{6,0},{7,1},{8,14},{9,15},{10,... | collective-permute-start | bytes 1161224 | tf_op jit(solution)/shard_map/ppermute | solution.py:323
  211.5 17.6 %collective-permute-start.51 = (bf16[128,2688]{1,0:T(8,128)(2,1)S(1)}, bf16[128,2688]{1,0:T(8,128)(2,1)S(1)}, u32[]{:S(2)}, u32[]{:S(2)}) collective-permute-start(bf16[128,2688]{1,0:T(8,128)(2,1)S(1)} %fusion.93), channel_id=1, source_target_pairs={{0,8},{1,9},{2,10},{3,11},{4,12},{5,13},{6,14},{7,15},{8,16},{9,17... | collective-permute-start | bytes 2064392 | tf_op jit(solution)/shard_map/ppermute | solution.py:331
  229.8 19.3 %collective-permute-start.52 = (bf16[128,2688]{1,0:T(8,128)(2,1)S(1)}, bf16[128,2688]{1,0:T(8,128)(2,1)S(1)}, u32[]{:S(2)}, u32[]{:S(2)}) collective-permute-start(bf16[128,2688]{1,0:T(8,128)(2,1)S(1)} %fusion.95), channel_id=1, source_target_pairs={{0,8},{1,9},{2,10},{3,11},{4,12},{5,13},{6,14},{7,15},{8,16},{9,17... | collective-permute-start | bytes 2064392 | tf_op jit(solution)/shard_map/ppermute | solution.py:331
  230.0 19.1 %collective-permute-start.53 = (bf16[72,2688]{1,0:T(8,128)(2,1)S(1)}, bf16[72,2688]{1,0:T(8,128)(2,1)S(1)}, u32[]{:S(2)}, u32[]{:S(2)}) collective-permute-start(bf16[72,2688]{1,0:T(8,128)(2,1)S(1)} %get-tuple-element.112), channel_id=1, source_target_pairs={{0,2},{1,3},{2,0},{3,1},{4,6},{5,7},{6,4},{7,5},{8,10},{9,11},{10,... | collective-permute-start | bytes 1161224 | tf_op jit(solution)/shard_map/ppermute | solution.py:323
  231.5 19.0 %collective-permute-start.54 = (bf16[72,2688]{1,0:T(8,128)(2,1)S(1)}, bf16[72,2688]{1,0:T(8,128)(2,1)S(1)}, u32[]{:S(2)}, u32[]{:S(2)}) collective-permute-start(bf16[72,2688]{1,0:T(8,128)(2,1)S(1)} %get-tuple-element.111), channel_id=1, source_target_pairs={{0,4},{1,5},{2,6},{3,7},{4,0},{5,1},{6,2},{7,3},{8,12},{9,13},{10,... | collective-permute-start | bytes 1161224 | tf_op jit(solution)/shard_map/ppermute | solution.py:323
  232.2 18.4 %collective-permute-start.55 = (bf16[72,2688]{1,0:T(8,128)(2,1)S(1)}, bf16[72,2688]{1,0:T(8,128)(2,1)S(1)}, u32[]{:S(2)}, u32[]{:S(2)}) collective-permute-start(bf16[72,2688]{1,0:T(8,128)(2,1)S(1)} %get-tuple-element.110), channel_id=1, source_target_pairs={{0,6},{1,7},{2,4},{3,5},{4,2},{5,3},{6,0},{7,1},{8,14},{9,15},{10,... | collective-permute-start | bytes 1161224 | tf_op jit(solution)/shard_map/ppermute | solution.py:323
  (30 other events, 302.5 us)
